TPU v7x, 32 devices: a whole 2x2x4 slice. The times are simulated.
32 devices in a mesh: section: 2 (over core), mp: 4 (over z), dp: 4 (over y, x).
Axes of the slice: x: 2, y: 2, z: 4, core: 2. Of those that a mesh axis runs over, the one named last changes fastest.
Arguments:
- inputs: bfloat16 [8, 1024, 768], P('dp', 'mp'), may hold values from -6 to 6
- cotangent: bfloat16 [8, 1024, 768], P('dp', 'mp'), may hold values from -6 to 6
- lengths: int32 [8, 4], P('dp'), may hold values from 1 to 832, 960 in all within a row
- norm_gains: float32 [2, 2, 768], P('section'), may hold values from 0.5 to 1.5
- norm_shifts: float32 [2, 2, 768], P('section'), may hold values from -3 to 3
- in_weight: bfloat16 [2, 768, 3, 768], P('section', None, None, 'mp'), may hold values from -0.21875 to 0.21875
- in_bias: float32 [2, 2, 768], P('section', None, 'mp'), may hold values from -3 to 3
- out_weight: bfloat16 [2, 768, 768], P('section', 'mp'), may hold values from -1.75 to 1.75
- up_weight: bfloat16 [2, 768, 3072], P('section', None, 'mp'), may hold values from -0.21875 to 0.21875
- up_bias: float32 [2, 3072], P('section', 'mp'), may hold values from -3 to 3
- down_weight: bfloat16 [2, 3072, 768], P('section', 'mp'), may hold values from -0.3125 to 0.3125
- branch_bias: float32 [2, 2, 768], P('section'), may hold values from -3 to 3
Outputs:
- section_outputs: bfloat16 [2, 8, 1024, 768], P('section', 'dp', 'mp')
- input_grads: float32 [2, 8, 1024, 768], P('section', 'dp', 'mp')
- grad_norm_gains: float32 [2, 2, 768], P('section')
- grad_norm_shifts: float32 [2, 2, 768], P('section')
- grad_in_weight: float32 [2, 768, 3, 768], P('section', None, None, 'mp')
- grad_in_bias: float32 [2, 2, 768], P('section', None, 'mp')
- grad_out_weight: float32 [2, 768, 768], P('section', 'mp')
- grad_up_weight: float32 [2, 768, 3072], P('section', None, 'mp')
- grad_up_bias: float32 [2, 3072], P('section', 'mp')
- grad_down_weight: float32 [2, 3072, 768], P('section', 'mp')
- grad_branch_bias: float32 [2, 2, 768], P('section')
Inputs may be any that keep to these rules, and one draw needn't show every extreme that they name: `lengths`: the 4 documents of a row fill its first 960 tokens in order, and its last 64 tokens are padding; in every row one document has exactly 832 tokens.
All inputs are finite; a program needn't handle non-finite values.
Results may differ from a plain program's by a relative error of at most 0.019.
Values may be sent and summed in bfloat16 or wider, within the bound.
A program may use at most 192 MiB of HBM per device.

v0:
```python
from functools import partial

import jax
import jax.numpy as jnp
from jax import lax
from jax.sharding import PartitionSpec as P

HEAD = 64


branch_scale = 12.0 ** (-0.5)
norm_eps = 1e-05
masked_score = -1000000000.0
block_rows = 512


def shifted(value, axis, by):
    count = lax.axis_size(axis)
    pairs = [(i, i + by) for i in range(count) if 0 <= i + by < count]
    return lax.ppermute(value, axis, pairs)


def layer_norm(values, gain, shift):
    mean = jnp.mean(values, axis=-1, keepdims=True)
    centred = values - mean
    spread = jnp.mean(centred * centred, axis=-1, keepdims=True)
    return centred * lax.rsqrt(spread + norm_eps) * gain + shift


def segment_ids(lengths, length):
    ends = jnp.cumsum(lengths, axis=-1)
    positions = jnp.arange(length, dtype=jnp.int32)
    return jnp.sum((positions[None, :, None] >= ends[:, None, :]).astype(jnp.int32), axis=-1)


def block_mask(segs, start, count, docs):
    length = segs.shape[0]
    query_pos = start + jnp.arange(count, dtype=jnp.int32)
    key_pos = jnp.arange(length, dtype=jnp.int32)
    query_seg = lax.dynamic_slice_in_dim(segs, start, count, 0)
    same = segs[None, :] == query_seg[:, None]
    causal = key_pos[None, :] <= query_pos[:, None]
    real = (segs[None, :] < docs) | (key_pos[None, :] == query_pos[:, None])
    return same & causal & real


def attend_row(queries, keys, values, segs, docs):
    heads, length, width = queries.shape
    count = min(block_rows, length)
    scale = width ** (-0.5)

    def one_block(index):
        start = index * count
        block = lax.dynamic_slice_in_dim(queries, start, count, 1)
        scores = jnp.einsum("hqd,hkd->hqk", block, keys, preferred_element_type=jnp.float32) * scale
        scores = jnp.where(block_mask(segs, start, count, docs)[None], scores, masked_score)
        top = jnp.max(scores, axis=-1, keepdims=True)
        weights = jnp.exp(scores - top)
        total = jnp.sum(weights, axis=-1, keepdims=True)
        probs = (weights / total).astype(jnp.bfloat16)
        mixed = jnp.einsum("hqk,hkd->hqd", probs, values, preferred_element_type=jnp.float32)
        return (mixed, top[..., 0] + jnp.log(total[..., 0]))

    mixed, logsum = lax.map(one_block, jnp.arange(length // count, dtype=jnp.int32))
    mixed = mixed.transpose(1, 0, 2, 3).reshape(heads, length, width)
    logsum = logsum.transpose(1, 0, 2).reshape(heads, length)
    return (mixed, logsum)


def attend_row_back(queries, keys, values, segs, logsum, grad_mixed, docs):
    heads, length, width = queries.shape
    count = min(block_rows, length)
    scale = width ** (-0.5)

    def one_block(carry, index):
        grad_keys, grad_values = carry
        start = index * count
        block = lax.dynamic_slice_in_dim(queries, start, count, 1)
        grad_block = lax.dynamic_slice_in_dim(grad_mixed, start, count, 1)
        block_sum = lax.dynamic_slice_in_dim(logsum, start, count, 1)
        scores = jnp.einsum("hqd,hkd->hqk", block, keys, preferred_element_type=jnp.float32) * scale
        scores = jnp.where(block_mask(segs, start, count, docs)[None], scores, masked_score)
        probs = jnp.exp(scores - block_sum[..., None])
        grad_values = grad_values + jnp.einsum(
            "hqk,hqd->hkd",
            probs.astype(jnp.bfloat16),
            grad_block,
            preferred_element_type=jnp.float32,
        )
        grad_probs = jnp.einsum(
            "hqd,hkd->hqk", grad_block, values, preferred_element_type=jnp.float32
        )
        grad_scores = probs * (grad_probs - jnp.sum(probs * grad_probs, axis=-1, keepdims=True))
        grad_low = grad_scores.astype(jnp.bfloat16)
        grad_queries = (
            jnp.einsum("hqk,hkd->hqd", grad_low, keys, preferred_element_type=jnp.float32) * scale
        )
        grad_keys = (
            grad_keys
            + jnp.einsum("hqk,hqd->hkd", grad_low, block, preferred_element_type=jnp.float32)
            * scale
        )
        return ((grad_keys, grad_values), grad_queries)

    zeros = jnp.zeros((heads, length, width), jnp.float32)
    (grad_keys, grad_values), grad_queries = lax.scan(
        one_block, (zeros, zeros), jnp.arange(length // count, dtype=jnp.int32)
    )
    grad_queries = grad_queries.transpose(1, 0, 2, 3).reshape(heads, length, width)
    return (grad_queries, grad_keys, grad_values)


def to_sequences(flat, parts, rows):
    per_part = flat.shape[0] // (parts * rows)
    return (
        flat.reshape(parts, rows, per_part, flat.shape[1])
        .transpose(1, 0, 2, 3)
        .reshape(rows, parts * per_part, flat.shape[1])
    )


def to_flat(seqs, parts):
    rows, length, width = seqs.shape
    per_part = length // parts
    return (
        seqs.reshape(rows, parts, per_part, width)
        .transpose(1, 0, 2, 3)
        .reshape(parts * rows * per_part, width)
    )


def split_heads(flat, parts, rows):
    seqs = to_sequences(flat, parts, rows)
    count, length, width = seqs.shape
    return seqs.reshape(count, length, 3, width // (3 * HEAD), HEAD).transpose(2, 0, 3, 1, 4)


def heads_of(flat, parts, rows):
    seqs = to_sequences(flat, parts, rows)
    count, length, width = seqs.shape
    return seqs.reshape(count, length, width // HEAD, HEAD).transpose(0, 2, 1, 3)


def merge_heads(stacked, parts):
    groups, rows, heads, length, width = stacked.shape
    seqs = stacked.transpose(1, 3, 0, 2, 4).reshape(rows, length, groups * heads * width)
    return to_flat(seqs, parts)


def spread_tokens(local):
    return lax.all_gather(local, "mp", axis=0, tiled=True)


def sum_tokens(left, right, contract, rows):

    def term(start, count):
        return lax.dot_general(
            left, right, (((1,), (contract,)), ((), ())), preferred_element_type=jnp.float32
        )

    return lax.psum_scatter(
        term(jnp.int32(0), rows * lax.axis_size("mp")).astype(jnp.bfloat16),
        "mp",
        scatter_dimension=0,
        tiled=True,
    ).astype(jnp.float32)


def first_dims(left, right):
    return lax.dot_general(
        left, right, (((0,), (0,)), ((), ())), preferred_element_type=jnp.float32
    )


def attention_forward(state, segs, weights, parts, docs):
    gains, shifts, mixing, mix_bias, out_local, up_local, up_shift, down_local, branch_shift = (
        weights
    )
    rows = segs.shape[0]
    normed = layer_norm(state, gains[0], shifts[0]).astype(jnp.bfloat16)
    normed_all = spread_tokens(normed)
    mixed_all = (jnp.dot(normed_all, mixing, preferred_element_type=jnp.float32) + mix_bias).astype(
        jnp.bfloat16
    )
    heads = split_heads(mixed_all, parts, rows)

    def attention_per_row(item):
        return attend_row(item[0], item[1], item[2], item[3], docs)

    attended, logsum = lax.map(attention_per_row, (heads[0], heads[1], heads[2], segs))
    attended = merge_heads(attended[None], parts).astype(jnp.bfloat16)
    branch = sum_tokens(attended, out_local, 0, state.shape[0])
    middle = state + branch_scale * (branch + branch_shift[0])
    upper = layer_norm(middle, gains[1], shifts[1]).astype(jnp.bfloat16)
    upper_all = spread_tokens(upper)
    hidden_pre = jnp.dot(upper_all, up_local, preferred_element_type=jnp.float32) + up_shift
    hidden = jax.nn.gelu(hidden_pre, approximate=True).astype(jnp.bfloat16)
    return (normed_all, heads, logsum, attended, middle, upper_all, hidden_pre, hidden)


def finish_layer(state, kept, weights):
    down = sum_tokens(kept[7], weights[7], 0, state.shape[0])
    return kept[4] + branch_scale * (down + weights[8][1])


def unit_backward(grad_out, kept, weights):
    normed_all, heads, logsum, attended, middle, upper_all, hidden_pre, hidden = kept
    gains, shifts, mixing, mix_bias, out_local, up_local, up_shift, down_local, branch_shift = (
        weights
    )
    scaled = branch_scale * grad_out
    grad_branch = jnp.sum(scaled, axis=0)
    scaled_all = spread_tokens(scaled.astype(jnp.bfloat16))
    grad_down = first_dims(hidden, scaled_all)
    grad_hidden = lax.dot_general(
        scaled_all, down_local, (((1,), (1,)), ((), ())), preferred_element_type=jnp.float32
    )
    unused, gelu_back = jax.vjp(partial(jax.nn.gelu, approximate=True), hidden_pre)
    grad_pre = gelu_back(grad_hidden)[0].astype(jnp.bfloat16)
    grad_up_shift = jnp.sum(grad_pre, axis=0, dtype=jnp.float32)
    grad_up = first_dims(upper_all, grad_pre)
    grad_upper = sum_tokens(grad_pre, up_local, 1, grad_out.shape[0])
    unused, norm_back = jax.vjp(layer_norm, middle, gains[1], shifts[1])
    grad_middle, grad_gain, grad_shift = norm_back(grad_upper)
    return (
        grad_out + grad_middle,
        (grad_up, grad_up_shift, grad_down),
        (grad_gain, grad_shift, grad_branch),
    )


def head_backward(grad_mid, state, segs, kept, weights, parts, docs):
    normed_all, heads, logsum, attended, middle, upper_all, hidden_pre, hidden = kept
    gains, shifts, mixing, mix_bias, out_local, up_local, up_shift, down_local, branch_shift = (
        weights
    )
    rows = segs.shape[0]
    scaled = branch_scale * grad_mid
    grad_branch = jnp.sum(scaled, axis=0)
    scaled_all = spread_tokens(scaled.astype(jnp.bfloat16))
    grad_out_local = first_dims(attended, scaled_all)
    grad_attended = lax.dot_general(
        scaled_all, out_local, (((1,), (1,)), ((), ())), preferred_element_type=jnp.float32
    ).astype(jnp.bfloat16)
    grad_heads = heads_of(grad_attended, parts, rows)

    def head_per_row(item):
        return attend_row_back(item[0], item[1], item[2], item[3], item[4], item[5], docs)

    grad_queries, grad_keys, grad_values = lax.map(
        head_per_row, (heads[0], heads[1], heads[2], segs, logsum, grad_heads)
    )
    grad_mix = merge_heads(jnp.stack([grad_queries, grad_keys, grad_values]), parts).astype(
        jnp.bfloat16
    )
    local_width = grad_attended.shape[1]
    grad_bias = jnp.stack(
        [
            jnp.sum(grad_mix[:, :local_width], axis=0, dtype=jnp.float32),
            jnp.sum(grad_mix[:, 2 * local_width :], axis=0, dtype=jnp.float32),
        ]
    )
    grad_mixing = first_dims(normed_all, grad_mix)
    grad_normed = sum_tokens(grad_mix, mixing, 1, state.shape[0])
    unused, norm_back = jax.vjp(layer_norm, state, gains[0], shifts[0])
    grad_state, grad_gain, grad_shift = norm_back(grad_normed)
    return (
        grad_mid + grad_state,
        (grad_mixing, grad_bias, grad_out_local),
        (grad_gain, grad_shift, grad_branch),
    )


def masked_add(totals, terms, valid):
    return tuple((total + jnp.where(valid, term, 0.0) for total, term in zip(totals, terms)))


def per_device(
    inputs,
    cotangent,
    lengths,
    norm_gains,
    norm_shifts,
    in_weight,
    in_bias,
    out_weight,
    up_weight,
    up_bias,
    down_weight,
    branch_bias,
):
    section = lax.axis_index("section")
    sections = lax.axis_size("section")
    parts = lax.axis_size("mp")
    micro = inputs.shape[0]
    per_part = inputs.shape[1]
    width = inputs.shape[2]
    docs = lengths.shape[1]
    local_width = in_weight.shape[3]
    mixing = in_weight[0].reshape(width, 3 * local_width)
    mix_bias = jnp.concatenate(
        [in_bias[0, 0], jnp.zeros((local_width,), jnp.float32), in_bias[0, 1]]
    )
    weights = (
        norm_gains[0],
        norm_shifts[0],
        mixing,
        mix_bias,
        out_weight[0],
        up_weight[0],
        up_bias[0],
        down_weight[0],
        branch_bias[0],
    )
    ticks = micro + sections - 1
    first = section == 0
    last = section == sections - 1

    def row_segments(slot):
        return segment_ids(lax.dynamic_slice_in_dim(lengths, slot, 1, 0), per_part * parts)

    incoming = jnp.zeros((per_part, width), jnp.bfloat16)
    arrived_all = jnp.zeros((micro, per_part, width), jnp.bfloat16)
    results_all = jnp.zeros((micro, per_part, width), jnp.bfloat16)
    for tick in range(ticks):
        fresh = inputs[min(tick, micro - 1)]
        arrived = jnp.where(first, fresh, incoming)
        number = tick - section
        valid = (number >= 0) & (number < micro)
        slot = jnp.clip(number, 0, micro - 1)
        state = arrived.astype(jnp.float32)
        kept = attention_forward(state, row_segments(slot), weights, parts, docs)
        result = finish_layer(state, kept, weights).astype(jnp.bfloat16)
        arrived_all = jnp.where(
            valid, lax.dynamic_update_index_in_dim(arrived_all, arrived, slot, 0), arrived_all
        )
        results_all = jnp.where(
            valid, lax.dynamic_update_index_in_dim(results_all, result, slot, 0), results_all
        )
        if tick + 1 < ticks:
            incoming = shifted(result, "section", 1)
    unit_grads = (
        jnp.zeros(up_weight.shape[1:], jnp.float32),
        jnp.zeros(up_bias.shape[1:], jnp.float32),
        jnp.zeros(down_weight.shape[1:], jnp.float32),
    )
    head_grads = (
        jnp.zeros(mixing.shape, jnp.float32),
        jnp.zeros(in_bias.shape[1:], jnp.float32),
        jnp.zeros(out_weight.shape[1:], jnp.float32),
    )
    vector_grads = (
        jnp.zeros(norm_gains.shape[1:], jnp.float32),
        jnp.zeros(norm_shifts.shape[1:], jnp.float32),
        jnp.zeros(branch_bias.shape[1:], jnp.float32),
    )
    grads_all = jnp.zeros((micro, per_part, width), jnp.float32)
    incoming = jnp.zeros((per_part, width), jnp.bfloat16)
    for tick in range(ticks):
        number = tick - (sections - 1 - section)
        valid = (number >= 0) & (number < micro)
        slot = jnp.clip(number, 0, micro - 1)
        fresh = cotangent[min(tick, micro - 1)].astype(jnp.float32)
        grad_out = jnp.where(last, fresh, incoming.astype(jnp.float32))
        state = lax.dynamic_index_in_dim(arrived_all, slot, 0, keepdims=False).astype(jnp.float32)
        segs = row_segments(slot)
        kept = attention_forward(state, segs, weights, parts, docs)
        grad_mid, unit_terms, unit_vectors = unit_backward(grad_out, kept, weights)
        unit_grads = masked_add(unit_grads, unit_terms, valid)
        grad_in, head_terms, head_vectors = head_backward(
            grad_mid, state, segs, kept, weights, parts, docs
        )
        head_grads = masked_add(head_grads, head_terms, valid)
        vector_terms = tuple(
            (
                jnp.stack([head_part, unit_part])
                for head_part, unit_part in zip(head_vectors, unit_vectors)
            )
        )
        vector_grads = masked_add(vector_grads, vector_terms, valid)
        grads_all = jnp.where(
            valid, lax.dynamic_update_index_in_dim(grads_all, grad_in, slot, 0), grads_all
        )
        if tick + 1 < ticks:
            incoming = shifted(grad_in.astype(jnp.bfloat16), "section", -1)
    summed = (
        lax.psum(unit_grads[0].astype(jnp.bfloat16), "dp").astype(jnp.float32),
        lax.psum(unit_grads[1].astype(jnp.bfloat16), "dp").astype(jnp.float32),
        lax.psum(unit_grads[2].astype(jnp.bfloat16), "dp").astype(jnp.float32),
        lax.psum(head_grads[0].astype(jnp.bfloat16), "dp").astype(jnp.float32),
        lax.psum(head_grads[1].astype(jnp.bfloat16), "dp").astype(jnp.float32),
        lax.psum(head_grads[2].astype(jnp.bfloat16), "dp").astype(jnp.float32),
    )
    unit_grads = summed[:3]
    head_grads = summed[3:]
    vector_grads = lax.psum((vector_grads[0], vector_grads[1], vector_grads[2]), ("mp", "dp"))
    return (
        results_all[None],
        grads_all[None],
        vector_grads[0][None],
        vector_grads[1][None],
        head_grads[0].reshape(1, width, 3, local_width),
        head_grads[1][None],
        head_grads[2][None],
        unit_grads[0][None],
        unit_grads[1][None],
        unit_grads[2][None],
        vector_grads[2][None],
    )


def solution(mesh):
    in_specs = (
        P("dp", "mp", None),
        P("dp", "mp", None),
        P("dp", None),
        P("section", None, None),
        P("section", None, None),
        P("section", None, None, "mp"),
        P("section", None, "mp"),
        P("section", "mp", None),
        P("section", None, "mp"),
        P("section", "mp"),
        P("section", "mp", None),
        P("section", None, None),
    )
    out_specs = (
        P("section", "dp", "mp", None),
        P("section", "dp", "mp", None),
        P("section", None, None),
        P("section", None, None),
        P("section", None, None, "mp"),
        P("section", None, "mp"),
        P("section", "mp", None),
        P("section", None, "mp"),
        P("section", "mp"),
        P("section", "mp", None),
        P("section", None, None),
    )
    return jax.shard_map(
        per_device, mesh=mesh, in_specs=in_specs, out_specs=out_specs, check_vma=False
    )
```

profile of v0, /device:TPU:0, one launch (start us, length us, event | category | flops | bytes accessed | tf_op | source)
XLA Modules:
  0.0 1633.5 jit_solution(3736711797449079322)
XLA Ops:
  15.2 37.3 %all-gather.19.cloned.1.call-done = bf16[1024,768]{1,0:T(8,128)(2,1)} async-done(((bf16[256,768]{1,0:T(8,128)(2,1)}), bf16[1024,768]{1,0:T(8,128)(2,1)}) %all-gather.19.cloned.1.call-update) | async-done | bytes 1572880 | tf_op jit(solution)/shard_map/all_gather | solution.py:151
  56.2 24.1 %while.192 = (s32[]{:T(128)}, bf16[2,3,512,64]{2,3,1,0:T(8,128)(2,1)S(1)}, s32[1024]{0:T(1024)S(1)}, s32[2]{0:T(128)S(1)}, bf16[3,1024,64]{1,2,0:T(8,128)(2,1)},...) while((s32[]{:T(128)}, ...), condition=%wide.region_7.8_spmd, body=%wide.region_4.7_spmd.sunk | while | flops 415238656 | bytes 15042751 | solution.py:64
  82.9 34.2 %reduce-scatter.16.cloned.1.call-done = bf16[256,768]{1,0:T(8,128)(2,1)} async-done(((bf16[1024,768]{1,0:T(8,128)(2,1)}), bf16[256,768]{1,0:T(8,128)(2,1)}) %reduce-scatter.16.cloned.1.call-update) | async-done | bytes 393232 | tf_op jit(solution)/shard_map/reduce_scatter | solution.py:161
  121.8 36.1 %all-gather.21.cloned.1.call-done = bf16[1024,768]{1,0:T(8,128)(2,1)} async-done(((bf16[256,768]{1,0:T(8,128)(2,1)}), bf16[1024,768]{1,0:T(8,128)(2,1)}) %all-gather.21.cloned.1.call-update) | async-done | bytes 1572880 | tf_op jit(solution)/shard_map/all_gather | solution.py:151
  163.9 34.2 %reduce-scatter.18.cloned.1.call-done = bf16[256,768]{1,0:T(8,128)(2,1)} async-done(((bf16[1024,768]{1,0:T(8,128)(2,1)}), bf16[256,768]{1,0:T(8,128)(2,1)}) %reduce-scatter.18.cloned.1.call-update) | async-done | bytes 393232 | tf_op jit(solution)/shard_map/reduce_scatter | solution.py:161
  205.5 37.1 %all-gather.23.cloned.1.call-done = bf16[1024,768]{1,0:T(8,128)(2,1)} async-done(((bf16[256,768]{1,0:T(8,128)(2,1)}), bf16[1024,768]{1,0:T(8,128)(2,1)}) %all-gather.23.cloned.1.call-update) | async-done | bytes 1572880 | tf_op jit(solution)/shard_map/all_gather | solution.py:151
  247.2 27.7 %while.193 = (s32[]{:T(128)}, bf16[2,3,512,64]{2,3,1,0:T(8,128)(2,1)}, s32[1024]{0:T(1024)S(1)}, s32[2]{0:T(128)S(1)}, bf16[3,1024,64]{1,2,0:T(8,128)(2,1)}, /*i...) while((s32[]{:T(128)}, ...), condition=%wide.region_19.20_spmd, body=%wide.region_16.19_spmd.sunk | while | flops 415238656 | bytes 15040703 | solution.py:64
  250.2 6.2 fusion.632
  264.1 6.2 fusion.632
  281.9 34.2 %reduce-scatter.20.cloned.1.call-done = bf16[256,768]{1,0:T(8,128)(2,1)} async-done(((bf16[1024,768]{1,0:T(8,128)(2,1)}), bf16[256,768]{1,0:T(8,128)(2,1)}) %reduce-scatter.20.cloned.1.call-update) | async-done | bytes 393232 | tf_op jit(solution)/shard_map/reduce_scatter | solution.py:161
  320.8 36.2 %all-gather.25.cloned.1.call-done = bf16[1024,768]{1,0:T(8,128)(2,1)} async-done(((bf16[256,768]{1,0:T(8,128)(2,1)}), bf16[1024,768]{1,0:T(8,128)(2,1)}) %all-gather.25.cloned.1.call-update) | async-done | bytes 1572880 | tf_op jit(solution)/shard_map/all_gather | solution.py:151
  356.9 5.9 convolution_convert_fusion.11
  362.9 34.2 %reduce-scatter.22.cloned.1.call-done = bf16[256,768]{1,0:T(8,128)(2,1)} async-done(((bf16[1024,768]{1,0:T(8,128)(2,1)}), bf16[256,768]{1,0:T(8,128)(2,1)}) %reduce-scatter.22.cloned.1.call-update) | async-done | bytes 393232 | tf_op jit(solution)/shard_map/reduce_scatter | solution.py:161
  406.5 35.5 %all-gather.33.cloned.1.call-done = bf16[1024,768]{1,0:T(8,128)(2,1)} async-done(((bf16[256,768]{1,0:T(8,128)(2,1)}), bf16[1024,768]{1,0:T(8,128)(2,1)}) %all-gather.33.cloned.1.call-update) | async-done | bytes 1572880 | tf_op jit(solution)/shard_map/all_gather | solution.py:151
  446.8 19.3 %while.195 = (s32[]{:T(128)}, bf16[2,3,512,64]{2,3,1,0:T(8,128)(2,1)}, f32[2,3,512]{2,1,0:T(4,128)}, s32[1024]{0:T(1024)S(1)}, s32[2]{0:T(128)}, /*index=5*/bf16...) while((s32[]{:T(128)}, ...), condition=%wide.region_43.44_spmd, body=%wide.region_40.43_spmd.sunk | while | flops 424673280 | bytes 25671996 | solution.py:64
  474.1 33.5 %reduce-scatter.28.cloned.1.call-done = bf16[256,768]{1,0:T(8,128)(2,1)} async-done(((bf16[1024,768]{1,0:T(8,128)(2,1)}), bf16[256,768]{1,0:T(8,128)(2,1)}) %reduce-scatter.28.cloned.1.call-update) | async-done | bytes 393232 | tf_op jit(solution)/shard_map/reduce_scatter | solution.py:161
  514.9 31.0 %all-gather.27.cloned.1.call-done = bf16[1024,768]{1,0:T(8,128)(2,1)} async-done(((bf16[256,768]{1,0:T(8,128)(2,1)}), bf16[1024,768]{1,0:T(8,128)(2,1)}) %all-gather.27.cloned.1.call-update) | async-done | bytes 1572880 | tf_op jit(solution)/shard_map/all_gather | solution.py:151
  550.5 27.9 %while.194 = (s32[]{:T(128)}, bf16[2,3,512,64]{2,3,1,0:T(8,128)(2,1)}, s32[1024]{0:T(1024)S(1)}, s32[2]{0:T(128)S(1)}, bf16[3,1024,64]{1,2,0:T(8,128)(2,1)}, /*i...) while((s32[]{:T(128)}, ...), condition=%wide.region_31.32_spmd, body=%wide.region_28.31_spmd.sunk | while | flops 415238656 | bytes 15040703 | solution.py:64
  553.5 6.3 fusion.638
  567.5 6.2 fusion.638
  589.8 32.1 %all-gather.31.cloned.1.call-done = bf16[1024,768]{1,0:T(8,128)(2,1)} async-done(((bf16[256,768]{1,0:T(8,128)(2,1)}), bf16[1024,768]{1,0:T(8,128)(2,1)}) %all-gather.31.cloned.1.call-update) | async-done | bytes 1572880 | tf_op jit(solution)/shard_map/all_gather | solution.py:151
  622.0 6.3 convert_reduce_fusion.2
  633.5 25.4 %reduce-scatter.24.cloned.1.call-done = bf16[256,768]{1,0:T(8,128)(2,1)} async-done(((bf16[1024,768]{1,0:T(8,128)(2,1)}), bf16[256,768]{1,0:T(8,128)(2,1)}) %reduce-scatter.24.cloned.1.call-update) | async-done | bytes 393232 | tf_op jit(solution)/shard_map/reduce_scatter | solution.py:161
  658.9 37.0 %reduce-scatter.30.cloned.1.call-done = bf16[256,768]{1,0:T(8,128)(2,1)} async-done(((bf16[1024,768]{1,0:T(8,128)(2,1)}), bf16[256,768]{1,0:T(8,128)(2,1)}) %reduce-scatter.30.cloned.1.call-update) | async-done | bytes 393232 | tf_op jit(solution)/shard_map/reduce_scatter | solution.py:161
  701.5 35.3 %all-gather.41.cloned.1.call-done = bf16[1024,768]{1,0:T(8,128)(2,1)} async-done(((bf16[256,768]{1,0:T(8,128)(2,1)}), bf16[1024,768]{1,0:T(8,128)(2,1)}) %all-gather.41.cloned.1.call-update) | async-done | bytes 1572880 | tf_op jit(solution)/shard_map/all_gather | solution.py:151
  742.4 19.3 %while.196 = (s32[]{:T(128)}, bf16[2,3,512,64]{2,3,1,0:T(8,128)(2,1)}, f32[2,3,512]{2,1,0:T(4,128)}, s32[1024]{0:T(1024)S(1)}, s32[2]{0:T(128)}, /*index=5*/bf16...) while((s32[]{:T(128)}, ...), condition=%wide.region_63.64_spmd, body=%wide.region_60.63_spmd.sunk | while | flops 424673280 | bytes 27244888 | solution.py:64
  770.4 33.0 %reduce-scatter.34.cloned.1.call-done = bf16[256,768]{1,0:T(8,128)(2,1)} async-done(((bf16[1024,768]{1,0:T(8,128)(2,1)}), bf16[256,768]{1,0:T(8,128)(2,1)}) %reduce-scatter.34.cloned.1.call-update) | async-done | bytes 393232 | tf_op jit(solution)/shard_map/reduce_scatter | solution.py:161
  810.3 35.9 %all-gather.37.cloned.1.call-done = bf16[1024,768]{1,0:T(8,128)(2,1)} async-done(((bf16[256,768]{1,0:T(8,128)(2,1)}), bf16[1024,768]{1,0:T(8,128)(2,1)}) %all-gather.37.cloned.1.call-update) | async-done | bytes 1572880 | tf_op jit(solution)/shard_map/all_gather | solution.py:151
  849.8 24.9 %while.198 = (s32[]{:T(128)}, f32[3,1024,64]{1,2,0:T(8,128)S(1)}, f32[3,1024,64]{1,2,0:T(8,128)}, bf16[2,3,512,64]{2,3,1,0:T(8,128)(2,1)}, s32[1024]{0:T(1024)S(...) while((s32[]{:T(128)}, f32[3,1024,64]{1,2,0:T(8,128)S(1)}, ...), condition=%wide.region_52.53_spmd.clone, body=%wide.region_50.52_spmd.clone.sunk | while | flops 1034452992 | bytes 67439136 | solution.py:106
  881.9 34.0 %reduce-scatter.32.cloned.1.call-done = bf16[256,768]{1,0:T(8,128)(2,1)} async-done(((bf16[1024,768]{1,0:T(8,128)(2,1)}), bf16[256,768]{1,0:T(8,128)(2,1)}) %reduce-scatter.32.cloned.1.call-update) | async-done | bytes 393232 | tf_op jit(solution)/shard_map/reduce_scatter | solution.py:161
  933.7 25.6 %all-gather.49.cloned.1.call-done = bf16[1024,768]{1,0:T(8,128)(2,1)} async-done(((bf16[256,768]{1,0:T(8,128)(2,1)}), bf16[1024,768]{1,0:T(8,128)(2,1)}) %all-gather.49.cloned.1.call-update) | async-done | bytes 1572880 | tf_op jit(solution)/shard_map/all_gather | solution.py:151
  963.0 34.4 %all-gather.43.cloned.1.call-done = bf16[1024,768]{1,0:T(8,128)(2,1)} async-done(((bf16[256,768]{1,0:T(8,128)(2,1)}), bf16[1024,768]{1,0:T(8,128)(2,1)}) %all-gather.43.cloned.1.call-update) | async-done | bytes 1572880 | tf_op jit(solution)/shard_map/all_gather | solution.py:151
  1001.9 33.6 %all-gather.39.cloned.1.call-done = bf16[1024,768]{1,0:T(8,128)(2,1)} async-done(((bf16[256,768]{1,0:T(8,128)(2,1)}), bf16[1024,768]{1,0:T(8,128)(2,1)}) %all-gather.39.cloned.1.call-update) | async-done | bytes 1572880 | tf_op jit(solution)/shard_map/all_gather | solution.py:151
  1035.6 6.3 convert_reduce_fusion.1
  1047.6 18.8 %while.197 = (s32[]{:T(128)}, bf16[2,3,512,64]{2,3,1,0:T(8,128)(2,1)}, f32[2,3,512]{2,1,0:T(4,128)}, s32[1024]{0:T(1024)S(1)}, s32[2]{0:T(128)S(1)}, /*index=5*/...) while((s32[]{:T(128)}, ...), condition=%wide.region_83.84_spmd, body=%wide.region_80.83_spmd.sunk | while | flops 424673280 | bytes 25569540 | solution.py:64
  1083.0 34.1 %reduce-scatter.40.cloned.1.call-done = bf16[256,768]{1,0:T(8,128)(2,1)} async-done(((bf16[1024,768]{1,0:T(8,128)(2,1)}), bf16[256,768]{1,0:T(8,128)(2,1)}) %reduce-scatter.40.cloned.1.call-update) | async-done | bytes 393232 | tf_op jit(solution)/shard_map/reduce_scatter | solution.py:161
  1123.8 36.0 %all-gather.45.cloned.1.call-done = bf16[1024,768]{1,0:T(8,128)(2,1)} async-done(((bf16[256,768]{1,0:T(8,128)(2,1)}), bf16[1024,768]{1,0:T(8,128)(2,1)}) %all-gather.45.cloned.1.call-update) | async-done | bytes 1572880 | tf_op jit(solution)/shard_map/all_gather | solution.py:151
  1164.0 27.9 %while.199 = (s32[]{:T(128)}, f32[3,1024,64]{1,2,0:T(8,128)S(1)}, f32[3,1024,64]{1,2,0:T(8,128)}, bf16[2,3,512,64]{2,3,1,0:T(8,128)(2,1)}, s32[1024]{0:T(1024)S(...) while((s32[]{:T(128)}, f32[3,1024,64]{1,2,0:T(8,128)S(1)}, ...), condition=%wide.region_72.73_spmd.clone, body=%wide.region_70.72_spmd.clone.sunk | while | flops 1034452992 | bytes 69011896 | solution.py:106
  1201.2 33.5 %reduce-scatter.38.cloned.1.call-done = bf16[256,768]{1,0:T(8,128)(2,1)} async-done(((bf16[1024,768]{1,0:T(8,128)(2,1)}), bf16[256,768]{1,0:T(8,128)(2,1)}) %reduce-scatter.38.cloned.1.call-update) | async-done | bytes 393232 | tf_op jit(solution)/shard_map/reduce_scatter | solution.py:161
  1249.7 30.6 %all-gather.51.cloned.1.call-done = bf16[1024,768]{1,0:T(8,128)(2,1)} async-done(((bf16[256,768]{1,0:T(8,128)(2,1)}), bf16[1024,768]{1,0:T(8,128)(2,1)}) %all-gather.51.cloned.1.call-update) | async-done | bytes 1572880 | tf_op jit(solution)/shard_map/all_gather | solution.py:151
  1284.8 33.6 %all-gather.47.cloned.1.call-done = bf16[1024,768]{1,0:T(8,128)(2,1)} async-done(((bf16[256,768]{1,0:T(8,128)(2,1)}), bf16[1024,768]{1,0:T(8,128)(2,1)}) %all-gather.47.cloned.1.call-update) | async-done | bytes 1572880 | tf_op jit(solution)/shard_map/all_gather | solution.py:151
  1318.5 6.3 convert_reduce_fusion
  1329.8 33.0 %reduce-scatter.42.cloned.1.call-done = bf16[256,768]{1,0:T(8,128)(2,1)} async-done(((bf16[1024,768]{1,0:T(8,128)(2,1)}), bf16[256,768]{1,0:T(8,128)(2,1)}) %reduce-scatter.42.cloned.1.call-update) | async-done | bytes 393232 | tf_op jit(solution)/shard_map/reduce_scatter | solution.py:161
  1373.2 35.0 %all-gather.53.cloned.1.call-done = bf16[1024,768]{1,0:T(8,128)(2,1)} async-done(((bf16[256,768]{1,0:T(8,128)(2,1)}), bf16[1024,768]{1,0:T(8,128)(2,1)}) %all-gather.53.cloned.1.call-update) | async-done | bytes 1572880 | tf_op jit(solution)/shard_map/all_gather | solution.py:151
  1411.9 27.4 %while.200 = (s32[]{:T(128)}, f32[3,1024,64]{1,2,0:T(8,128)S(1)}, f32[3,1024,64]{1,2,0:T(8,128)}, bf16[2,3,512,64]{2,3,1,0:T(8,128)(2,1)}, s32[1024]{0:T(1024)S(...) while((s32[]{:T(128)}, f32[3,1024,64]{1,2,0:T(8,128)S(1)}, ...), condition=%wide.region_92.93_spmd.clone, body=%wide.region_90.92_spmd.clone.sunk | while | flops 1034452992 | bytes 65866116 | solution.py:106
  1506.0 10.5 all-reduce.1
  1525.8 73.7 %all-reduce = (f32[1,2,768]{2,1,0:T(2,128)}, f32[1,2,768]{2,1,0:T(2,128)}, f32[1,2,768]{2,1,0:T(2,128)}) all-reduce(f32[1,2,768]{2,1,0:T(2,128)} %fusion.389, f32[1,2,768]{2,1,0:T(2,128)} %fusion.392, f32[1,2,768]{2,1,0:T(2,128)} %fusion.395), channel_id=1, replica_groups=mesh['section'=2,'mp'=4,'dp'=4] {'mp','dp'}, use_global_device_ids=true, to_apply=%region_102.103 | all-reduce | flops 4608 | bytes 36864 | tf_op jit(solution)/shard_map/psum | solution.py:396
  1605.5 13.3 all-reduce.5.cloned.1.call-done
  (877 shorter events, 511.0 us)
Async XLA Ops:
  7.2 150.8 %copy-start = (bf16[1,768,768]{2,1,0:T(8,128)(2,1)S(1)}, bf16[1,768,768]{2,1,0:T(8,128)(2,1)}, u32[]{:S(2)}) copy-start(bf16[1,768,768]{2,1,0:T(8,128)(2,1)} %param.38) | copy-start | bytes 3538948
  7.2 45.3 %all-gather.19.cloned.1.call-start = ((), (), s32[]{:S(2)}) async-start(), calls=%async_computation.15 | async-start | bytes 1966080 | tf_op jit(solution)/shard_map/all_gather | solution.py:151
  10.5 193.6 %copy-start.88 = (f32[768]{0:T(1024)}, f32[768]{0:T(1024)S(1)}, u32[]{:S(2)}) copy-start(f32[768]{0:T(1024)S(1)} %get-tuple-element.807) | copy-start | bytes 9220
  10.5 308.1 %copy-start.82 = (f32[768]{0:T(1024)}, f32[768]{0:T(1024)S(1)}, u32[]{:S(2)}) copy-start(f32[768]{0:T(1024)S(1)} %get-tuple-element.808) | copy-start | bytes 9220
  10.6 688.3 %copy-start.73 = (f32[768]{0:T(1024)}, f32[768]{0:T(1024)S(1)}, u32[]{:S(2)}) copy-start(f32[768]{0:T(1024)S(1)} %get-tuple-element.1053) | copy-start | bytes 9220
  12.5 104.6 %reduce-scatter.16.cloned.1.call-start = ((), (), s32[]{:S(2)}) async-start(), calls=%async_computation.16 | async-start | bytes 1966080 | tf_op jit(solution)/shard_map/reduce_scatter | solution.py:161
  15.1 227.5 %copy-start.131 = (f32[576]{0:T(1024)}, f32[576]{0:T(1024)S(1)}, u32[]{:S(2)}) copy-start(f32[576]{0:T(1024)S(1)} %pad_maximum_fusion) | copy-start | bytes 6916
  82.8 75.1 %all-gather.21.cloned.1.call-start = ((), (), s32[]{:S(2)}) async-start(), calls=%async_computation.17 | async-start | bytes 1966080 | tf_op jit(solution)/shard_map/all_gather | solution.py:151
  82.9 115.3 %copy-start.90 = (f32[768]{0:T(1024)}, f32[768]{0:T(1024)S(1)}, u32[]{:S(2)}) copy-start(f32[768]{0:T(1024)S(1)} %get-tuple-element.803) | copy-start | bytes 9220
  121.7 76.4 %reduce-scatter.18.cloned.1.call-start = ((), (), s32[]{:S(2)}) async-start(), calls=%async_computation.18 | async-start | bytes 1966080 | tf_op jit(solution)/shard_map/reduce_scatter | solution.py:161
  163.9 78.8 %all-gather.23.cloned.1.call-start = ((), (), s32[]{:S(2)}) async-start(), calls=%async_computation.19 | async-start | bytes 1966080 | tf_op jit(solution)/shard_map/all_gather | solution.py:151
  200.3 3.3 collective-permute-start
  205.2 111.0 %reduce-scatter.20.cloned.1.call-start = ((), (), s32[]{:S(2)}) async-start(), calls=%async_computation.20 | async-start | bytes 1966080 | tf_op jit(solution)/shard_map/reduce_scatter | solution.py:161
  281.9 75.1 %all-gather.25.cloned.1.call-start = ((), (), s32[]{:S(2)}) async-start(), calls=%async_computation.21 | async-start | bytes 1966080 | tf_op jit(solution)/shard_map/all_gather | solution.py:151
  320.7 76.4 %reduce-scatter.22.cloned.1.call-start = ((), (), s32[]{:S(2)}) async-start(), calls=%async_computation.22 | async-start | bytes 1966080 | tf_op jit(solution)/shard_map/reduce_scatter | solution.py:161
  362.9 79.2 %all-gather.33.cloned.1.call-start = ((), (), s32[]{:S(2)}) async-start(), calls=%async_computation.28 | async-start | bytes 1966080 | tf_op jit(solution)/shard_map/all_gather | solution.py:151
  399.5 3.1 collective-permute-start.1
  402.8 293.1 %copy-start.7 = (bf16[256,768]{1,0:T(8,128)(2,1)}, bf16[256,768]{1,0:T(8,128)(2,1)S(1)}, u32[]{:S(2)}) copy-start(bf16[256,768]{1,0:T(8,128)(2,1)S(1)} %get-tuple-element.987) | copy-start | bytes 1179652
  405.6 102.1 %reduce-scatter.28.cloned.1.call-start = ((), (), s32[]{:S(2)}) async-start(), calls=%async_computation.29 | async-start | bytes 1966080 | tf_op jit(solution)/shard_map/reduce_scatter | solution.py:161
  473.3 72.5 %all-gather.27.cloned.1.call-start = ((), (), s32[]{:S(2)}) async-start(), calls=%async_computation.23 | async-start | bytes 1966080 | tf_op jit(solution)/shard_map/all_gather | solution.py:151
  474.1 111.3 %all-gather.35.cloned.1.call-start = ((), (), s32[]{:S(2)}) async-start(), calls=%async_computation.30 | async-start | bytes 1966080 | tf_op jit(solution)/shard_map/all_gather | solution.py:151
  512.3 109.7 %all-gather.31.cloned.1.call-start = ((), (), s32[]{:S(2)}) async-start(), calls=%async_computation.27 | async-start | bytes 1966080 | tf_op jit(solution)/shard_map/all_gather | solution.py:151
  514.2 144.7 %reduce-scatter.24.cloned.1.call-start = ((), (), s32[]{:S(2)}) async-start(), calls=%async_computation.24 | async-start | bytes 1966080 | tf_op jit(solution)/shard_map/reduce_scatter | solution.py:161
  585.3 110.6 %reduce-scatter.30.cloned.1.call-start = ((), (), s32[]{:S(2)}) async-start(), calls=%async_computation.31 | async-start | bytes 1966080 | tf_op jit(solution)/shard_map/reduce_scatter | solution.py:161
  632.1 104.8 %all-gather.41.cloned.1.call-start = ((), (), s32[]{:S(2)}) async-start(), calls=%async_computation.35 | async-start | bytes 1966080 | tf_op jit(solution)/shard_map/all_gather | solution.py:151
  700.6 102.8 %reduce-scatter.34.cloned.1.call-start = ((), (), s32[]{:S(2)}) async-start(), calls=%async_computation.36 | async-start | bytes 1966080 | tf_op jit(solution)/shard_map/reduce_scatter | solution.py:161
  769.0 77.2 %all-gather.37.cloned.1.call-start = ((), (), s32[]{:S(2)}) async-start(), calls=%async_computation.32 | async-start | bytes 1966080 | tf_op jit(solution)/shard_map/all_gather | solution.py:151
  810.0 105.9 %reduce-scatter.32.cloned.1.call-start = ((), (), s32[]{:S(2)}) async-start(), calls=%async_computation.33 | async-start | bytes 1966080 | tf_op jit(solution)/shard_map/reduce_scatter | solution.py:161
  881.6 77.7 %all-gather.49.cloned.1.call-start = ((), (), s32[]{:S(2)}) async-start(), calls=%async_computation.42 | async-start | bytes 1966080 | tf_op jit(solution)/shard_map/all_gather | solution.py:151
  923.1 74.3 %all-gather.43.cloned.1.call-start = ((), (), s32[]{:S(2)}) async-start(), calls=%async_computation.37 | async-start | bytes 1966080 | tf_op jit(solution)/shard_map/all_gather | solution.py:151
  923.8 111.7 %all-gather.39.cloned.1.call-start = ((), (), s32[]{:S(2)}) async-start(), calls=%async_computation.34 | async-start | bytes 1966080 | tf_op jit(solution)/shard_map/all_gather | solution.py:151
  928.2 3.6 collective-permute-start.2
  932.7 147.3 %reduce-scatter.36.cloned.1.call-start = ((), (), s32[]{:S(2)}) async-start(), calls=%async_computation.38 | async-start | bytes 1966080 | tf_op jit(solution)/shard_map/reduce_scatter | solution.py:161
  1045.7 71.3 %reduce-scatter.40.cloned.1.call-start = ((), (), s32[]{:S(2)}) async-start(), calls=%async_computation.43 | async-start | bytes 1966080 | tf_op jit(solution)/shard_map/reduce_scatter | solution.py:161
  1073.6 86.2 %all-gather.45.cloned.1.call-start = ((), (), s32[]{:S(2)}) async-start(), calls=%async_computation.39 | async-start | bytes 1966080 | tf_op jit(solution)/shard_map/all_gather | solution.py:151
  1123.6 111.1 %reduce-scatter.38.cloned.1.call-start = ((), (), s32[]{:S(2)}) async-start(), calls=%async_computation.40 | async-start | bytes 1966080 | tf_op jit(solution)/shard_map/reduce_scatter | solution.py:161
  1200.4 79.9 %all-gather.51.cloned.1.call-start = ((), (), s32[]{:S(2)}) async-start(), calls=%async_computation.44 | async-start | bytes 1966080 | tf_op jit(solution)/shard_map/all_gather | solution.py:151
  1244.1 74.3 %all-gather.47.cloned.1.call-start = ((), (), s32[]{:S(2)}) async-start(), calls=%async_computation.41 | async-start | bytes 1966080 | tf_op jit(solution)/shard_map/all_gather | solution.py:151
  1244.2 3.8 collective-permute-start.3
  1249.6 113.2 %reduce-scatter.42.cloned.1.call-start = ((), (), s32[]{:S(2)}) async-start(), calls=%async_computation.45 | async-start | bytes 1966080 | tf_op jit(solution)/shard_map/reduce_scatter | solution.py:161
  1328.6 79.7 %all-gather.53.cloned.1.call-start = ((), (), s32[]{:S(2)}) async-start(), calls=%async_computation.46 | async-start | bytes 1966080 | tf_op jit(solution)/shard_map/all_gather | solution.py:151
  1372.0 85.4 %all-gather.29.cloned.1.call-start = ((), (), s32[]{:S(2)}) async-start(), calls=%async_computation.25 | async-start | bytes 1966080 | tf_op jit(solution)/shard_map/all_gather | solution.py:151
  1372.8 146.2 %reduce-scatter.44.cloned.1.call-start = ((), (), s32[]{:S(2)}) async-start(), calls=%async_computation.47 | async-start | bytes 1966080 | tf_op jit(solution)/shard_map/reduce_scatter | solution.py:161
  1446.1 154.6 %reduce-scatter.26.cloned.1.call-start = ((), (), s32[]{:S(2)}) async-start(), calls=%async_computation.26 | async-start | bytes 1966080 | tf_op jit(solution)/shard_map/reduce_scatter | solution.py:161
  1463.4 155.4 %all-reduce.5.cloned.1.call-start = ((), (), s32[]{:S(2)}) async-start(), calls=%async_computation.48 | async-start | bytes 7077888 | tf_op jit(solution)/shard_map/psum | solution.py:390
  1499.9 100.8 %copy-start.31 = (bf16[256,768]{1,0:T(8,128)(2,1)S(1)}, bf16[256,768]{1,0:T(8,128)(2,1)}, u32[]{:S(2)}) copy-start(bf16[256,768]{1,0:T(8,128)(2,1)} %reduce-scatter.24.cloned.1.call-done) | copy-start | bytes 1179652
  1499.9 100.8 %copy-start.91 = (f32[768]{0:T(1024)S(1)}, f32[768]{0:T(1024)}, u32[]{:S(2)}) copy-start(f32[768]{0:T(1024)} %copy-done.90) | copy-start | bytes 9220
  1499.9 103.0 %copy-start.25 = (f32[256,768]{1,0:T(8,128)S(1)}, f32[256,768]{1,0:T(8,128)}, u32[]{:S(2)}) copy-start(f32[256,768]{1,0:T(8,128)} %copy-done.24) | copy-start | bytes 2359300
  (187 other events, 2293.6 us)
Sparse Core Ops, SparseCore 0:
  12.7 39.7 all-gather.18
  82.9 34.1 reduce-scatter.15
  121.9 36.0 all-gather.20
  164.0 34.1 reduce-scatter.17
  205.3 37.2 all-gather.22
  282.0 34.1 reduce-scatter.19
  320.8 36.0 all-gather.24
  363.0 34.1 reduce-scatter.21
  405.7 36.2 all-gather.32
  473.4 34.1 reduce-scatter.27
  509.8 36.0 all-gather.26
  547.9 35.9 all-gather.34
  586.0 35.9 all-gather.30
  624.7 34.1 reduce-scatter.23
  661.6 34.2 reduce-scatter.29
  700.7 36.0 all-gather.40
  769.2 34.1 reduce-scatter.33
  810.1 36.0 all-gather.36
  881.7 34.1 reduce-scatter.31
  923.2 36.0 all-gather.48
  961.4 35.9 all-gather.42
  999.6 35.9 all-gather.38
  1045.8 34.1 reduce-scatter.35
  1082.8 34.2 reduce-scatter.39
  1123.7 36.0 all-gather.44
  1200.5 34.1 reduce-scatter.37
  1244.2 36.0 all-gather.50
  1282.5 35.9 all-gather.46
  1328.7 34.1 reduce-scatter.41
  1372.2 36.0 all-gather.52
  1410.4 35.9 all-gather.28
  1448.7 34.1 reduce-scatter.43
  1485.0 34.2 reduce-scatter.25
  1524.0 94.7 all-reduce.4
where the time goes:
time: 1650 us; the launch traced here: 1630 us
  waiting for transfers between devices  973 us (59%)
  matrix products  270 us (16%)
  other arithmetic  160 us (10%)
  local copies, waits for them, and re-layouts  106 us (6%)
  blocking collectives  84.2 us (5%)
    all_gather x18, waiting for transfers between devices, spread_tokens(): return lax.all_gather(local, 'mp', axis=0, tiled=True)  545 us
    reduce_scatter x15, waiting for transfers between devices, sum_tokens(): lax.psum_scatter(term(jnp.int32(0), rows * lax.axis_size('mp')).astype(jn...  406 us
    psum x1, blocking collectives, per_device(): lax.psum((vector_grads[0], vector_grads[1], vector_grads[2]), ('mp', 'dp'))  73.7 us
    dot_general x15, matrix products, term(): lax.dot_general(left, right, (((1,), (contract,)), ((), ())), preferred_e...  49.1 us
    dot_general x12, matrix products, one_block(): jnp.einsum('hqk,hkd->hqd', probs, values, preferred_element_type=jnp.floa...  41.7 us
    sub x6, matrix products, one_block(): weights = jnp.exp(scores - top)  36.7 us
  transfers between devices with their start and end apart: 38, of which 34 were waited for; matrix products, arithmetic and copies ran while one was open for 14% of the time, Pallas kernels for 0%

commit v1 on v0

v1 whole, which is shorter than its diff:
```python
from functools import partial

import jax
import jax.numpy as jnp
from jax import lax
from jax.experimental import pallas as pl
from jax.experimental.pallas import tpu as pltpu
from jax.sharding import PartitionSpec as P

HEAD = 64
branch_scale = 12.0 ** (-0.5)
norm_eps = 1e-05
masked_score = -1000000000.0
block = 256
cube = 0.044715
root = 0.7978845608

f32 = jnp.float32
bf16 = jnp.bfloat16


def mm(left, right):
    return jnp.dot(left, right, preferred_element_type=f32)


def mm_nt(left, right):
    return lax.dot_general(left, right, (((1,), (1,)), ((), ())), preferred_element_type=f32)


def mm_tn(left, right):
    return lax.dot_general(left, right, (((0,), (0,)), ((), ())), preferred_element_type=f32)


def normalize(values):
    mean = jnp.mean(values, axis=-1, keepdims=True)
    centred = values - mean
    spread = jnp.mean(centred * centred, axis=-1, keepdims=True)
    rstd = lax.rsqrt(spread + norm_eps)
    return centred * rstd, rstd


def norm_back(normal, rstd, grad, gain):
    scaled = grad * gain
    first = jnp.mean(scaled, axis=-1, keepdims=True)
    second = jnp.mean(scaled * normal, axis=-1, keepdims=True)
    return (scaled - first - normal * second) * rstd


def head_lanes(heads):
    found = []
    for head in range(heads):
        start = (head // 2) * 2 * HEAD
        width = min(2 * HEAD, heads * HEAD - start)
        found.append((start, width, head % 2))
    return found


def own_lanes(value, width, upper):
    if width == HEAD:
        return value
    lane = lax.broadcasted_iota(jnp.int32, value.shape, 1)
    keep = (lane >= HEAD) if upper else (lane < HEAD)
    return jnp.where(keep, value, jnp.zeros_like(value))


def block_mask(seg_col, seg_row, rows, count):
    same = seg_col[0:count, :] == seg_row[:, rows]
    key = lax.broadcasted_iota(jnp.int32, (count, rows.stop - rows.start), 0)
    query = lax.broadcasted_iota(jnp.int32, (count, rows.stop - rows.start), 1) + rows.start
    return same & (key <= query)


def attend_kernel(q_ref, k_ref, v_ref, seg_col, seg_row, out_ref, logsum_ref):
    length, width = q_ref.shape
    for start in range(0, length, block):
        rows = slice(start, start + block)
        count = start + block
        mask = block_mask(seg_col, seg_row, rows, count)
        mixed = []
        for head, (lane, lanes, upper) in enumerate(head_lanes(width // HEAD)):
            cols = slice(lane, lane + lanes)
            queries = own_lanes(q_ref[rows, cols], lanes, upper) * bf16(HEAD ** (-0.5))
            scores = mm_nt(k_ref[0:count, cols], queries)
            scores = jnp.where(mask, scores, masked_score)
            top = jnp.max(scores, axis=0, keepdims=True)
            weights = jnp.exp(scores - top)
            total = jnp.sum(weights, axis=0, keepdims=True)
            result = mm_tn(v_ref[0:count, cols], weights.astype(bf16)) / total
            logsum_ref[head : head + 1, rows] = top + jnp.log(total)
            mixed.append((lanes, result))
        for pair in range(0, len(mixed), 2):
            lane = pair * HEAD
            lanes, result = mixed[pair]
            if lanes > HEAD:
                result = jnp.concatenate([result[:HEAD], mixed[pair + 1][1][HEAD:]], axis=0)
            out_ref[rows, lane : lane + lanes] = result.T.astype(bf16)


def attend(q, k, v, seg_col, seg_row):
    length, width = q.shape
    return pl.pallas_call(
        attend_kernel,
        out_shape=(
            jax.ShapeDtypeStruct((length, width), bf16),
            jax.ShapeDtypeStruct((width // HEAD, length), f32),
        ),
        in_specs=[pl.BlockSpec(memory_space=pltpu.VMEM)] * 5,
        out_specs=[pl.BlockSpec(memory_space=pltpu.VMEM)] * 2,
        compiler_params=pltpu.CompilerParams(vmem_limit_bytes=40 * 2**20),
        name="attend",
    )(q, k, v, seg_col, seg_row)


def attend_back_kernel(
    q_ref, k_ref, v_ref, grad_ref, logsum_ref, seg_col, seg_row, dq_ref, dk_ref, dv_ref, dk_sum, dv_sum
):
    length, width = q_ref.shape
    dk_sum[...] = jnp.zeros_like(dk_sum)
    dv_sum[...] = jnp.zeros_like(dv_sum)
    scale = bf16(HEAD ** (-0.5))
    for start in range(0, length, block):
        rows = slice(start, start + block)
        count = start + block
        mask = block_mask(seg_col, seg_row, rows, count)
        mixed = []
        for head, (lane, lanes, upper) in enumerate(head_lanes(width // HEAD)):
            cols = slice(lane, lane + lanes)
            queries = own_lanes(q_ref[rows, cols], lanes, upper) * scale
            grads = own_lanes(grad_ref[rows, cols], lanes, upper)
            keys = k_ref[0:count, cols]
            scores = mm_nt(keys, queries)
            scores = jnp.where(mask, scores, masked_score)
            probs = jnp.exp(scores - logsum_ref[head : head + 1, rows])
            grad_probs = mm_nt(v_ref[0:count, cols], grads)
            dv_sum[0:count, cols] += mm(probs.astype(bf16), grads)
            term = probs * grad_probs
            delta = jnp.sum(term, axis=0, keepdims=True)
            grad_scores = (term - probs * delta).astype(bf16)
            dk_sum[0:count, cols] += mm(grad_scores, queries)
            mixed.append((lanes, mm_tn(keys, grad_scores)))
        for pair in range(0, len(mixed), 2):
            lane = pair * HEAD
            lanes, result = mixed[pair]
            if lanes > HEAD:
                result = jnp.concatenate([result[:HEAD], mixed[pair + 1][1][HEAD:]], axis=0)
            dq_ref[rows, lane : lane + lanes] = (result.T * HEAD ** (-0.5)).astype(bf16)
    dk_ref[...] = dk_sum[...].astype(bf16)
    dv_ref[...] = dv_sum[...].astype(bf16)


def attend_back(q, k, v, grad, logsum, seg_col, seg_row):
    length, width = q.shape
    like = jax.ShapeDtypeStruct((length, width), bf16)
    return pl.pallas_call(
        attend_back_kernel,
        out_shape=(like, like, like),
        in_specs=[pl.BlockSpec(memory_space=pltpu.VMEM)] * 7,
        out_specs=[pl.BlockSpec(memory_space=pltpu.VMEM)] * 3,
        scratch_shapes=[pltpu.VMEM((length, width), f32)] * 2,
        compiler_params=pltpu.CompilerParams(vmem_limit_bytes=40 * 2**20),
        name="attend_back",
    )(q, k, v, grad, logsum, seg_col, seg_row)


def segment_ids(lengths, length):
    ends = jnp.cumsum(lengths)
    positions = jnp.arange(length, dtype=jnp.int32)
    segs = jnp.sum((positions[:, None] >= ends[None, :]).astype(jnp.int32), axis=-1)
    docs = lengths.shape[0]
    return jnp.where(segs < docs, segs, docs + positions)


def per_device(
    inputs,
    cotangent,
    lengths,
    norm_gains,
    norm_shifts,
    in_weight,
    in_bias,
    out_weight,
    up_weight,
    up_bias,
    down_weight,
    branch_bias,
):
    core = lax.axis_index("section")
    z = lax.axis_index("mp")
    dp = lax.axis_index("dp")
    copies = lax.axis_size("dp")
    mine = z // 2
    side = z % 2
    quarter, width = inputs.shape[1:]
    half = 2 * quarter
    length = 4 * quarter
    local = in_weight.shape[3]
    units = up_weight.shape[2]

    def at(c, m):
        return c * 4 + m

    every = [(c, m) for c in range(2) for m in range(4)]

    def route(value, pairs):
        return lax.ppermute(value, ("section", "mp"), pairs)

    swap_core = [(at(c, m), at(1 - c, m)) for c, m in every]
    swap_side = [(at(c, m), at(c, m ^ 1)) for c, m in every]
    swap_pair = [(at(c, m), at(c, m ^ 2)) for c, m in every]

    def pick(flag, yes, no):
        return jnp.where(flag, yes, no)

    def rows_in(array):
        pairs = [(at(c, m), at(c, m ^ 2)) for c, m in every if c == m // 2]
        far = route(pick(mine == 0, array[1], array[0]), pairs)
        here = pick(core == mine, pick(mine == 0, array[0], array[1]), far)
        there = route(here, swap_side)
        return pick(
            side == 0,
            jnp.concatenate([here, there], axis=0),
            jnp.concatenate([there, here], axis=0),
        )

    def fetch(array):
        part = array.shape[0] // copies
        piece = lax.dynamic_slice_in_dim(array, dp * part, part, 0)
        piece = route(piece, swap_pair)
        return lax.all_gather(piece, "dp", axis=0, tiled=True)

    def both_layers(array):
        other = route(array, swap_core)
        return [pick(core == layer, array, other) for layer in range(2)]

    mixing = in_weight[0].reshape(width, 3 * local)
    in_own, in_far = both_layers(mixing), both_layers(fetch(mixing))
    out_own, out_far = both_layers(out_weight[0]), both_layers(fetch(out_weight[0]))
    up_own, up_far = both_layers(up_weight[0]), both_layers(fetch(up_weight[0]))
    down_own, down_far = both_layers(down_weight[0]), both_layers(fetch(down_weight[0]))
    shard_vec = jnp.concatenate([in_bias[0].reshape(-1), up_bias[0]])
    far_vec = route(shard_vec, swap_pair)
    whole_vec = jnp.concatenate(
        [norm_gains[0].reshape(-1), norm_shifts[0].reshape(-1), branch_bias[0].reshape(-1)]
    )
    vecs = both_layers(jnp.concatenate([shard_vec, far_vec, whole_vec]))

    def unpack(vec):
        found = []
        at_ = 0
        for size, shape in (
            (2 * local, (2, local)),
            (units, (units,)),
            (2 * local, (2, local)),
            (units, (units,)),
            (2 * width, (2, width)),
            (2 * width, (2, width)),
            (2 * width, (2, width)),
        ):
            found.append(vec[at_ : at_ + size].reshape(shape))
            at_ += size
        return found

    row_lengths = pick(mine == 0, lengths[0], lengths[1])
    segs = segment_ids(row_lengths, length)
    seg_col, seg_row = segs[:, None], segs[None, :]

    def to_heads(packed):
        keep = pick(core == 0, packed[0], packed[1])
        give = pick(core == 0, packed[1], packed[0])
        got = route(give, swap_core)
        return pick(
            core == 0,
            jnp.concatenate([keep, got], axis=0),
            jnp.concatenate([got, keep], axis=0),
        )

    def to_tokens(whole):
        keep = lax.dynamic_slice_in_dim(whole, core * half, half, 0)
        give = lax.dynamic_slice_in_dim(whole, (1 - core) * half, half, 0)
        got = route(give, swap_core)
        return pick(core == 0, jnp.stack([keep, got]), jnp.stack([got, keep]))

    def pair_sum(partial_sum):
        low = partial_sum.astype(bf16)
        return low.astype(f32) + route(low, swap_side).astype(f32)

    state = rows_in(inputs)
    grad = rows_in(cotangent).astype(f32)
    saved = []
    outputs = []
    for layer in range(2):
        bias_own, up_b_own, bias_far, up_b_far, gains, shifts, branch = unpack(vecs[layer])
        w_in = (in_own[layer], in_far[layer])
        zero = jnp.zeros((local,), f32)
        qkv_bias = [jnp.concatenate([b[0], zero, b[1]]) for b in (bias_own, bias_far)]
        start = state.astype(f32)
        normal, rstd = normalize(start)
        normed = (normal * gains[0] + shifts[0]).astype(bf16)
        packed = jnp.stack([(mm(normed, w_in[k]) + qkv_bias[k]).astype(bf16) for k in range(2)])
        heads = to_heads(packed)
        q, k, v = (heads[:, j * local : (j + 1) * local] for j in range(3))
        mixed, logsum = attend(q, k, v, seg_col, seg_row)
        attended = to_tokens(mixed)
        part = mm(attended[0], out_own[layer]) + mm(attended[1], out_far[layer])
        middle = start + branch_scale * (pair_sum(part) + branch[0])
        normal2, rstd2 = normalize(middle)
        upper = (normal2 * gains[1] + shifts[1]).astype(bf16)
        hidden, slope = [], []
        for w, b in ((up_own[layer], up_b_own), (up_far[layer], up_b_far)):
            pre = mm(upper, w) + b
            curve = jnp.tanh(root * (pre + cube * pre * pre * pre))
            hidden.append((0.5 * pre * (1.0 + curve)).astype(bf16))
            slope.append(
                (
                    0.5 * (1.0 + curve)
                    + 0.5 * pre * (1.0 - curve * curve) * root * (1.0 + 3.0 * cube * pre * pre)
                ).astype(bf16)
            )
        part = mm(hidden[0], down_own[layer]) + mm(hidden[1], down_far[layer])
        result = middle + branch_scale * (pair_sum(part) + branch[1])
        saved.append((start, normed, q, k, v, logsum, attended, middle, upper, hidden, slope))
        state = result.astype(bf16)
        outputs.append(state)

    partials = [None, None]
    vectors = [None, None]
    grads_out = [None, None]
    for layer in (1, 0):
        start, normed, q, k, v, logsum, attended, middle, upper, hidden, slope = saved[layer]
        bias_own, up_b_own, bias_far, up_b_far, gains, shifts, branch = unpack(vecs[layer])
        gz = branch_scale * grad
        d_branch1 = jnp.sum(gz, axis=0)
        gz = gz.astype(bf16)
        d_pre, d_up, d_down, d_up_bias = [], [], [], []
        for i, w in enumerate((down_own[layer], down_far[layer])):
            dp_ = (mm_nt(gz, w) * slope[i].astype(f32)).astype(bf16)
            d_pre.append(dp_)
            d_down.append(mm_tn(hidden[i], gz).astype(bf16))
            d_up.append(mm_tn(upper, dp_).astype(bf16))
            d_up_bias.append(jnp.sum(dp_.astype(f32), axis=0))
        part = mm_nt(d_pre[0], up_own[layer]) + mm_nt(d_pre[1], up_far[layer])
        d_upper = pair_sum(part)
        normal2, rstd2 = normalize(middle)
        d_gain1 = jnp.sum(d_upper * normal2, axis=0)
        d_shift1 = jnp.sum(d_upper, axis=0)
        d_middle = grad + norm_back(normal2, rstd2, d_upper, gains[1])
        gy = branch_scale * d_middle
        d_branch0 = jnp.sum(gy, axis=0)
        gy = gy.astype(bf16)
        d_out = [mm_tn(attended[i], gy).astype(bf16) for i in range(2)]
        d_att = jnp.stack(
            [mm_nt(gy, w).astype(bf16) for w in (out_own[layer], out_far[layer])]
        )
        d_heads = to_heads(d_att)
        dq, dk, dv = attend_back(q, k, v, d_heads, logsum, seg_col, seg_row)
        d_mix = to_tokens(jnp.concatenate([dq, dk, dv], axis=1))
        d_in = [mm_tn(normed, d_mix[i]).astype(bf16) for i in range(2)]
        d_mix_sum = jnp.sum(d_mix.astype(f32), axis=1)
        part = mm_nt(d_mix[0], in_own[layer]) + mm_nt(d_mix[1], in_far[layer])
        d_normed = pair_sum(part)
        normal, rstd = normalize(start)
        d_gain0 = jnp.sum(d_normed * normal, axis=0)
        d_shift0 = jnp.sum(d_normed, axis=0)
        d_state = d_middle + norm_back(normal, rstd, d_normed, gains[0])
        low = d_state.astype(bf16)
        grads_out[layer] = low
        grad = low.astype(f32)
        partials[layer] = (d_in, d_out, d_up, d_down)
        shard_terms = [
            jnp.concatenate([d_mix_sum[i, :local], d_mix_sum[i, 2 * local :], d_up_bias[i]])
            for i in range(2)
        ]
        vectors[layer] = (
            shard_terms,
            jnp.concatenate([d_gain0, d_gain1, d_shift0, d_shift1, d_branch0, d_branch1]),
        )

    def reduce_layer(index, layer):
        own, far = partials[layer][index]
        got = route(pick(core == 0, far, own), swap_core)
        total = (pick(core == 0, own, far).astype(f32) + got.astype(f32)).astype(bf16)
        piece = lax.psum_scatter(total, "dp", scatter_dimension=0, tiled=True)
        cross = route(piece, [(at(1, m), at(0, m ^ 2)) for m in range(4)])
        return piece + cross

    final = []
    for index in range(4):
        first = reduce_layer(index, 0)
        second = reduce_layer(index, 1)
        second = route(second, [(at(0, m), at(1, m)) for m in range(4)])
        final.append(lax.all_gather(pick(core == 0, first, second), "dp", axis=0, tiled=True).astype(f32))
    g_in, g_out, g_up, g_down = final

    shard_sum, whole_sum = [], []
    for layer in range(2):
        (own, far), whole = vectors[layer]
        shard_sum.append(jnp.stack([own, far]))
        whole_sum.append(whole)
    shard_sum = jnp.stack(shard_sum)
    across = route(shard_sum[:, 1], swap_pair)
    shard_sum = lax.psum(shard_sum[:, 0] + across, ("section", "dp"))
    whole_sum = lax.psum(jnp.stack(whole_sum), ("section", "mp", "dp")) * 0.5
    shard_mine = pick(core == 0, shard_sum[0], shard_sum[1])
    whole_mine = pick(core == 0, whole_sum[0], whole_sum[1]).reshape(3, 2, width)

    def rows_out(pair):
        both = jnp.stack(pair)
        send = lax.dynamic_slice_in_dim(both, side * quarter, quarter, 1)
        far = route(send, [(at(c, m), at(c, m ^ 2)) for c, m in every if c != m // 2])
        rows = pick(mine == 0, jnp.stack([send, far], 1), jnp.stack([far, send], 1))
        other = route(
            pick(mine == 0, rows[1], rows[0]),
            [(at(c, m), at(1 - c, m)) for c, m in every if c == m // 2],
        )
        here = pick(core == 0, rows[0], rows[1])
        return pick(core == mine, here, other)

    section_outputs = rows_out(outputs)
    input_grads = rows_out(grads_out).astype(f32)
    return (
        section_outputs[None],
        input_grads[None],
        whole_mine[0][None],
        whole_mine[1][None],
        g_in.reshape(1, width, 3, local),
        shard_mine[: 2 * local].reshape(1, 2, local),
        g_out[None],
        g_up[None],
        shard_mine[2 * local :][None],
        g_down[None],
        whole_mine[2][None],
    )


def solution(mesh):
    in_specs = (
        P("dp", "mp", None),
        P("dp", "mp", None),
        P("dp", None),
        P("section", None, None),
        P("section", None, None),
        P("section", None, None, "mp"),
        P("section", None, "mp"),
        P("section", "mp", None),
        P("section", None, "mp"),
        P("section", "mp"),
        P("section", "mp", None),
        P("section", None, None),
    )
    out_specs = (
        P("section", "dp", "mp", None),
        P("section", "dp", "mp", None),
        P("section", None, None),
        P("section", None, None),
        P("section", None, None, "mp"),
        P("section", None, "mp"),
        P("section", "mp", None),
        P("section", None, "mp"),
        P("section", "mp"),
        P("section", "mp", None),
        P("section", None, None),
    )
    return jax.shard_map(
        per_device, mesh=mesh, in_specs=in_specs, out_specs=out_specs, check_vma=False
    )
```

time: 1650 us -> 659 us (0.40)
  waiting for transfers between devices: 973 us -> 202 us
  matrix products: 270 us -> 87.8 us
  other arithmetic: 160 us -> 85.7 us
  starting transfers between devices: 10.9 us -> 70.6 us
  local copies, waits for them, and re-layouts: 106 us -> 48.6 us
  blocking collectives: 84.2 us -> 110 us
  Pallas kernels: 0 us -> 25.7 us
    all_gather x18 -> x4, waiting for transfers between devices: 545 us -> 34.8 us  [the longest x2 19.7 us: fetch(): return lax.all_gather(piece, 'dp', axis=0, tiled=True)]
    reduce_scatter x15 -> x6, waiting for transfers between devices: 406 us -> 0.09 us  [reduce_layer(): piece = lax.psum_scatter(total, 'dp', scatter_dimension=0, tiled=True)]
    ppermute x4 -> x59, waiting for transfers between devices: 6.75 us -> 167 us  [route(): return lax.ppermute(value, ('section', 'mp'), pairs)]
    dot_general x90 -> x48, matrix products: 233 us -> 87.8 us  [the longest x16 34.8 us: mm_tn(): lax.dot_general(left, right, (((0,), (0,)), ((), ())), preferred_element_...]
    ppermute x4 -> x59, starting transfers between devices: 6.86 us -> 69.4 us  [route(): return lax.ppermute(value, ('section', 'mp'), pairs)]
    all_gather x0 -> x4, blocking collectives: none -> 48.7 us  [the longest x2 24.6 us: fetch(): return lax.all_gather(piece, 'dp', axis=0, tiled=True)]
    sub x6 -> x0, matrix products: 36.7 us -> none  [one_block(): weights = jnp.exp(scores - top)]
    reduce_sum x44 -> x19, other arithmetic: 59.2 us -> 27 us  [the longest x2 6.4 us: per_device(): d_branch0 = jnp.sum(gy, axis=0)]
  transfers between devices with their start and end apart: 38 -> 71, of which waited for: 34 -> 24; matrix products, arithmetic and copies ran while one was open for 14% -> 27% of each run, Pallas kernels for 0% -> 3%
where the time goes in v1:
time: 659 us; the launch traced here: 648 us
  waiting for transfers between devices  202 us (31%)
  blocking collectives  110 us (17%)
  matrix products  87.8 us (13%)
  other arithmetic  85.7 us (13%)
  starting transfers between devices  70.6 us (11%)
  local copies, waits for them, and re-layouts  48.6 us (7%)
  Pallas kernels  25.7 us (4%)
  between operations  16.7 us (3%)
    ppermute x59, waiting for transfers between devices, route(): return lax.ppermute(value, ('section', 'mp'), pairs)  167 us
    ppermute x59, starting transfers between devices, route(): return lax.ppermute(value, ('section', 'mp'), pairs)  69.4 us
    psum x1, blocking collectives, per_device(): whole_sum = lax.psum(jnp.stack(whole_sum), ('section', 'mp', 'dp')) * 0.5  45.9 us
    dot_general x16, matrix products, mm_tn(): lax.dot_general(left, right, (((0,), (0,)), ((), ())), preferred_element_...  34.8 us
    dot_general x16, matrix products, mm_nt(): lax.dot_general(left, right, (((1,), (1,)), ((), ())), preferred_element_...  28.6 us
    all_gather x2, blocking collectives, fetch(): return lax.all_gather(piece, 'dp', axis=0, tiled=True)  24.6 us
    dot_general x16, matrix products, mm(): return jnp.dot(left, right, preferred_element_type=f32)  24.3 us
    all_gather x2, blocking collectives, per_device(): lax.all_gather(pick(core == 0, first, second), 'dp', axis=0, tiled=True)  24.1 us
  transfers between devices with their start and end apart: 71, of which 24 were waited for; matrix products, arithmetic and copies ran while one was open for 27% of the time, Pallas kernels for 3%

profile of v1, /device:TPU:0, one launch (start us, length us, event | category | flops | bytes accessed | tf_op | source)
XLA Modules:
  0.0 647.9 jit_solution(15167480415815068048)
XLA Ops:
  8.7 4.1 collective-permute-start.2
  15.4 4.7 collective-permute-start
  28.2 15.0 %collective-permute-done.5 = bf16[192,576]{0,1:T(8,128)(2,1)S(1)} collective-permute-done((bf16[192,576]{0,1:T(8,128)(2,1)S(1)}, bf16[192,576]{0,1:T(8,128)(2,1)S(1)}, u32[]{:S(2)}, u32[]{:S(2)}) %collective-permute-start.5) | collective-permute-done | bytes 221216 | tf_op jit(solution)/shard_map/ppermute | solution.py:205
  43.5 6.0 collective-permute-start.1
  49.5 15.3 %all_gather.24 = bf16[768,576]{1,0:T(8,128)(2,1)S(1)} all-gather(bf16[192,576]{1,0:T(8,128)(2,1)S(1)} %copy.112), channel_id=1, replica_groups=mesh['section'=2,'mp'=4,'dp'=4] {'dp'}, dimensions={0}, use_global_device_ids=true | all-gather | bytes 1105920 | tf_op jit(solution)/shard_map/all_gather | solution.py:229
  73.7 7.7 %collective-permute-done.15 = bf16[192,768]{1,0:T(8,128)(2,1)S(1)} collective-permute-done((bf16[192,768]{1,0:T(8,128)(2,1)}, bf16[192,768]{1,0:T(8,128)(2,1)S(1)}, u32[]{:S(2)}, u32[]{:S(2)}) %collective-permute-start.15) | collective-permute-done | bytes 294944 | tf_op jit(solution)/shard_map/ppermute | solution.py:205
  84.4 5.8 attend.2
  90.4 9.3 %all_gather.25 = bf16[192,768]{1,0:T(8,128)(2,1)S(1)} all-gather(bf16[48,768]{1,0:T(8,128)(2,1)} %collective-permute-done.10), channel_id=1, replica_groups=mesh['section'=2,'mp'=4,'dp'=4] {'dp'}, dimensions={0}, use_global_device_ids=true | all-gather | bytes 368640 | tf_op jit(solution)/shard_map/all_gather | solution.py:229
  104.4 19.7 %all-gather.5.cloned.1.call-done = bf16[768,768]{1,0:T(8,128)(2,1)} async-done(((bf16[192,768]{1,0:T(8,128)(2,1)}), bf16[768,768]{1,0:T(8,128)(2,1)}) %all-gather.5.cloned.1.call-update) | async-done | bytes 1179664 | tf_op jit(solution)/shard_map/all_gather | solution.py:229
  137.2 16.8 %collective-permute-done.19 = bf16[512,768]{1,0:T(8,128)(2,1)S(1)} collective-permute-done((bf16[512,768]{1,0:T(8,128)(2,1)S(1)}, bf16[512,768]{1,0:T(8,128)(2,1)S(1)}, u32[]{:S(2)}, u32[]{:S(2)}) %collective-permute-start.19) | collective-permute-done | bytes 786464 | tf_op jit(solution)/shard_map/ppermute | solution.py:205
  156.7 3.2 broadcast_select_fusion.19
  166.8 5.9 attend.3
  179.1 5.1 collective-permute-start.26
  184.1 15.8 %collective-permute-done.26 = bf16[256,768]{1,0:T(8,128)(2,1)} collective-permute-done((bf16[256,768]{1,0:T(8,128)(2,1)}, bf16[256,768]{1,0:T(8,128)(2,1)}, u32[]{:S(2)}, u32[]{:S(2)}) %collective-permute-start.26) | collective-permute-done | bytes 393248 | tf_op jit(solution)/shard_map/ppermute | solution.py:205
  205.9 6.7 %collective-permute-done.27 = bf16[256,768]{1,0:T(8,128)(2,1)S(1)} collective-permute-done((bf16[256,768]{1,0:T(8,128)(2,1)S(1)}, bf16[256,768]{1,0:T(8,128)(2,1)S(1)}, u32[]{:S(2)}, u32[]{:S(2)}) %collective-permute-start.27) | collective-permute-done | bytes 393248 | tf_op jit(solution)/shard_map/ppermute | solution.py:205
  212.6 3.7 convert_reduce_fusion.4
  219.6 4.5 convert_reduce_fusion.5
  237.1 10.1 %collective-permute-done.28 = bf16[512,768]{1,0:T(8,128)(2,1)S(1)} collective-permute-done((bf16[512,768]{1,0:T(8,128)(2,1)S(1)}, bf16[512,768]{1,0:T(8,128)(2,1)S(1)}, u32[]{:S(2)}, u32[]{:S(2)}) %collective-permute-start.28) | collective-permute-done | bytes 786464 | tf_op jit(solution)/shard_map/ppermute | solution.py:205
  248.6 12.3 %collective-permute-done.23 = bf16[512,768]{1,0:T(8,128)(2,1)S(1)} collective-permute-done((bf16[512,768]{1,0:T(8,128)(2,1)S(1)}, bf16[512,768]{1,0:T(8,128)(2,1)S(1)}, u32[]{:S(2)}, u32[]{:S(2)}) %collective-permute-start.23) | collective-permute-done | bytes 786464 | tf_op jit(solution)/shard_map/ppermute | solution.py:205
  260.9 3.6 multiply_reduce_fusion.7
  269.3 7.0 %attend_back.2 = (bf16[1024,192]{1,0:T(8,128)(2,1)S(1)}, bf16[1024,192]{1,0:T(8,128)(2,1)S(1)}, bf16[1024,192]{1,0:T(8,128)(2,1)S(1)}) custom-call(bf16[1024,192]{1,0:T(8,128)(2,1)S(1)} %copy-done.1, bf16[1024,192]{1,0:T(8,128)(2,1)S(1)} %get-tuple-element.83.k_ref, bf16[1024,192]{1,0:T(8,128)(2,1)S(1)} %get-tuple-element.82.v_ref, ...), custom_call_target="tpu_custom_call" | custom-call | tf_op jit(solution)/shard_map/attend_back/pallas_call | solution.py:154
  278.9 3.9 convolution_convert_fusion.1
  290.8 3.1 add_convert_fusion.8
  299.8 13.0 %collective-permute-done.31 = bf16[512,768]{1,0:T(8,128)(2,1)} collective-permute-done((bf16[512,768]{1,0:T(8,128)(2,1)}, bf16[512,768]{1,0:T(8,128)(2,1)}, u32[]{:S(2)}, u32[]{:S(2)}) %collective-permute-start.31) | collective-permute-done | bytes 786464 | tf_op jit(solution)/shard_map/ppermute | solution.py:205
  315.2 2.9 fusion.2
  322.1 3.5 convert_reduce_fusion.7
  325.6 3.4 add_convert_fusion.7
  336.8 12.5 %collective-permute-done.32 = bf16[512,768]{1,0:T(8,128)(2,1)} collective-permute-done((bf16[512,768]{1,0:T(8,128)(2,1)}, bf16[512,768]{1,0:T(8,128)(2,1)}, u32[]{:S(2)}, u32[]{:S(2)}) %collective-permute-start.32) | collective-permute-done | bytes 786464 | tf_op jit(solution)/shard_map/ppermute | solution.py:205
  362.2 3.4 convolution_convert_fusion.7
  368.5 3.7 broadcast_select_fusion.7
  373.5 8.7 %collective-permute-done.24 = bf16[2,256,768]{2,1,0:T(8,128)(2,1)} collective-permute-done((bf16[2,256,768]{2,1,0:T(8,128)(2,1)}, bf16[2,256,768]{2,1,0:T(8,128)(2,1)}, u32[]{:S(2)}, u32[]{:S(2)}) %collective-permute-start.24) | collective-permute-done | bytes 786464 | tf_op jit(solution)/shard_map/ppermute | solution.py:205
  389.6 5.4 collective-permute-done.47
  398.7 3.6 convolution_convert_fusion.3
  405.6 4.1 broadcast_select_fusion.5
  413.1 7.0 %attend_back.3 = (bf16[1024,192]{1,0:T(8,128)(2,1)S(1)}, bf16[1024,192]{1,0:T(8,128)(2,1)S(1)}, bf16[1024,192]{1,0:T(8,128)(2,1)S(1)}) custom-call(bf16[1024,192]{1,0:T(8,128)(2,1)S(1)} %get-tuple-element.89.q_ref, bf16[1024,192]{1,0:T(8,128)(2,1)S(1)} %get-tuple-element.88.k_ref, bf16[1024,192]{1,0:T(8,128)(2,1)S(1)} %get-tuple-element.87.v_ref, ...), custom_call_target="tpu_custom_call" | custom-call | tf_op jit(solution)/shard_map/attend_back/pallas_call | solution.py:154
  430.7 7.0 %collective-permute-done.52 = bf16[192,768]{1,0:T(8,128)(2,1)S(1)} collective-permute-done((bf16[192,768]{1,0:T(8,128)(2,1)}, bf16[192,768]{1,0:T(8,128)(2,1)S(1)}, u32[]{:S(2)}, u32[]{:S(2)}) %collective-permute-start.52) | collective-permute-done | bytes 294944 | tf_op jit(solution)/shard_map/ppermute | solution.py:205
  454.9 10.1 %collective-permute-done.43 = f32[2,1152]{1,0:T(2,128)S(1)} collective-permute-done((f32[2,1152]{1,0:T(2,128)S(1)}, f32[2,1152]{1,0:T(2,128)S(1)}, u32[]{:S(2)}, u32[]{:S(2)}) %collective-permute-start.43) | collective-permute-done | bytes 9248 | tf_op jit(solution)/shard_map/ppermute | solution.py:205
  465.1 15.7 %psum.15 = f32[2,1152]{1,0:T(2,128)S(1)} all-reduce(f32[2,1152]{1,0:T(2,128)S(1)} %fusion.100), channel_id=1, replica_groups=mesh['section'=2,'mp'=4,'dp'=4] {'section','dp'}, use_global_device_ids=true, to_apply=%region_39.40 | all-reduce | flops 2304 | bytes 18432 | tf_op jit(solution)/shard_map/psum | solution.py:401
  483.4 4.3 collective-permute-start.38
  489.1 10.1 %all_gather.29 = bf16[192,768]{1,0:T(8,128)(2,1)} all-gather(bf16[48,768]{1,0:T(8,128)(2,1)S(1)} %add_select_fusion.3), channel_id=1, replica_groups=mesh['section'=2,'mp'=4,'dp'=4] {'dp'}, dimensions={0}, use_global_device_ids=true | all-gather | bytes 368640 | tf_op jit(solution)/shard_map/all_gather | solution.py:391
  504.1 9.2 %collective-permute-done.41 = bf16[192,576]{0,1:T(8,128)(2,1)S(1)} collective-permute-done((bf16[192,576]{0,1:T(8,128)(2,1)}, bf16[192,576]{0,1:T(8,128)(2,1)S(1)}, u32[]{:S(2)}, u32[]{:S(2)}) %collective-permute-start.41) | collective-permute-done | bytes 221216 | tf_op jit(solution)/shard_map/ppermute | solution.py:205
  523.0 3.0 fusion.81
  530.1 45.9 %psum.14 = f32[2,4608]{1,0:T(2,128)S(1)} all-reduce(f32[2,4608]{1,0:T(2,128)S(1)} %pad_maximum_fusion.2), channel_id=1, replica_groups=mesh['section'=2,'mp'=4,'dp'=4] {'section','mp','dp'}, use_global_device_ids=true, to_apply=%region_30.31 | all-reduce | flops 9216 | bytes 73728 | tf_op jit(solution)/shard_map/psum | solution.py:402
  583.0 3.5 collective-permute-start.37
  586.4 4.0 collective-permute-done.55
  596.9 7.0 %collective-permute-done.39 = bf16[192,576]{0,1:T(8,128)(2,1)S(1)} collective-permute-done((bf16[192,576]{0,1:T(8,128)(2,1)S(1)}, bf16[192,576]{0,1:T(8,128)(2,1)S(1)}, u32[]{:S(2)}, u32[]{:S(2)}) %collective-permute-start.39) | collective-permute-done | bytes 221216 | tf_op jit(solution)/shard_map/ppermute | solution.py:205
  604.2 13.9 %all_gather.28 = bf16[768,576]{1,0:T(8,128)(2,1)S(1)} all-gather(bf16[192,576]{1,0:T(8,128)(2,1)S(1)} %copy.140), channel_id=1, replica_groups=mesh['section'=2,'mp'=4,'dp'=4] {'dp'}, dimensions={0}, use_global_device_ids=true | all-gather | bytes 1105920 | tf_op jit(solution)/shard_map/all_gather | solution.py:391
  622.9 15.2 %all-gather.11.cloned.1.call-done = bf16[768,768]{1,0:T(8,128)(2,1)} async-done(((bf16[192,768]{1,0:T(8,128)(2,1)}), bf16[768,768]{1,0:T(8,128)(2,1)}) %all-gather.11.cloned.1.call-update) | async-done | bytes 1179664 | tf_op jit(solution)/shard_map/all_gather | solution.py:391
  (625 shorter events, 221.6 us)
Async XLA Ops:
  7.2 97.0 %all-gather.7.cloned.1.call-start = ((), (), s32[]{:S(2)}) async-start(), calls=%async_computation.9 | async-start | bytes 1474560 | tf_op jit(solution)/shard_map/all_gather | solution.py:229
  12.8 56.3 %collective-permute-start.4 = (bf16[768,576]{0,1:T(8,128)(2,1)}, bf16[768,576]{0,1:T(8,128)(2,1)}, u32[]{:S(2)}, u32[]{:S(2)}) collective-permute-start(bf16[768,576]{0,1:T(8,128)(2,1)} %bitcast.238), channel_id=1, source_target_pairs={{0,16},{4,20},{8,24},{12,28},{16,0},{20,4},{24,8},{28,12},{1,17},{... | collective-permute-start | bytes 2654216 | tf_op jit(solution)/shard_map/ppermute | solution.py:205
  14.0 29.2 %collective-permute-start.5 = (bf16[192,576]{0,1:T(8,128)(2,1)S(1)}, bf16[192,576]{0,1:T(8,128)(2,1)S(1)}, u32[]{:S(2)}, u32[]{:S(2)}) collective-permute-start(bf16[192,576]{0,1:T(8,128)(2,1)S(1)} %constant_dynamic-slice_fusion.6), channel_id=1, source_target_pairs={{0,8},{4,12},{8,0},{12,4},{16,24},{20,28},{24,16},{28,20},{1,9},{5... | collective-permute-start | bytes 663560 | tf_op jit(solution)/shard_map/ppermute | solution.py:205
  15.4 28.0 %collective-permute-start = (bf16[256,768]{1,0:T(8,128)(2,1)S(1)}, bf16[256,768]{1,0:T(8,128)(2,1)S(1)}, u32[]{:S(2)}, u32[]{:S(2)}) collective-permute-start(bf16[256,768]{1,0:T(8,128)(2,1)S(1)} %select_bitcast_fusion.2), channel_id=1, source_target_pairs={{0,8},{4,12},{24,16},{28,20},{1,9},{5,13},{25,17},{29,21},{2,10},{... | collective-permute-start | bytes 1179656 | tf_op jit(solution)/shard_map/ppermute | solution.py:205
  21.7 68.7 %collective-permute-start.10 = (bf16[48,768]{1,0:T(8,128)(2,1)}, bf16[48,768]{1,0:T(8,128)(2,1)}, u32[]{:S(2)}, u32[]{:S(2)}) collective-permute-start(bf16[48,768]{1,0:T(8,128)(2,1)} %dynamic-slice_bitcast_fusion.4), channel_id=1, source_target_pairs={{0,8},{4,12},{8,0},{12,4},{16,24},{20,28},{24,16},{28,20},{1,9},{5... | collective-permute-start | bytes 221192 | tf_op jit(solution)/shard_map/ppermute | solution.py:205
  24.6 41.7 %collective-permute-start.17 = (bf16[192,768]{1,0:T(8,128)(2,1)S(1)}, bf16[192,768]{1,0:T(8,128)(2,1)S(1)}, u32[]{:S(2)}, u32[]{:S(2)}) collective-permute-start(bf16[192,768]{1,0:T(8,128)(2,1)S(1)} %dynamic-slice_bitcast_fusion), channel_id=1, source_target_pairs={{0,8},{4,12},{8,0},{12,4},{16,24},{20,28},{24,16},{28,20},{1,9},{5... | collective-permute-start | bytes 884744 | tf_op jit(solution)/shard_map/ppermute | solution.py:205
  43.5 23.8 %collective-permute-start.1 = (bf16[256,768]{1,0:T(8,128)(2,1)S(1)}, bf16[256,768]{1,0:T(8,128)(2,1)S(1)}, u32[]{:S(2)}, u32[]{:S(2)}) collective-permute-start(bf16[256,768]{1,0:T(8,128)(2,1)S(1)} %bitcast_select_fusion.4), channel_id=1, source_target_pairs={{0,4},{4,0},{8,12},{12,8},{16,20},{20,16},{24,28},{28,24},{1,5},{5... | collective-permute-start | bytes 1179656 | tf_op jit(solution)/shard_map/ppermute | solution.py:205
  66.4 15.1 %collective-permute-start.15 = (bf16[192,768]{1,0:T(8,128)(2,1)}, bf16[192,768]{1,0:T(8,128)(2,1)S(1)}, u32[]{:S(2)}, u32[]{:S(2)}) collective-permute-start(bf16[192,768]{1,0:T(8,128)(2,1)} %dynamic-slice_bitcast_fusion.1), channel_id=1, source_target_pairs={{0,8},{4,12},{8,0},{12,4},{16,24},{20,28},{24,16},{28,20},{1,9},{5... | collective-permute-start | bytes 884744 | tf_op jit(solution)/shard_map/ppermute | solution.py:205
  67.2 56.8 %all-gather.5.cloned.1.call-start = ((), (), s32[]{:S(2)}) async-start(), calls=%async_computation.8 | async-start | bytes 1474560 | tf_op jit(solution)/shard_map/all_gather | solution.py:229
  82.2 306.2 %reduce-scatter.15.cloned.1.call-start = ((), (), s32[]{:S(2)}) async-start(), calls=%async_computation.11 | async-start | bytes 368640 | tf_op jit(solution)/shard_map/reduce_scatter | solution.py:382
  103.7 20.4 %collective-permute-start.12 = (bf16[512,768]{1,0:T(8,128)(2,1)}, bf16[512,768]{1,0:T(8,128)(2,1)}, u32[]{:S(2)}, u32[]{:S(2)}) collective-permute-start(bf16[512,768]{1,0:T(8,128)(2,1)} %add_convert_fusion.17), channel_id=1, source_target_pairs={{0,4},{4,0},{8,12},{12,8},{16,20},{20,16},{24,28},{28,24},{1,5},{5... | collective-permute-start | bytes 2359304 | tf_op jit(solution)/shard_map/ppermute | solution.py:205
  103.7 29.0 %collective-permute-start.14 = (bf16[768,768]{1,0:T(8,128)(2,1)}, bf16[768,768]{1,0:T(8,128)(2,1)}, u32[]{:S(2)}, u32[]{:S(2)}) collective-permute-start(bf16[768,768]{1,0:T(8,128)(2,1)} %bitcast.14), channel_id=1, source_target_pairs={{0,16},{4,20},{8,24},{12,28},{16,0},{20,4},{24,8},{28,12},{1,17},{... | collective-permute-start | bytes 3538952 | tf_op jit(solution)/shard_map/ppermute | solution.py:205
  103.9 22.9 %collective-permute-start.13 = (bf16[768,768]{1,0:T(8,128)(2,1)}, bf16[768,768]{1,0:T(8,128)(2,1)}, u32[]{:S(2)}, u32[]{:S(2)}) collective-permute-start(bf16[768,768]{1,0:T(8,128)(2,1)} %bitcast.13), channel_id=1, source_target_pairs={{0,16},{4,20},{8,24},{12,28},{16,0},{20,4},{24,8},{28,12},{1,17},{... | collective-permute-start | bytes 3538952 | tf_op jit(solution)/shard_map/ppermute | solution.py:205
  104.2 26.3 %collective-permute-start.18 = (bf16[768,768]{1,0:T(8,128)(2,1)}, bf16[768,768]{1,0:T(8,128)(2,1)}, u32[]{:S(2)}, u32[]{:S(2)}) collective-permute-start(bf16[768,768]{1,0:T(8,128)(2,1)} %all-gather.7.cloned.1.call-done), channel_id=1, source_target_pairs={{0,16},{4,20},{8,24},{12,28},{16,0},{20,4},{24,8},{28,12},{1,17},{... | collective-permute-start | bytes 3538952 | tf_op jit(solution)/shard_map/ppermute | solution.py:205
  135.1 18.9 %collective-permute-start.19 = (bf16[512,768]{1,0:T(8,128)(2,1)S(1)}, bf16[512,768]{1,0:T(8,128)(2,1)S(1)}, u32[]{:S(2)}, u32[]{:S(2)}) collective-permute-start(bf16[512,768]{1,0:T(8,128)(2,1)S(1)} %add_convert_fusion.15), channel_id=1, source_target_pairs={{0,4},{4,0},{8,12},{12,8},{16,20},{20,16},{24,28},{28,24},{1,5},{5... | collective-permute-start | bytes 2359304 | tf_op jit(solution)/shard_map/ppermute | solution.py:205
  176.8 24.5 %collective-permute-start.22 = (bf16[512,768]{1,0:T(8,128)(2,1)}, bf16[512,768]{1,0:T(8,128)(2,1)}, u32[]{:S(2)}, u32[]{:S(2)}) collective-permute-start(bf16[512,768]{1,0:T(8,128)(2,1)} %add_convert_fusion.13), channel_id=1, source_target_pairs={{0,4},{4,0},{8,12},{12,8},{16,20},{20,16},{24,28},{28,24},{1,5},{5... | collective-permute-start | bytes 2359304 | tf_op jit(solution)/shard_map/ppermute | solution.py:205
  179.1 20.9 %collective-permute-start.26 = (bf16[256,768]{1,0:T(8,128)(2,1)}, bf16[256,768]{1,0:T(8,128)(2,1)}, u32[]{:S(2)}, u32[]{:S(2)}) collective-permute-start(bf16[256,768]{1,0:T(8,128)(2,1)} %select_bitcast_fusion.1), channel_id=1, source_target_pairs={{0,8},{4,12},{24,16},{28,20},{1,9},{5,13},{25,17},{29,21},{2,10},{... | collective-permute-start | bytes 1179656 | tf_op jit(solution)/shard_map/ppermute | solution.py:205
  226.6 20.5 %collective-permute-start.28 = (bf16[512,768]{1,0:T(8,128)(2,1)S(1)}, bf16[512,768]{1,0:T(8,128)(2,1)S(1)}, u32[]{:S(2)}, u32[]{:S(2)}) collective-permute-start(bf16[512,768]{1,0:T(8,128)(2,1)S(1)} %add_convert_fusion.9), channel_id=1, source_target_pairs={{0,4},{4,0},{8,12},{12,8},{16,20},{20,16},{24,28},{28,24},{1,5},{5... | collective-permute-start | bytes 2359304 | tf_op jit(solution)/shard_map/ppermute | solution.py:205
  231.9 29.0 %collective-permute-start.23 = (bf16[512,768]{1,0:T(8,128)(2,1)S(1)}, bf16[512,768]{1,0:T(8,128)(2,1)S(1)}, u32[]{:S(2)}, u32[]{:S(2)}) collective-permute-start(bf16[512,768]{1,0:T(8,128)(2,1)S(1)} %add_convert_fusion.11), channel_id=1, source_target_pairs={{0,4},{4,0},{8,12},{12,8},{16,20},{20,16},{24,28},{28,24},{1,5},{5... | collective-permute-start | bytes 2359304 | tf_op jit(solution)/shard_map/ppermute | solution.py:205
  237.1 59.8 %collective-permute-start.51 = (bf16[768,768]{1,0:T(8,128)(2,1)}, bf16[768,768]{1,0:T(8,128)(2,1)}, u32[]{:S(2)}, u32[]{:S(2)}) collective-permute-start(bf16[768,768]{1,0:T(8,128)(2,1)} %get-tuple-element.154), channel_id=1, source_target_pairs={{0,16},{4,20},{8,24},{12,28},{16,0},{20,4},{24,8},{28,12},{1,17},{... | collective-permute-start | bytes 3538952 | tf_op jit(solution)/shard_map/ppermute | solution.py:205
  268.6 16.4 %collective-permute-start.46 = (bf16[192,768]{1,0:T(8,128)(2,1)}, bf16[192,768]{1,0:T(8,128)(2,1)}, u32[]{:S(2)}, u32[]{:S(2)}) collective-permute-start(bf16[192,768]{1,0:T(8,128)(2,1)} %get-tuple-element.150), channel_id=1, source_target_pairs={{0,16},{4,20},{8,24},{12,28},{16,0},{20,4},{24,8},{28,12},{1,17},{... | collective-permute-start | bytes 884744 | tf_op jit(solution)/shard_map/ppermute | solution.py:205
  286.8 138.3 %reduce-scatter.19.cloned.1.call-start = ((), (), s32[]{:S(2)}) async-start(), calls=%async_computation.13 | async-start | bytes 1474560 | tf_op jit(solution)/shard_map/reduce_scatter | solution.py:382
  293.9 18.9 %collective-permute-start.31 = (bf16[512,768]{1,0:T(8,128)(2,1)}, bf16[512,768]{1,0:T(8,128)(2,1)}, u32[]{:S(2)}, u32[]{:S(2)}) collective-permute-start(bf16[512,768]{1,0:T(8,128)(2,1)} %add_convert_fusion.8), channel_id=1, source_target_pairs={{0,4},{4,0},{8,12},{12,8},{16,20},{20,16},{24,28},{28,24},{1,5},{5... | collective-permute-start | bytes 2359304 | tf_op jit(solution)/shard_map/ppermute | solution.py:205
  296.9 32.3 %collective-permute-start.56 = (bf16[768,768]{1,0:T(8,128)(2,1)}, bf16[768,768]{1,0:T(8,128)(2,1)}, u32[]{:S(2)}, u32[]{:S(2)}) collective-permute-start(bf16[768,768]{1,0:T(8,128)(2,1)} %get-tuple-element.158), channel_id=1, source_target_pairs={{0,16},{4,20},{8,24},{12,28},{16,0},{20,4},{24,8},{28,12},{1,17},{... | collective-permute-start | bytes 3538952 | tf_op jit(solution)/shard_map/ppermute | solution.py:205
  299.7 126.8 %reduce-scatter.23.cloned.1.call-start = ((), (), s32[]{:S(2)}) async-start(), calls=%async_computation.16 | async-start | bytes 1474560 | tf_op jit(solution)/shard_map/reduce_scatter | solution.py:382
  328.9 20.4 %collective-permute-start.32 = (bf16[512,768]{1,0:T(8,128)(2,1)}, bf16[512,768]{1,0:T(8,128)(2,1)}, u32[]{:S(2)}, u32[]{:S(2)}) collective-permute-start(bf16[512,768]{1,0:T(8,128)(2,1)} %add_convert_fusion.7), channel_id=1, source_target_pairs={{0,4},{4,0},{8,12},{12,8},{16,20},{20,16},{24,28},{28,24},{1,5},{5... | collective-permute-start | bytes 2359304 | tf_op jit(solution)/shard_map/ppermute | solution.py:205
  332.0 149.4 %reduce-scatter.13.cloned.1.call-start = ((), (), s32[]{:S(2)}) async-start(), calls=%async_computation.10 | async-start | bytes 368640 | tf_op jit(solution)/shard_map/reduce_scatter | solution.py:382
  336.5 29.0 %collective-permute-start.40 = (bf16[768,576]{0,1:T(8,128)(2,1)}, bf16[768,576]{0,1:T(8,128)(2,1)}, u32[]{:S(2)}, u32[]{:S(2)}) collective-permute-start(bf16[768,576]{0,1:T(8,128)(2,1)} %get-tuple-element.138), channel_id=1, source_target_pairs={{0,16},{4,20},{8,24},{12,28},{16,0},{20,4},{24,8},{28,12},{1,17},{... | collective-permute-start | bytes 2654216 | tf_op jit(solution)/shard_map/ppermute | solution.py:205
  359.0 23.2 %collective-permute-start.24 = (bf16[2,256,768]{2,1,0:T(8,128)(2,1)}, bf16[2,256,768]{2,1,0:T(8,128)(2,1)}, u32[]{:S(2)}, u32[]{:S(2)}) collective-permute-start(bf16[2,256,768]{2,1,0:T(8,128)(2,1)} %fusion.77), channel_id=1, source_target_pairs={{8,0},{12,4},{16,24},{20,28},{9,1},{13,5},{17,25},{21,29},{10,2},{... | collective-permute-start | bytes 2359304 | tf_op jit(solution)/shard_map/ppermute | solution.py:205
  362.1 137.1 %reduce-scatter.27.cloned.1.call-start = ((), (), s32[]{:S(2)}) async-start(), calls=%async_computation.19 | async-start | bytes 1228800
  368.5 160.1 %reduce-scatter.17.cloned.1.call-start = ((), (), s32[]{:S(2)}) async-start(), calls=%async_computation.12 | async-start | bytes 1474560 | tf_op jit(solution)/shard_map/reduce_scatter | solution.py:382
  372.2 30.0 %collective-permute-start.49 = (bf16[768,768]{1,0:T(8,128)(2,1)}, bf16[768,768]{1,0:T(8,128)(2,1)}, u32[]{:S(2)}, u32[]{:S(2)}) collective-permute-start(bf16[768,768]{1,0:T(8,128)(2,1)} %get-tuple-element.156), channel_id=1, source_target_pairs={{0,16},{4,20},{8,24},{12,28},{16,0},{20,4},{24,8},{28,12},{1,17},{... | collective-permute-start | bytes 3538952 | tf_op jit(solution)/shard_map/ppermute | solution.py:205
  386.0 37.8 %collective-permute-start.25 = (bf16[2,256,768]{2,1,0:T(8,128)(2,1)}, bf16[2,256,768]{2,1,0:T(8,128)(2,1)}, u32[]{:S(2)}, u32[]{:S(2)}) collective-permute-start(bf16[2,256,768]{2,1,0:T(8,128)(2,1)} %fusion.74), channel_id=1, source_target_pairs={{0,16},{4,20},{24,8},{28,12},{1,17},{5,21},{25,9},{29,13},{2,18},{... | collective-permute-start | bytes 2359304 | tf_op jit(solution)/shard_map/ppermute | solution.py:205
  396.6 86.8 %collective-permute-start.48 = (bf16[48,768]{1,0:T(8,128)(2,1)}, bf16[48,768]{1,0:T(8,128)(2,1)}, u32[]{:S(2)}, u32[]{:S(2)}) collective-permute-start(bf16[48,768]{1,0:T(8,128)(2,1)} %add.499), channel_id=1, source_target_pairs={{0,16},{4,20},{8,24},{12,28},{1,17},{5,21},{9,25},{13,29},{2,18},{... | collective-permute-start | bytes 221192 | tf_op jit(solution)/shard_map/ppermute | solution.py:205
  405.1 173.8 %reduce-scatter.21.cloned.1.call-start = ((), (), s32[]{:S(2)}) async-start(), calls=%async_computation.15 | async-start | bytes 1474560 | tf_op jit(solution)/shard_map/reduce_scatter | solution.py:382
  409.6 18.2 %collective-permute-start.54 = (bf16[768,768]{1,0:T(8,128)(2,1)}, bf16[768,768]{1,0:T(8,128)(2,1)}, u32[]{:S(2)}, u32[]{:S(2)}) collective-permute-start(bf16[768,768]{1,0:T(8,128)(2,1)} %get-tuple-element.160), channel_id=1, source_target_pairs={{0,16},{4,20},{8,24},{12,28},{16,0},{20,4},{24,8},{28,12},{1,17},{... | collective-permute-start | bytes 3538952 | tf_op jit(solution)/shard_map/ppermute | solution.py:205
  423.7 20.2 %collective-permute-start.34 = (bf16[512,576]{0,1:T(8,128)(2,1)}, bf16[512,576]{0,1:T(8,128)(2,1)}, u32[]{:S(2)}, u32[]{:S(2)}) collective-permute-start(bf16[512,576]{0,1:T(8,128)(2,1)} %copy.139), channel_id=1, source_target_pairs={{0,16},{4,20},{8,24},{12,28},{16,0},{20,4},{24,8},{28,12},{1,17},{... | collective-permute-start | bytes 1769480 | tf_op jit(solution)/shard_map/ppermute | solution.py:205
  430.7 162.5 %reduce-scatter.25.cloned.1.call-start = ((), (), s32[]{:S(2)}) async-start(), calls=%async_computation.18 | async-start | bytes 1228800
  438.5 139.4 %collective-permute-start.53 = (bf16[192,768]{1,0:T(8,128)(2,1)}, bf16[192,768]{1,0:T(8,128)(2,1)}, u32[]{:S(2)}, u32[]{:S(2)}) collective-permute-start(bf16[192,768]{1,0:T(8,128)(2,1)} %add.503), channel_id=1, source_target_pairs={{0,16},{4,20},{8,24},{12,28},{1,17},{5,21},{9,25},{13,29},{2,18},{... | collective-permute-start | bytes 884744 | tf_op jit(solution)/shard_map/ppermute | solution.py:205
  441.7 144.7 %collective-permute-start.58 = (bf16[192,768]{1,0:T(8,128)(2,1)}, bf16[192,768]{1,0:T(8,128)(2,1)}, u32[]{:S(2)}, u32[]{:S(2)}) collective-permute-start(bf16[192,768]{1,0:T(8,128)(2,1)} %add.507), channel_id=1, source_target_pairs={{0,16},{4,20},{8,24},{12,28},{1,17},{5,21},{9,25},{13,29},{2,18},{... | collective-permute-start | bytes 884744 | tf_op jit(solution)/shard_map/ppermute | solution.py:205
  448.2 68.9 %collective-permute-start.35 = (bf16[512,768]{1,0:T(8,128)(2,1)S(1)}, bf16[512,768]{1,0:T(8,128)(2,1)S(1)}, u32[]{:S(2)}, u32[]{:S(2)}) collective-permute-start(bf16[512,768]{1,0:T(8,128)(2,1)S(1)} %add_convert_fusion.6), channel_id=1, source_target_pairs={{0,4},{4,0},{8,12},{12,8},{16,20},{20,16},{24,28},{28,24},{1,5},{5... | collective-permute-start | bytes 2359304 | tf_op jit(solution)/shard_map/ppermute | solution.py:205
  448.5 16.5 %collective-permute-start.43 = (f32[2,1152]{1,0:T(2,128)S(1)}, f32[2,1152]{1,0:T(2,128)S(1)}, u32[]{:S(2)}, u32[]{:S(2)}) collective-permute-start(f32[2,1152]{1,0:T(2,128)S(1)} %fusion.101), channel_id=1, source_target_pairs={{0,8},{4,12},{8,0},{12,4},{16,24},{20,28},{24,16},{28,20},{1,9},{5... | collective-permute-start | bytes 27656 | tf_op jit(solution)/shard_map/ppermute | solution.py:205
  483.4 34.7 %collective-permute-start.38 = (bf16[768,576]{0,1:T(8,128)(2,1)}, bf16[768,576]{0,1:T(8,128)(2,1)}, u32[]{:S(2)}, u32[]{:S(2)}) collective-permute-start(bf16[768,576]{0,1:T(8,128)(2,1)} %get-tuple-element.140), channel_id=1, source_target_pairs={{0,16},{4,20},{8,24},{12,28},{16,0},{20,4},{24,8},{28,12},{1,17},{... | collective-permute-start | bytes 2654216 | tf_op jit(solution)/shard_map/ppermute | solution.py:205
  515.1 81.8 %collective-permute-start.42 = (bf16[192,576]{0,1:T(8,128)(2,1)}, bf16[192,576]{0,1:T(8,128)(2,1)}, u32[]{:S(2)}, u32[]{:S(2)}) collective-permute-start(bf16[192,576]{0,1:T(8,128)(2,1)} %add.494), channel_id=1, source_target_pairs={{0,16},{4,20},{8,24},{12,28},{1,17},{5,21},{9,25},{13,29},{2,18},{... | collective-permute-start | bytes 663560 | tf_op jit(solution)/shard_map/ppermute | solution.py:205
  523.0 97.1 %all-gather.9.cloned.1.call-start = ((), (), s32[]{:S(2)}) async-start(), calls=%async_computation.14 | async-start | bytes 1474560 | tf_op jit(solution)/shard_map/all_gather | solution.py:391
  527.1 53.0 %collective-permute-start.36 = (bf16[2,256,768]{2,1,0:T(8,128)(2,1)S(1)}, bf16[2,256,768]{2,1,0:T(8,128)(2,1)S(1)}, u32[]{:S(2)}, u32[]{:S(2)}) collective-permute-start(bf16[2,256,768]{2,1,0:T(8,128)(2,1)S(1)} %fusion.76), channel_id=1, source_target_pairs={{8,0},{12,4},{16,24},{20,28},{9,1},{13,5},{17,25},{21,29},{10,2},{... | collective-permute-start | bytes 2359304 | tf_op jit(solution)/shard_map/ppermute | solution.py:205
  528.6 49.3 %collective-permute-start.50 = (bf16[192,768]{1,0:T(8,128)(2,1)}, bf16[192,768]{1,0:T(8,128)(2,1)S(1)}, u32[]{:S(2)}, u32[]{:S(2)}) collective-permute-start(bf16[192,768]{1,0:T(8,128)(2,1)} %reduce-scatter.17.cloned.1.call-done), channel_id=1, source_target_pairs={{16,8},{20,12},{24,0},{28,4},{17,9},{21,13},{25,1},{29,5},{18,10},... | collective-permute-start | bytes 884744 | tf_op jit(solution)/shard_map/ppermute | solution.py:205
  578.8 59.3 %all-gather.11.cloned.1.call-start = ((), (), s32[]{:S(2)}) async-start(), calls=%async_computation.17 | async-start | bytes 1474560 | tf_op jit(solution)/shard_map/all_gather | solution.py:391
  (166 other events, 1164.8 us)
Sparse Core Ops, SparseCore 0:
  67.4 26.4 all-gather.6
  96.3 27.7 all-gather.4
  286.9 21.5 reduce-scatter.14
  311.3 28.5 reduce-scatter.18
  342.6 28.5 reduce-scatter.22
  373.8 24.1 reduce-scatter.12
  401.0 27.2 reduce-scatter.26
  431.8 28.5 reduce-scatter.16
  463.8 29.0 reduce-scatter.20
  523.1 26.1 reduce-scatter.24
  578.9 28.8 all-gather.8
  610.0 28.0 all-gather.10

commit v2 on v1

--- a/solution.py
+++ b/solution.py
@@ -68,47 +68,6 @@
     key = lax.broadcasted_iota(jnp.int32, (count, rows.stop - rows.start), 0)
     query = lax.broadcasted_iota(jnp.int32, (count, rows.stop - rows.start), 1) + rows.start
     return same & (key <= query)
-
-
-def attend_kernel(q_ref, k_ref, v_ref, seg_col, seg_row, out_ref, logsum_ref):
-    length, width = q_ref.shape
-    for start in range(0, length, block):
-        rows = slice(start, start + block)
-        count = start + block
-        mask = block_mask(seg_col, seg_row, rows, count)
-        mixed = []
-        for head, (lane, lanes, upper) in enumerate(head_lanes(width // HEAD)):
-            cols = slice(lane, lane + lanes)
-            queries = own_lanes(q_ref[rows, cols], lanes, upper) * bf16(HEAD ** (-0.5))
-            scores = mm_nt(k_ref[0:count, cols], queries)
-            scores = jnp.where(mask, scores, masked_score)
-            top = jnp.max(scores, axis=0, keepdims=True)
-            weights = jnp.exp(scores - top)
-            total = jnp.sum(weights, axis=0, keepdims=True)
-            result = mm_tn(v_ref[0:count, cols], weights.astype(bf16)) / total
-            logsum_ref[head : head + 1, rows] = top + jnp.log(total)
-            mixed.append((lanes, result))
-        for pair in range(0, len(mixed), 2):
-            lane = pair * HEAD
-            lanes, result = mixed[pair]
-            if lanes > HEAD:
-                result = jnp.concatenate([result[:HEAD], mixed[pair + 1][1][HEAD:]], axis=0)
-            out_ref[rows, lane : lane + lanes] = result.T.astype(bf16)
-
-
-def attend(q, k, v, seg_col, seg_row):
-    length, width = q.shape
-    return pl.pallas_call(
-        attend_kernel,
-        out_shape=(
-            jax.ShapeDtypeStruct((length, width), bf16),
-            jax.ShapeDtypeStruct((width // HEAD, length), f32),
-        ),
-        in_specs=[pl.BlockSpec(memory_space=pltpu.VMEM)] * 5,
-        out_specs=[pl.BlockSpec(memory_space=pltpu.VMEM)] * 2,
-        compiler_params=pltpu.CompilerParams(vmem_limit_bytes=40 * 2**20),
-        name="attend",
-    )(q, k, v, seg_col, seg_row)
 
 
 def attend_back_kernel(
@@ -162,6 +121,204 @@
     )(q, k, v, grad, logsum, seg_col, seg_row)
 
 
+MESH = pl.DeviceIdType.MESH
+
+
+def send(src, dst, sems, index, device):
+    return pltpu.make_async_remote_copy(
+        src_ref=src,
+        dst_ref=dst,
+        send_sem=sems.at[0, index],
+        recv_sem=sems.at[1, index],
+        device_id=device,
+        device_id_type=MESH,
+    )
+
+
+def attend_block(qkv_ref, mask, rows, count, logsum_ref):
+    heads = qkv_ref.shape[2] // HEAD
+    mixed = []
+    for head, (lane, lanes, upper) in enumerate(head_lanes(heads)):
+        cols = slice(lane, lane + lanes)
+        queries = own_lanes(qkv_ref[0, rows, cols], lanes, upper) * bf16(HEAD ** (-0.5))
+        scores = mm_nt(qkv_ref[1, 0:count, cols], queries)
+        scores = jnp.where(mask, scores, masked_score)
+        top = jnp.max(scores, axis=0, keepdims=True)
+        weights = jnp.exp(scores - top)
+        total = jnp.sum(weights, axis=0, keepdims=True)
+        result = mm_tn(qkv_ref[2, 0:count, cols], weights.astype(bf16)) / total
+        logsum_ref[head : head + 1, rows] = top + jnp.log(total)
+        mixed.append((lanes, result))
+    found = []
+    for pair in range(0, heads, 2):
+        lanes, result = mixed[pair]
+        if lanes > HEAD:
+            result = jnp.concatenate([result[:HEAD], mixed[pair + 1][1][HEAD:]], axis=0)
+        found.append((pair * HEAD, lanes, result.T.astype(bf16)))
+    return found
+
+
+def forward_kernel(
+    state_ref,
+    w_in,
+    w_out,
+    w_up,
+    w_down,
+    b_in,
+    b_up,
+    vec_ref,
+    seg_col,
+    seg_row,
+    out_ref,
+    normed_ref,
+    qkv_ref,
+    logsum_ref,
+    att_ref,
+    middle_ref,
+    upper_ref,
+    hidden_ref,
+    slope_ref,
+    qkv_out,
+    att_out,
+    low,
+    got,
+    qkv_sems,
+    att_sems,
+    pair_sems,
+):
+    core = lax.axis_index("section")
+    z = lax.axis_index("mp")
+    dp = lax.axis_index("dp")
+    sibling = (1 - core, z, dp)
+    partner = (core, z + 1 - 2 * lax.rem(z, 2), dp)
+    barrier = pltpu.get_barrier_semaphore()
+    for device in (sibling, partner):
+        pl.semaphore_signal(barrier, inc=1, device_id=device, device_id_type=MESH)
+    pl.semaphore_wait(barrier, 2)
+
+    half = state_ref.shape[0]
+    blocks = half // block
+    first = pl.multiple_of(core * half, half)
+
+    copies = []
+    for j in range(blocks):
+        rows = slice(j * block, (j + 1) * block)
+        normal, _ = normalize(state_ref[rows, :].astype(f32))
+        normed = (normal * vec_ref[0:1, :] + vec_ref[2:3, :]).astype(bf16)
+        normed_ref[rows, :] = normed
+        for part in range(3):
+            qkv_out[j, part] = (mm(normed, w_in[1 - core, part]) + b_in[1 - core, part]).astype(bf16)
+        there = pl.ds(pl.multiple_of(first + j * block, block), block)
+        copy = send(qkv_out.at[j], qkv_ref.at[:, there, :], qkv_sems, j, sibling)
+        copy.start()
+        copies.append(copy)
+        for part in range(3):
+            qkv_ref[part, there, :] = (mm(normed, w_in[core, part]) + b_in[core, part]).astype(bf16)
+    for copy in copies:
+        copy.wait()
+
+    def send_low(index, rows, value):
+        low[index, rows, :] = value.astype(bf16)
+        copy = send(low.at[index, rows], got.at[index, rows], pair_sems, index * blocks + rows.start // block, partner)
+        copy.start()
+
+    def received(index, rows):
+        copy = send(low.at[index, rows], got.at[index, rows], pair_sems, index * blocks + rows.start // block, partner)
+        copy.wait()
+        return low[index, rows, :].astype(f32) + got[index, rows, :].astype(f32)
+
+    for i in range(2 * blocks):
+        owner, j = i // blocks, i % blocks
+        rows = slice(i * block, (i + 1) * block)
+        own = slice(j * block, (j + 1) * block)
+        count = (i + 1) * block
+        mask = block_mask(seg_col, seg_row, rows, count)
+        found = attend_block(qkv_ref, mask, rows, count, logsum_ref)
+        copy = send(att_out.at[j], att_ref.at[core, own], att_sems, j, sibling)
+
+        @pl.when(core == owner)
+        def _():
+            for lane, lanes, result in found:
+                att_ref[core, own, lane : lane + lanes] = result
+            copy.wait_recv()
+            send_low(0, own, mm(att_ref[0, own, :], w_out[0]) + mm(att_ref[1, own, :], w_out[1]))
+
+        @pl.when(core != owner)
+        def _():
+            for lane, lanes, result in found:
+                att_out[j, :, lane : lane + lanes] = result
+            copy.start()
+
+    for j in range(blocks):
+        own = slice(j * block, (j + 1) * block)
+        send(att_out.at[j], att_ref.at[core, own], att_sems, j, sibling).wait_send()
+
+    for j in range(blocks):
+        rows = slice(j * block, (j + 1) * block)
+        middle = state_ref[rows, :].astype(f32) + branch_scale * (received(0, rows) + vec_ref[4:5, :])
+        middle_ref[rows, :] = middle
+        normal, _ = normalize(middle)
+        upper = (normal * vec_ref[1:2, :] + vec_ref[3:4, :]).astype(bf16)
+        upper_ref[rows, :] = upper
+        total = None
+        for k in range(2):
+            pre = mm(upper, w_up[k]) + b_up[k]
+            square = pre * pre
+            curve = jnp.tanh(root * pre * (1.0 + cube * square))
+            rise = 0.5 * (1.0 + curve)
+            hidden = (pre * rise).astype(bf16)
+            hidden_ref[k, rows, :] = hidden
+            slope = rise + pre * (rise * (1.0 - curve)) * (root * (1.0 + 3.0 * cube * square))
+            slope_ref[k, rows, :] = slope.astype(bf16)
+            term = mm(hidden, w_down[k])
+            total = term if total is None else total + term
+        send_low(1, rows, total)
+
+    for j in range(blocks):
+        rows = slice(j * block, (j + 1) * block)
+        result = middle_ref[rows, :] + branch_scale * (received(1, rows) + vec_ref[5:6, :])
+        out_ref[rows, :] = result.astype(bf16)
+
+
+def forward_layer(state, w_in, w_out, w_up, w_down, b_in, b_up, vec, seg_col, seg_row):
+    half, width = state.shape
+    length = seg_col.shape[0]
+    local = w_in.shape[3]
+    units = w_up.shape[2]
+    blocks = half // block
+    vmem = pl.BlockSpec(memory_space=pltpu.VMEM)
+    shape = jax.ShapeDtypeStruct
+    return pl.pallas_call(
+        forward_kernel,
+        out_shape=(
+            shape((half, width), bf16),
+            shape((half, width), bf16),
+            shape((3, length, local), bf16),
+            shape((local // HEAD, length), f32),
+            shape((2, half, local), bf16),
+            shape((half, width), f32),
+            shape((half, width), bf16),
+            shape((2, half, units), bf16),
+            shape((2, half, units), bf16),
+        ),
+        in_specs=[vmem] * 10,
+        out_specs=[vmem] * 9,
+        scratch_shapes=[
+            pltpu.VMEM((blocks, 3, block, local), bf16),
+            pltpu.VMEM((blocks, block, local), bf16),
+            pltpu.VMEM((2, half, width), bf16),
+            pltpu.VMEM((2, half, width), bf16),
+            pltpu.SemaphoreType.DMA((2, blocks)),
+            pltpu.SemaphoreType.DMA((2, blocks)),
+            pltpu.SemaphoreType.DMA((2, 2 * blocks)),
+        ],
+        compiler_params=pltpu.CompilerParams(
+            vmem_limit_bytes=50 * 2**20, collective_id=1, has_side_effects=True
+        ),
+        name="forward_layer",
+    )(state, w_in, w_out, w_up, w_down, b_in, b_up, vec, seg_col, seg_row)
+
+
 def segment_ids(lengths, length):
     ends = jnp.cumsum(lengths)
     positions = jnp.arange(length, dtype=jnp.int32)
@@ -222,21 +379,26 @@
             jnp.concatenate([there, here], axis=0),
         )
 
-    def fetch(array):
-        part = array.shape[0] // copies
-        piece = lax.dynamic_slice_in_dim(array, dp * part, part, 0)
+    def fetch(array, axis):
+        part = array.shape[axis] // copies
+        piece = lax.dynamic_slice_in_dim(array, dp * part, part, axis)
         piece = route(piece, swap_pair)
-        return lax.all_gather(piece, "dp", axis=0, tiled=True)
+        return lax.all_gather(piece, "dp", axis=axis, tiled=True)
 
     def both_layers(array):
         other = route(array, swap_core)
         return [pick(core == layer, array, other) for layer in range(2)]
 
-    mixing = in_weight[0].reshape(width, 3 * local)
-    in_own, in_far = both_layers(mixing), both_layers(fetch(mixing))
-    out_own, out_far = both_layers(out_weight[0]), both_layers(fetch(out_weight[0]))
-    up_own, up_far = both_layers(up_weight[0]), both_layers(fetch(up_weight[0]))
-    down_own, down_far = both_layers(down_weight[0]), both_layers(fetch(down_weight[0]))
+    mixing = in_weight[0].transpose(1, 0, 2)
+
+    def slots(array, axis):
+        far = fetch(array, axis)
+        return [jnp.stack(pair) for pair in zip(both_layers(array), both_layers(far))]
+
+    w_in = slots(mixing, 1)
+    w_out = slots(out_weight[0], 0)
+    w_up = slots(up_weight[0], 0)
+    w_down = slots(down_weight[0], 0)
     shard_vec = jnp.concatenate([in_bias[0].reshape(-1), up_bias[0]])
     far_vec = route(shard_vec, swap_pair)
     whole_vec = jnp.concatenate(
@@ -290,55 +452,36 @@
     outputs = []
     for layer in range(2):
         bias_own, up_b_own, bias_far, up_b_far, gains, shifts, branch = unpack(vecs[layer])
-        w_in = (in_own[layer], in_far[layer])
         zero = jnp.zeros((local,), f32)
-        qkv_bias = [jnp.concatenate([b[0], zero, b[1]]) for b in (bias_own, bias_far)]
-        start = state.astype(f32)
-        normal, rstd = normalize(start)
-        normed = (normal * gains[0] + shifts[0]).astype(bf16)
-        packed = jnp.stack([(mm(normed, w_in[k]) + qkv_bias[k]).astype(bf16) for k in range(2)])
-        heads = to_heads(packed)
-        q, k, v = (heads[:, j * local : (j + 1) * local] for j in range(3))
-        mixed, logsum = attend(q, k, v, seg_col, seg_row)
-        attended = to_tokens(mixed)
-        part = mm(attended[0], out_own[layer]) + mm(attended[1], out_far[layer])
-        middle = start + branch_scale * (pair_sum(part) + branch[0])
-        normal2, rstd2 = normalize(middle)
-        upper = (normal2 * gains[1] + shifts[1]).astype(bf16)
-        hidden, slope = [], []
-        for w, b in ((up_own[layer], up_b_own), (up_far[layer], up_b_far)):
-            pre = mm(upper, w) + b
-            curve = jnp.tanh(root * (pre + cube * pre * pre * pre))
-            hidden.append((0.5 * pre * (1.0 + curve)).astype(bf16))
-            slope.append(
-                (
-                    0.5 * (1.0 + curve)
-                    + 0.5 * pre * (1.0 - curve * curve) * root * (1.0 + 3.0 * cube * pre * pre)
-                ).astype(bf16)
-            )
-        part = mm(hidden[0], down_own[layer]) + mm(hidden[1], down_far[layer])
-        result = middle + branch_scale * (pair_sum(part) + branch[1])
-        saved.append((start, normed, q, k, v, logsum, attended, middle, upper, hidden, slope))
-        state = result.astype(bf16)
+        b_in = jnp.stack([jnp.stack([b[0], zero, b[1]]) for b in (bias_own, bias_far)])[:, :, None]
+        b_up = jnp.stack([up_b_own, up_b_far])[:, None]
+        vec = jnp.concatenate([gains, shifts, branch], axis=0)
+        start = state
+        state, *kept = forward_layer(
+            state, w_in[layer], w_out[layer], w_up[layer], w_down[layer], b_in, b_up, vec, seg_col, seg_row
+        )
+        saved.append((start, *kept))
         outputs.append(state)
 
     partials = [None, None]
     vectors = [None, None]
     grads_out = [None, None]
     for layer in (1, 0):
-        start, normed, q, k, v, logsum, attended, middle, upper, hidden, slope = saved[layer]
+        start, normed, qkv, logsum, attended, middle, upper, hidden, slope = saved[layer]
+        q, k, v = qkv[0], qkv[1], qkv[2]
+        start = start.astype(f32)
         bias_own, up_b_own, bias_far, up_b_far, gains, shifts, branch = unpack(vecs[layer])
         gz = branch_scale * grad
         d_branch1 = jnp.sum(gz, axis=0)
         gz = gz.astype(bf16)
         d_pre, d_up, d_down, d_up_bias = [], [], [], []
-        for i, w in enumerate((down_own[layer], down_far[layer])):
+        for i, w in enumerate(w_down[layer]):
             dp_ = (mm_nt(gz, w) * slope[i].astype(f32)).astype(bf16)
             d_pre.append(dp_)
             d_down.append(mm_tn(hidden[i], gz).astype(bf16))
             d_up.append(mm_tn(upper, dp_).astype(bf16))
             d_up_bias.append(jnp.sum(dp_.astype(f32), axis=0))
-        part = mm_nt(d_pre[0], up_own[layer]) + mm_nt(d_pre[1], up_far[layer])
+        part = mm_nt(d_pre[0], w_up[layer][0]) + mm_nt(d_pre[1], w_up[layer][1])
         d_upper = pair_sum(part)
         normal2, rstd2 = normalize(middle)
         d_gain1 = jnp.sum(d_upper * normal2, axis=0)
@@ -349,14 +492,14 @@
         gy = gy.astype(bf16)
         d_out = [mm_tn(attended[i], gy).astype(bf16) for i in range(2)]
         d_att = jnp.stack(
-            [mm_nt(gy, w).astype(bf16) for w in (out_own[layer], out_far[layer])]
+            [mm_nt(gy, w).astype(bf16) for w in w_out[layer]]
         )
         d_heads = to_heads(d_att)
         dq, dk, dv = attend_back(q, k, v, d_heads, logsum, seg_col, seg_row)
         d_mix = to_tokens(jnp.concatenate([dq, dk, dv], axis=1))
-        d_in = [mm_tn(normed, d_mix[i]).astype(bf16) for i in range(2)]
+        d_in = [jnp.stack([mm_tn(normed, d_mix[i][:, j * local : (j + 1) * local]).astype(bf16) for j in range(3)]) for i in range(2)]
         d_mix_sum = jnp.sum(d_mix.astype(f32), axis=1)
-        part = mm_nt(d_mix[0], in_own[layer]) + mm_nt(d_mix[1], in_far[layer])
+        part = sum(mm_nt(d_mix[i][:, j * local : (j + 1) * local], w_in[layer][i, j]) for i in range(2) for j in range(3))
         d_normed = pair_sum(part)
         normal, rstd = normalize(start)
         d_gain0 = jnp.sum(d_normed * normal, axis=0)
@@ -379,7 +522,7 @@
         own, far = partials[layer][index]
         got = route(pick(core == 0, far, own), swap_core)
         total = (pick(core == 0, own, far).astype(f32) + got.astype(f32)).astype(bf16)
-        piece = lax.psum_scatter(total, "dp", scatter_dimension=0, tiled=True)
+        piece = lax.psum_scatter(total, "dp", scatter_dimension=total.ndim - 2, tiled=True)
         cross = route(piece, [(at(1, m), at(0, m ^ 2)) for m in range(4)])
         return piece + cross
 
@@ -388,7 +531,7 @@
         first = reduce_layer(index, 0)
         second = reduce_layer(index, 1)
         second = route(second, [(at(0, m), at(1, m)) for m in range(4)])
-        final.append(lax.all_gather(pick(core == 0, first, second), "dp", axis=0, tiled=True).astype(f32))
+        final.append(lax.all_gather(pick(core == 0, first, second), "dp", axis=first.ndim - 2, tiled=True).astype(f32))
     g_in, g_out, g_up, g_down = final
 
     shard_sum, whole_sum = [], []
@@ -422,7 +565,7 @@
         input_grads[None],
         whole_mine[0][None],
         whole_mine[1][None],
-        g_in.reshape(1, width, 3, local),
+        g_in.transpose(1, 0, 2)[None],
         shard_mine[: 2 * local].reshape(1, 2, local),
         g_out[None],
         g_up[None],

time: 659 us -> 684 us (1.038)
  Pallas kernels: 25.7 us -> 108 us
  waiting for transfers between devices: 202 us -> 128 us
  other arithmetic: 85.7 us -> 117 us
  matrix products: 87.8 us -> 70 us
  blocking collectives: 110 us -> 117 us
    pallas_call x2, Pallas kernels: 11.7 us -> 93.2 us  [forward_layer(): pl.pallas_call(forward_kernel, out_shape=(shape((half, width), bf16), sha...]
    ppermute x59 -> x51, waiting for transfers between devices: 167 us -> 112 us  [route(): return lax.ppermute(value, ('section', 'mp'), pairs)]
    another operation x2 -> x19, other arithmetic: 0.18 us -> 29.4 us  [the longest x14 29.1 us: slots(): jnp.stack(pair)]
    dot_general x16 -> x0, matrix products: 24.3 us -> none  [mm(): return jnp.dot(left, right, preferred_element_type=f32)]
    all_gather x4, waiting for transfers between devices: 34.8 us -> 15.5 us  [the longest x2 15.5 us: per_device(): lax.all_gather(pick(core == 0, first, second), 'dp', axis=first.ndim - 2,...]
    dot_general x16 -> x24, matrix products: 28.6 us -> 37.1 us  [mm_nt(): lax.dot_general(left, right, (((1,), (1,)), ((), ())), preferred_element_...]
    ppermute x59 -> x51, starting transfers between devices: 69.4 us -> 64.9 us  [route(): return lax.ppermute(value, ('section', 'mp'), pairs)]
    dot_general x16 -> x24, matrix products: 34.8 us -> 32.8 us  [mm_tn(): lax.dot_general(left, right, (((0,), (0,)), ((), ())), preferred_element_...]
  transfers between devices with their start and end apart: 71 -> 63, of which waited for: 24 -> 15; matrix products, arithmetic and copies ran while one was open for 27% -> 32% of each run, Pallas kernels for 3% -> 16%
where the time goes in v2:
time: 684 us; the launch traced here: 673 us
  waiting for transfers between devices  128 us (19%)
  other arithmetic  117 us (17%)
  blocking collectives  117 us (17%)
  Pallas kernels  108 us (16%)
  matrix products  70 us (10%)
  starting transfers between devices  65.9 us (10%)
  local copies, waits for them, and re-layouts  51 us (7%)
  between operations  16.6 us (2%)
    ppermute x51, waiting for transfers between devices, route(): return lax.ppermute(value, ('section', 'mp'), pairs)  112 us
    pallas_call x2, Pallas kernels, forward_layer(): pl.pallas_call(forward_kernel, out_shape=(shape((half, width), bf16), sha...  93.2 us
    ppermute x51, starting transfers between devices, route(): return lax.ppermute(value, ('section', 'mp'), pairs)  64.9 us
    psum x1, blocking collectives, per_device(): whole_sum = lax.psum(jnp.stack(whole_sum), ('section', 'mp', 'dp')) * 0.5  45.7 us
    dot_general x24, matrix products, mm_nt(): lax.dot_general(left, right, (((1,), (1,)), ((), ())), preferred_element_...  37.1 us
    dot_general x24, matrix products, mm_tn(): lax.dot_general(left, right, (((0,), (0,)), ((), ())), preferred_element_...  32.8 us
    all_gather x2, blocking collectives, fetch(): return lax.all_gather(piece, 'dp', axis=axis, tiled=True)  30.7 us
    another operation x14, other arithmetic, slots(): jnp.stack(pair)  29.1 us
  transfers between devices with their start and end apart: 63, of which 15 were waited for; matrix products, arithmetic and copies ran while one was open for 32% of the time, Pallas kernels for 16%

profile of v2, /device:TPU:0, one launch (start us, length us, event | category | flops | bytes accessed | tf_op | source)
XLA Modules:
  0.0 673.0 jit_solution(11837523379668570691)
XLA Ops:
  8.8 4.1 collective-permute-start.14
  15.6 2.9 collective-permute-start.12
  28.7 17.5 %collective-permute-done.12 = bf16[192,768]{1,0:T(8,128)(2,1)S(1)} collective-permute-done((bf16[192,768]{1,0:T(8,128)(2,1)}, bf16[192,768]{1,0:T(8,128)(2,1)S(1)}, u32[]{:S(2)}, u32[]{:S(2)}) %collective-permute-start.12) | collective-permute-done | bytes 294944 | tf_op jit(solution)/shard_map/ppermute | solution.py:362
  51.1 10.5 %all_gather.25 = bf16[192,768]{1,0:T(8,128)(2,1)S(1)} all-gather(bf16[48,768]{1,0:T(8,128)(2,1)S(1)} %collective-permute-done.6), channel_id=1, replica_groups=mesh['section'=2,'mp'=4,'dp'=4] {'dp'}, dimensions={0}, use_global_device_ids=true | all-gather | bytes 368640 | tf_op jit(solution)/shard_map/all_gather | solution.py:386
  61.5 5.8 collective-permute-done.3
  67.4 20.2 %all_gather.24 = bf16[3,768,192]{2,1,0:T(8,128)(2,1)S(1)} all-gather(bf16[3,192,192]{2,1,0:T(8,128)(2,1)} %collective-permute-done.3), channel_id=1, replica_groups=mesh['section'=2,'mp'=4,'dp'=4] {'dp'}, dimensions={1}, use_global_device_ids=true | all-gather | bytes 1105920 | tf_op jit(solution)/shard_map/all_gather | solution.py:386
  95.2 9.0 %collective-permute-done.1 = bf16[256,768]{1,0:T(8,128)(2,1)S(1)} collective-permute-done((bf16[256,768]{1,0:T(8,128)(2,1)S(1)}, bf16[256,768]{1,0:T(8,128)(2,1)S(1)}, u32[]{:S(2)}, u32[]{:S(2)}) %collective-permute-start.1) | collective-permute-done | bytes 393248 | tf_op jit(solution)/shard_map/ppermute | solution.py:362
  108.7 3.2 fusion.56
  114.5 2.9 select_bitcast_fusion
  120.4 3.5 pad_maximum_fusion.w_in
  135.9 44.1 %forward_layer.2 = (bf16[512,768]{1,0:T(8,128)(2,1)S(1)}, bf16[512,768]{1,0:T(8,128)(2,1)S(1)}, bf16[3,1024,192]{2,1,0:T(8,128)(2,1)}, f32[3,1024]{1,0:T(4,128)S...) custom-call(bf16[512,768]{1,0:T(8,128)(2,1)} %copy-done.15, ...), custom_call_target="tpu_custom_call" | custom-call | tf_op jit(solution)/shard_map/forward_layer/pallas_call | solution.py:291
  186.3 3.6 pad_maximum_fusion.4
  189.9 49.1 %forward_layer.3 = (bf16[512,768]{1,0:T(8,128)(2,1)S(1)}, bf16[512,768]{1,0:T(8,128)(2,1)S(1)}, bf16[3,1024,192]{2,1,0:T(8,128)(2,1)}, f32[3,1024]{1,0:T(4,128)S...) custom-call(bf16[512,768]{1,0:T(8,128)(2,1)} %copy-done, ...), custom_call_target="tpu_custom_call" | custom-call | tf_op jit(solution)/shard_map/forward_layer/pallas_call | solution.py:291
  250.2 4.1 broadcast_select_fusion.4
  254.3 7.0 %collective-permute-start.48 = (bf16[768,768]{1,0:T(8,128)(2,1)}, bf16[768,768]{1,0:T(8,128)(2,1)}, u32[]{:S(2)}, u32[]{:S(2)}) collective-permute-start(bf16[768,768]{1,0:T(8,128)(2,1)} %get-tuple-element.243), channel_id=1, source_target_pairs={{0,16},{4,20},{8,24},{12,28},{16,0},{20,4},{24,8},{28,12},{1,17},{... | collective-permute-start | bytes 3538952 | tf_op jit(solution)/shard_map/ppermute | solution.py:362
  261.3 3.4 convert_reduce_fusion.4
  264.7 3.6 convert_reduce_fusion.5
  275.4 14.7 %collective-permute-done.20 = bf16[512,768]{1,0:T(8,128)(2,1)S(1)} collective-permute-done((bf16[512,768]{1,0:T(8,128)(2,1)S(1)}, bf16[512,768]{1,0:T(8,128)(2,1)S(1)}, u32[]{:S(2)}, u32[]{:S(2)}) %collective-permute-start.20) | collective-permute-done | bytes 786464 | tf_op jit(solution)/shard_map/ppermute | solution.py:362
  291.5 3.0 multiply_reduce_fusion.7
  300.7 7.5 %attend_back.2 = (bf16[1024,192]{1,0:T(8,128)(2,1)S(1)}, bf16[1024,192]{1,0:T(8,128)(2,1)S(1)}, bf16[1024,192]{1,0:T(8,128)(2,1)S(1)}) custom-call(bf16[1024,192]{1,0:T(8,128)(2,1)S(1)} %get-tuple-element.173.q_ref, bf16[1024,192]{1,0:T(8,128)(2,1)S(1)} %get-tuple-element.172.k_ref, bf16[1024,192]{1,0:T(8,128)(2,1)S(1)} %get-tuple-element.171.v_ref, ...), custom_call_target="tpu_custom_call" | custom-call | tf_op jit(solution)/shard_map/attend_back/pallas_call | solution.py:113
  313.9 3.6 broadcast_select_fusion.6
  319.7 3.1 add_convert_fusion
  336.0 14.3 %collective-permute-done.23 = bf16[512,768]{1,0:T(8,128)(2,1)} collective-permute-done((bf16[512,768]{1,0:T(8,128)(2,1)}, bf16[512,768]{1,0:T(8,128)(2,1)}, u32[]{:S(2)}, u32[]{:S(2)}) %collective-permute-start.23) | collective-permute-done | bytes 786464 | tf_op jit(solution)/shard_map/ppermute | solution.py:362
  350.3 2.9 fusion.26
  359.9 3.1 add_convert_fusion.7
  372.5 10.1 %collective-permute-done.24 = bf16[512,768]{1,0:T(8,128)(2,1)} collective-permute-done((bf16[512,768]{1,0:T(8,128)(2,1)}, bf16[512,768]{1,0:T(8,128)(2,1)}, u32[]{:S(2)}, u32[]{:S(2)}) %collective-permute-start.24) | collective-permute-done | bytes 786464 | tf_op jit(solution)/shard_map/ppermute | solution.py:362
  382.6 3.0 multiply_reduce_fusion.1
  395.3 3.1 collective-permute-start.17
  399.3 3.0 convolution_convert_fusion.3
  403.8 3.5 add_convert_fusion.4
  407.4 3.5 broadcast_select_fusion.5
  415.6 6.2 collective-permute-done.39
  425.3 3.1 add_convert_fusion.1
  438.2 7.1 %attend_back.3 = (bf16[1024,192]{1,0:T(8,128)(2,1)S(1)}, bf16[1024,192]{1,0:T(8,128)(2,1)S(1)}, bf16[1024,192]{1,0:T(8,128)(2,1)S(1)}) custom-call(bf16[1024,192]{1,0:T(8,128)(2,1)S(1)} %get-tuple-element.170.q_ref, bf16[1024,192]{1,0:T(8,128)(2,1)S(1)} %get-tuple-element.169.k_ref, bf16[1024,192]{1,0:T(8,128)(2,1)S(1)} %get-tuple-element.168.v_ref, ...), custom_call_target="tpu_custom_call" | custom-call | tf_op jit(solution)/shard_map/attend_back/pallas_call | solution.py:113
  450.4 3.3 add_convert_fusion.3
  453.8 8.9 %collective-permute-done.49 = bf16[192,768]{1,0:T(8,128)(2,1)S(1)} collective-permute-done((bf16[192,768]{1,0:T(8,128)(2,1)}, bf16[192,768]{1,0:T(8,128)(2,1)S(1)}, u32[]{:S(2)}, u32[]{:S(2)}) %collective-permute-start.49) | collective-permute-done | bytes 294944 | tf_op jit(solution)/shard_map/ppermute | solution.py:362
  484.8 3.9 add_convert_fusion.6
  492.5 16.2 %psum.15 = f32[2,1152]{1,0:T(2,128)S(1)} all-reduce(f32[2,1152]{1,0:T(2,128)S(1)} %fusion.141), channel_id=1, replica_groups=mesh['section'=2,'mp'=4,'dp'=4] {'section','dp'}, use_global_device_ids=true, to_apply=%region_39.40 | all-reduce | flops 2304 | bytes 18432 | tf_op jit(solution)/shard_map/psum | solution.py:544
  512.4 3.7 collective-permute-done.37
  517.0 9.9 %all_gather.29 = bf16[192,768]{1,0:T(8,128)(2,1)S(1)} all-gather(bf16[48,768]{1,0:T(8,128)(2,1)S(1)} %add_select_fusion.3), channel_id=1, replica_groups=mesh['section'=2,'mp'=4,'dp'=4] {'dp'}, dimensions={0}, use_global_device_ids=true | all-gather | bytes 368640 | tf_op jit(solution)/shard_map/all_gather | solution.py:534
  529.1 9.4 %collective-permute-done.33 = bf16[3,192,192]{2,1,0:T(8,128)(2,1)S(1)} collective-permute-done((bf16[3,192,192]{2,1,0:T(8,128)(2,1)}, bf16[3,192,192]{2,1,0:T(8,128)(2,1)S(1)}, u32[]{:S(2)}, u32[]{:S(2)}) %collective-permute-start.33) | collective-permute-done | bytes 221216 | tf_op jit(solution)/shard_map/ppermute | solution.py:362
  546.8 3.7 add_convert_fusion.5
  556.4 45.7 %psum.14 = f32[2,4608]{1,0:T(2,128)S(1)} all-reduce(f32[2,4608]{1,0:T(2,128)S(1)} %pad_maximum_fusion.14), channel_id=1, replica_groups=mesh['section'=2,'mp'=4,'dp'=4] {'section','mp','dp'}, use_global_device_ids=true, to_apply=%region_30.31 | all-reduce | flops 9216 | bytes 73728 | tf_op jit(solution)/shard_map/psum | solution.py:545
  607.2 4.3 collective-permute-start.29
  611.6 4.2 collective-permute-done.42
  621.2 7.0 %collective-permute-done.31 = bf16[3,192,192]{2,1,0:T(8,128)(2,1)S(1)} collective-permute-done((bf16[3,192,192]{2,1,0:T(8,128)(2,1)}, bf16[3,192,192]{2,1,0:T(8,128)(2,1)S(1)}, u32[]{:S(2)}, u32[]{:S(2)}) %collective-permute-start.31) | collective-permute-done | bytes 221216 | tf_op jit(solution)/shard_map/ppermute | solution.py:362
  628.3 14.5 %all_gather.28 = bf16[3,768,192]{2,1,0:T(8,128)(2,1)S(1)} all-gather(bf16[3,192,192]{2,1,0:T(8,128)(2,1)S(1)} %add_select_fusion.2), channel_id=1, replica_groups=mesh['section'=2,'mp'=4,'dp'=4] {'dp'}, dimensions={1}, use_global_device_ids=true | all-gather | bytes 1105920 | tf_op jit(solution)/shard_map/all_gather | solution.py:534
  647.7 15.5 %all-gather.9.cloned.1.call-done = bf16[768,768]{1,0:T(8,128)(2,1)} async-done(((bf16[192,768]{1,0:T(8,128)(2,1)}), bf16[768,768]{1,0:T(8,128)(2,1)}) %all-gather.9.cloned.1.call-update) | async-done | bytes 1179664 | tf_op jit(solution)/shard_map/all_gather | solution.py:534
  (583 shorter events, 217.1 us)
Async XLA Ops:
  7.2 107.0 %all-gather.7.cloned.1.call-start = ((), (), s32[]{:S(2)}) async-start(), calls=%async_computation.9 | async-start | bytes 1474560 | tf_op jit(solution)/shard_map/all_gather | solution.py:386
  8.8 17.6 %collective-permute-start.14 = (f32[1152]{0:T(1024)S(1)}, f32[1152]{0:T(1024)S(1)}, u32[]{:S(2)}, u32[]{:S(2)}) collective-permute-start(f32[1152]{0:T(1024)S(1)} %pad_maximum_fusion.20), channel_id=1, source_target_pairs={{0,8},{4,12},{8,0},{12,4},{16,24},{20,28},{24,16},{28,20},{1,9},{5... | collective-permute-start | bytes 13832 | tf_op jit(solution)/shard_map/ppermute | solution.py:362
  13.8 35.2 %collective-permute-start.6 = (bf16[48,768]{1,0:T(8,128)(2,1)S(1)}, bf16[48,768]{1,0:T(8,128)(2,1)S(1)}, u32[]{:S(2)}, u32[]{:S(2)}) collective-permute-start(bf16[48,768]{1,0:T(8,128)(2,1)S(1)} %dynamic-slice_bitcast_fusion.2), channel_id=1, source_target_pairs={{0,8},{4,12},{8,0},{12,4},{16,24},{20,28},{24,16},{28,20},{1,9},{5... | collective-permute-start | bytes 221192 | tf_op jit(solution)/shard_map/ppermute | solution.py:362
  15.6 30.6 %collective-permute-start.12 = (bf16[192,768]{1,0:T(8,128)(2,1)}, bf16[192,768]{1,0:T(8,128)(2,1)S(1)}, u32[]{:S(2)}, u32[]{:S(2)}) collective-permute-start(bf16[192,768]{1,0:T(8,128)(2,1)} %dynamic-slice_bitcast_fusion), channel_id=1, source_target_pairs={{0,8},{4,12},{8,0},{12,4},{16,24},{20,28},{24,16},{28,20},{1,9},{5... | collective-permute-start | bytes 884744 | tf_op jit(solution)/shard_map/ppermute | solution.py:362
  20.2 68.8 %collective-permute-start.9 = (bf16[192,768]{1,0:T(8,128)(2,1)}, bf16[192,768]{1,0:T(8,128)(2,1)}, u32[]{:S(2)}, u32[]{:S(2)}) collective-permute-start(bf16[192,768]{1,0:T(8,128)(2,1)} %dynamic-slice_bitcast_fusion.1), channel_id=1, source_target_pairs={{0,8},{4,12},{8,0},{12,4},{16,24},{20,28},{24,16},{28,20},{1,9},{5... | collective-permute-start | bytes 884744 | tf_op jit(solution)/shard_map/ppermute | solution.py:362
  21.3 46.1 %collective-permute-start.3 = (bf16[3,192,192]{2,1,0:T(8,128)(2,1)}, bf16[3,192,192]{2,1,0:T(8,128)(2,1)}, u32[]{:S(2)}, u32[]{:S(2)}) collective-permute-start(bf16[3,192,192]{2,1,0:T(8,128)(2,1)} %bitcast.373), channel_id=1, source_target_pairs={{0,8},{4,12},{8,0},{12,4},{16,24},{20,28},{24,16},{28,20},{1,9},{5... | collective-permute-start | bytes 663560 | tf_op jit(solution)/shard_map/ppermute | solution.py:362
  28.1 60.9 %collective-permute-start.5 = (bf16[192,768]{1,0:T(8,128)(2,1)}, bf16[192,768]{1,0:T(8,128)(2,1)S(1)}, u32[]{:S(2)}, u32[]{:S(2)}) collective-permute-start(bf16[192,768]{1,0:T(8,128)(2,1)} %bitcast.10), channel_id=1, source_target_pairs={{0,16},{4,20},{8,24},{12,28},{16,0},{20,4},{24,8},{28,12},{1,17},{... | collective-permute-start | bytes 884744 | tf_op jit(solution)/shard_map/ppermute | solution.py:362
  46.2 46.6 %collective-permute-start.18 = (bf16[256,768]{1,0:T(8,128)(2,1)}, bf16[256,768]{1,0:T(8,128)(2,1)}, u32[]{:S(2)}, u32[]{:S(2)}) collective-permute-start(bf16[256,768]{1,0:T(8,128)(2,1)} %select_bitcast_fusion.3), channel_id=1, source_target_pairs={{0,8},{4,12},{24,16},{28,20},{1,9},{5,13},{25,17},{29,21},{2,10},{... | collective-permute-start | bytes 1179656 | tf_op jit(solution)/shard_map/ppermute | solution.py:362
  48.5 71.7 %all-gather.5.cloned.1.call-start = ((), (), s32[]{:S(2)}) async-start(), calls=%async_computation.8 | async-start | bytes 1474560 | tf_op jit(solution)/shard_map/all_gather | solution.py:386
  49.0 43.4 %collective-permute-start = (bf16[256,768]{1,0:T(8,128)(2,1)}, bf16[256,768]{1,0:T(8,128)(2,1)}, u32[]{:S(2)}, u32[]{:S(2)}) collective-permute-start(bf16[256,768]{1,0:T(8,128)(2,1)} %select_bitcast_fusion.4), channel_id=1, source_target_pairs={{0,8},{4,12},{24,16},{28,20},{1,9},{5,13},{25,17},{29,21},{2,10},{... | collective-permute-start | bytes 1179656 | tf_op jit(solution)/shard_map/ppermute | solution.py:362
  67.4 23.9 %collective-permute-start.7 = (bf16[192,768]{1,0:T(8,128)(2,1)S(1)}, bf16[192,768]{1,0:T(8,128)(2,1)}, u32[]{:S(2)}, u32[]{:S(2)}) collective-permute-start(bf16[192,768]{1,0:T(8,128)(2,1)S(1)} %all_gather.25), channel_id=1, source_target_pairs={{0,16},{4,20},{8,24},{12,28},{16,0},{20,4},{24,8},{28,12},{1,17},{... | collective-permute-start | bytes 884744 | tf_op jit(solution)/shard_map/ppermute | solution.py:362
  88.9 17.4 %collective-permute-start.2 = (bf16[3,768,192]{1,2,0:T(8,128)(2,1)}, bf16[3,768,192]{1,2,0:T(8,128)(2,1)}, u32[]{:S(2)}, u32[]{:S(2)}) collective-permute-start(bf16[3,768,192]{1,2,0:T(8,128)(2,1)} %bitcast.372), channel_id=1, source_target_pairs={{0,16},{4,20},{8,24},{12,28},{16,0},{20,4},{24,8},{28,12},{1,17},{... | collective-permute-start | bytes 2654216 | tf_op jit(solution)/shard_map/ppermute | solution.py:362
  88.9 325.3 %reduce-scatter.15.cloned.1.call-start = ((), (), s32[]{:S(2)}) async-start(), calls=%async_computation.13 | async-start | bytes 368640 | tf_op jit(solution)/shard_map/reduce_scatter | solution.py:525
  89.7 37.1 %collective-permute-start.11 = (bf16[768,768]{1,0:T(8,128)(2,1)}, bf16[768,768]{1,0:T(8,128)(2,1)}, u32[]{:S(2)}, u32[]{:S(2)}) collective-permute-start(bf16[768,768]{1,0:T(8,128)(2,1)} %bitcast.371), channel_id=1, source_target_pairs={{0,16},{4,20},{8,24},{12,28},{16,0},{20,4},{24,8},{28,12},{1,17},{... | collective-permute-start | bytes 3538952 | tf_op jit(solution)/shard_map/ppermute | solution.py:362
  91.3 32.6 %collective-permute-start.8 = (bf16[768,768]{1,0:T(8,128)(2,1)}, bf16[768,768]{1,0:T(8,128)(2,1)}, u32[]{:S(2)}, u32[]{:S(2)}) collective-permute-start(bf16[768,768]{1,0:T(8,128)(2,1)} %bitcast.14), channel_id=1, source_target_pairs={{0,16},{4,20},{8,24},{12,28},{16,0},{20,4},{24,8},{28,12},{1,17},{... | collective-permute-start | bytes 3538952 | tf_op jit(solution)/shard_map/ppermute | solution.py:362
  92.8 19.1 %collective-permute-start.4 = (bf16[3,768,192]{1,2,0:T(8,128)(2,1)}, bf16[3,768,192]{1,2,0:T(8,128)(2,1)}, u32[]{:S(2)}, u32[]{:S(2)}) collective-permute-start(bf16[3,768,192]{1,2,0:T(8,128)(2,1)} %copy.196), channel_id=1, source_target_pairs={{0,16},{4,20},{8,24},{12,28},{16,0},{20,4},{24,8},{28,12},{1,17},{... | collective-permute-start | bytes 2654216 | tf_op jit(solution)/shard_map/ppermute | solution.py:362
  104.2 143.7 %collective-permute-start.19 = (bf16[256,768]{1,0:T(8,128)(2,1)}, bf16[256,768]{1,0:T(8,128)(2,1)}, u32[]{:S(2)}, u32[]{:S(2)}) collective-permute-start(bf16[256,768]{1,0:T(8,128)(2,1)} %bitcast_select_fusion.5), channel_id=1, source_target_pairs={{0,4},{4,0},{8,12},{12,8},{16,20},{20,16},{24,28},{28,24},{1,5},{5... | collective-permute-start | bytes 1179656 | tf_op jit(solution)/shard_map/ppermute | solution.py:362
  114.2 15.2 %collective-permute-start.13 = (bf16[768,768]{1,0:T(8,128)(2,1)}, bf16[768,768]{1,0:T(8,128)(2,1)}, u32[]{:S(2)}, u32[]{:S(2)}) collective-permute-start(bf16[768,768]{1,0:T(8,128)(2,1)} %all-gather.7.cloned.1.call-done), channel_id=1, source_target_pairs={{0,16},{4,20},{8,24},{12,28},{16,0},{20,4},{24,8},{28,12},{1,17},{... | collective-permute-start | bytes 3538952 | tf_op jit(solution)/shard_map/ppermute | solution.py:362
  246.1 145.4 %collective-permute-start.16 = (bf16[2,256,768]{2,1,0:T(8,128)(2,1)}, bf16[2,256,768]{2,1,0:T(8,128)(2,1)}, u32[]{:S(2)}, u32[]{:S(2)}) collective-permute-start(bf16[2,256,768]{2,1,0:T(8,128)(2,1)} %fusion.60), channel_id=1, source_target_pairs={{8,0},{12,4},{16,24},{20,28},{9,1},{13,5},{17,25},{21,29},{10,2},{... | collective-permute-start | bytes 2359304 | tf_op jit(solution)/shard_map/ppermute | solution.py:362
  254.3 65.4 %collective-permute-start.48 = (bf16[768,768]{1,0:T(8,128)(2,1)}, bf16[768,768]{1,0:T(8,128)(2,1)}, u32[]{:S(2)}, u32[]{:S(2)}) collective-permute-start(bf16[768,768]{1,0:T(8,128)(2,1)} %get-tuple-element.243), channel_id=1, source_target_pairs={{0,16},{4,20},{8,24},{12,28},{16,0},{20,4},{24,8},{28,12},{1,17},{... | collective-permute-start | bytes 3538952 | tf_op jit(solution)/shard_map/ppermute | solution.py:362
  271.7 18.4 %collective-permute-start.20 = (bf16[512,768]{1,0:T(8,128)(2,1)S(1)}, bf16[512,768]{1,0:T(8,128)(2,1)S(1)}, u32[]{:S(2)}, u32[]{:S(2)}) collective-permute-start(bf16[512,768]{1,0:T(8,128)(2,1)S(1)} %add_convert_fusion.9), channel_id=1, source_target_pairs={{0,4},{4,0},{8,12},{12,8},{16,20},{20,16},{24,28},{28,24},{1,5},{5... | collective-permute-start | bytes 2359304 | tf_op jit(solution)/shard_map/ppermute | solution.py:362
  313.8 133.9 %reduce-scatter.23.cloned.1.call-start = ((), (), s32[]{:S(2)}) async-start(), calls=%async_computation.18 | async-start | bytes 1474560 | tf_op jit(solution)/shard_map/reduce_scatter | solution.py:525
  317.5 14.6 %collective-permute-start.43 = (bf16[768,768]{1,0:T(8,128)(2,1)}, bf16[768,768]{1,0:T(8,128)(2,1)}, u32[]{:S(2)}, u32[]{:S(2)}) collective-permute-start(bf16[768,768]{1,0:T(8,128)(2,1)} %get-tuple-element.239), channel_id=1, source_target_pairs={{0,16},{4,20},{8,24},{12,28},{16,0},{20,4},{24,8},{28,12},{1,17},{... | collective-permute-start | bytes 3538952 | tf_op jit(solution)/shard_map/ppermute | solution.py:362
  322.8 126.3 %reduce-scatter.19.cloned.1.call-start = ((), (), s32[]{:S(2)}) async-start(), calls=%async_computation.15 | async-start | bytes 1474560 | tf_op jit(solution)/shard_map/reduce_scatter | solution.py:525
  330.5 19.8 %collective-permute-start.23 = (bf16[512,768]{1,0:T(8,128)(2,1)}, bf16[512,768]{1,0:T(8,128)(2,1)}, u32[]{:S(2)}, u32[]{:S(2)}) collective-permute-start(bf16[512,768]{1,0:T(8,128)(2,1)} %add_convert_fusion.8), channel_id=1, source_target_pairs={{0,4},{4,0},{8,12},{12,8},{16,20},{20,16},{24,28},{28,24},{1,5},{5... | collective-permute-start | bytes 2359304 | tf_op jit(solution)/shard_map/ppermute | solution.py:362
  334.9 174.4 %reduce-scatter.13.cloned.1.call-start = ((), (), s32[]{:S(2)}) async-start(), calls=%async_computation.12 | async-start | bytes 368640 | tf_op jit(solution)/shard_map/reduce_scatter | solution.py:525
  363.0 19.5 %collective-permute-start.24 = (bf16[512,768]{1,0:T(8,128)(2,1)}, bf16[512,768]{1,0:T(8,128)(2,1)}, u32[]{:S(2)}, u32[]{:S(2)}) collective-permute-start(bf16[512,768]{1,0:T(8,128)(2,1)} %add_convert_fusion.7), channel_id=1, source_target_pairs={{0,4},{4,0},{8,12},{12,8},{16,20},{20,16},{24,28},{28,24},{1,5},{5... | collective-permute-start | bytes 2359304 | tf_op jit(solution)/shard_map/ppermute | solution.py:362
  370.4 31.9 %collective-permute-start.32 = (bf16[3,768,192]{1,2,0:T(8,128)(2,1)}, bf16[3,768,192]{1,2,0:T(8,128)(2,1)}, u32[]{:S(2)}, u32[]{:S(2)}) collective-permute-start(bf16[3,768,192]{1,2,0:T(8,128)(2,1)} %copy.233), channel_id=1, source_target_pairs={{0,16},{4,20},{8,24},{12,28},{16,0},{20,4},{24,8},{28,12},{1,17},{... | collective-permute-start | bytes 2654216 | tf_op jit(solution)/shard_map/ppermute | solution.py:362
  395.3 16.6 %collective-permute-start.17 = (bf16[2,256,768]{2,1,0:T(8,128)(2,1)}, bf16[2,256,768]{2,1,0:T(8,128)(2,1)}, u32[]{:S(2)}, u32[]{:S(2)}) collective-permute-start(bf16[2,256,768]{2,1,0:T(8,128)(2,1)} %select_bitcast_fusion.2), channel_id=1, source_target_pairs={{0,16},{4,20},{24,8},{28,12},{1,17},{5,21},{25,9},{29,13},{2,18},{... | collective-permute-start | bytes 2359304 | tf_op jit(solution)/shard_map/ppermute | solution.py:362
  399.3 127.6 %reduce-scatter.11.cloned.1.call-start = ((), (), s32[]{:S(2)}) async-start(), calls=%async_computation.11 | async-start | bytes 1474560 | tf_op jit(solution)/shard_map/reduce_scatter | solution.py:525
  407.4 147.6 %reduce-scatter.21.cloned.1.call-start = ((), (), s32[]{:S(2)}) async-start(), calls=%async_computation.17 | async-start | bytes 1474560 | tf_op jit(solution)/shard_map/reduce_scatter | solution.py:525
  411.0 14.3 %collective-permute-start.46 = (bf16[768,768]{1,0:T(8,128)(2,1)}, bf16[768,768]{1,0:T(8,128)(2,1)}, u32[]{:S(2)}, u32[]{:S(2)}) collective-permute-start(bf16[768,768]{1,0:T(8,128)(2,1)} %get-tuple-element.245), channel_id=1, source_target_pairs={{0,16},{4,20},{8,24},{12,28},{16,0},{20,4},{24,8},{28,12},{1,17},{... | collective-permute-start | bytes 3538952 | tf_op jit(solution)/shard_map/ppermute | solution.py:362
  423.4 87.9 %collective-permute-start.40 = (bf16[48,768]{1,0:T(8,128)(2,1)}, bf16[48,768]{1,0:T(8,128)(2,1)}, u32[]{:S(2)}, u32[]{:S(2)}) collective-permute-start(bf16[48,768]{1,0:T(8,128)(2,1)} %add.247), channel_id=1, source_target_pairs={{0,16},{4,20},{8,24},{12,28},{1,17},{5,21},{9,25},{13,29},{2,18},{... | collective-permute-start | bytes 221192 | tf_op jit(solution)/shard_map/ppermute | solution.py:362
  428.4 175.7 %reduce-scatter.17.cloned.1.call-start = ((), (), s32[]{:S(2)}) async-start(), calls=%async_computation.14 | async-start | bytes 1474560 | tf_op jit(solution)/shard_map/reduce_scatter | solution.py:525
  433.5 17.0 %collective-permute-start.41 = (bf16[768,768]{1,0:T(8,128)(2,1)}, bf16[768,768]{1,0:T(8,128)(2,1)}, u32[]{:S(2)}, u32[]{:S(2)}) collective-permute-start(bf16[768,768]{1,0:T(8,128)(2,1)} %get-tuple-element.241), channel_id=1, source_target_pairs={{0,16},{4,20},{8,24},{12,28},{16,0},{20,4},{24,8},{28,12},{1,17},{... | collective-permute-start | bytes 3538952 | tf_op jit(solution)/shard_map/ppermute | solution.py:362
  447.1 21.8 %collective-permute-start.26 = (bf16[512,576]{0,1:T(8,128)(2,1)}, bf16[512,576]{0,1:T(8,128)(2,1)}, u32[]{:S(2)}, u32[]{:S(2)}) collective-permute-start(bf16[512,576]{0,1:T(8,128)(2,1)} %copy.213), channel_id=1, source_target_pairs={{0,16},{4,20},{8,24},{12,28},{16,0},{20,4},{24,8},{28,12},{1,17},{... | collective-permute-start | bytes 1769480 | tf_op jit(solution)/shard_map/ppermute | solution.py:362
  447.8 14.9 %collective-permute-start.49 = (bf16[192,768]{1,0:T(8,128)(2,1)}, bf16[192,768]{1,0:T(8,128)(2,1)S(1)}, u32[]{:S(2)}, u32[]{:S(2)}) collective-permute-start(bf16[192,768]{1,0:T(8,128)(2,1)} %reduce-scatter.23.cloned.1.call-done), channel_id=1, source_target_pairs={{16,8},{20,12},{24,0},{28,4},{17,9},{21,13},{25,1},{29,5},{18,10},... | collective-permute-start | bytes 884744 | tf_op jit(solution)/shard_map/ppermute | solution.py:362
  449.1 16.8 %collective-permute-start.44 = (bf16[192,768]{1,0:T(8,128)(2,1)}, bf16[192,768]{1,0:T(8,128)(2,1)S(1)}, u32[]{:S(2)}, u32[]{:S(2)}) collective-permute-start(bf16[192,768]{1,0:T(8,128)(2,1)} %reduce-scatter.19.cloned.1.call-done), channel_id=1, source_target_pairs={{16,8},{20,12},{24,0},{28,4},{17,9},{21,13},{25,1},{29,5},{18,10},... | collective-permute-start | bytes 884744 | tf_op jit(solution)/shard_map/ppermute | solution.py:362
  453.8 164.7 %reduce-scatter.9.cloned.1.call-start = ((), (), s32[]{:S(2)}) async-start(), calls=%async_computation.10 | async-start | bytes 1474560 | tf_op jit(solution)/shard_map/reduce_scatter | solution.py:525
  463.5 139.7 %collective-permute-start.50 = (bf16[192,768]{1,0:T(8,128)(2,1)}, bf16[192,768]{1,0:T(8,128)(2,1)}, u32[]{:S(2)}, u32[]{:S(2)}) collective-permute-start(bf16[192,768]{1,0:T(8,128)(2,1)} %add.255), channel_id=1, source_target_pairs={{0,16},{4,20},{8,24},{12,28},{1,17},{5,21},{9,25},{13,29},{2,18},{... | collective-permute-start | bytes 884744 | tf_op jit(solution)/shard_map/ppermute | solution.py:362
  466.7 144.9 %collective-permute-start.45 = (bf16[192,768]{1,0:T(8,128)(2,1)}, bf16[192,768]{1,0:T(8,128)(2,1)}, u32[]{:S(2)}, u32[]{:S(2)}) collective-permute-start(bf16[192,768]{1,0:T(8,128)(2,1)} %add.251), channel_id=1, source_target_pairs={{0,16},{4,20},{8,24},{12,28},{1,17},{5,21},{9,25},{13,29},{2,18},{... | collective-permute-start | bytes 884744 | tf_op jit(solution)/shard_map/ppermute | solution.py:362
  490.6 51.7 %collective-permute-start.27 = (bf16[512,768]{1,0:T(8,128)(2,1)S(1)}, bf16[512,768]{1,0:T(8,128)(2,1)}, u32[]{:S(2)}, u32[]{:S(2)}) collective-permute-start(bf16[512,768]{1,0:T(8,128)(2,1)S(1)} %add_convert_fusion.6), channel_id=1, source_target_pairs={{0,4},{4,0},{8,12},{12,8},{16,20},{20,16},{24,28},{28,24},{1,5},{5... | collective-permute-start | bytes 2359304 | tf_op jit(solution)/shard_map/ppermute | solution.py:362
  511.3 33.2 %collective-permute-start.30 = (bf16[3,768,192]{1,2,0:T(8,128)(2,1)}, bf16[3,768,192]{1,2,0:T(8,128)(2,1)}, u32[]{:S(2)}, u32[]{:S(2)}) collective-permute-start(bf16[3,768,192]{1,2,0:T(8,128)(2,1)} %copy.225), channel_id=1, source_target_pairs={{0,16},{4,20},{8,24},{12,28},{16,0},{20,4},{24,8},{28,12},{1,17},{... | collective-permute-start | bytes 2654216 | tf_op jit(solution)/shard_map/ppermute | solution.py:362
  540.2 81.0 %collective-permute-start.34 = (bf16[3,192,192]{2,1,0:T(8,128)(2,1)}, bf16[3,192,192]{2,1,0:T(8,128)(2,1)}, u32[]{:S(2)}, u32[]{:S(2)}) collective-permute-start(bf16[3,192,192]{2,1,0:T(8,128)(2,1)} %add.242), channel_id=1, source_target_pairs={{0,16},{4,20},{8,24},{12,28},{1,17},{5,21},{9,25},{13,29},{2,18},{... | collective-permute-start | bytes 663560 | tf_op jit(solution)/shard_map/ppermute | solution.py:362
  550.5 94.3 %all-gather.11.cloned.1.call-start = ((), (), s32[]{:S(2)}) async-start(), calls=%async_computation.19 | async-start | bytes 1474560 | tf_op jit(solution)/shard_map/all_gather | solution.py:534
  553.6 51.8 %collective-permute-start.28 = (bf16[2,256,768]{2,1,0:T(8,128)(2,1)S(1)}, bf16[2,256,768]{2,1,0:T(8,128)(2,1)}, u32[]{:S(2)}, u32[]{:S(2)}) collective-permute-start(bf16[2,256,768]{2,1,0:T(8,128)(2,1)S(1)} %fusion.59), channel_id=1, source_target_pairs={{8,0},{12,4},{16,24},{20,28},{9,1},{13,5},{17,25},{21,29},{10,2},{... | collective-permute-start | bytes 2359304 | tf_op jit(solution)/shard_map/ppermute | solution.py:362
  555.0 48.2 %collective-permute-start.47 = (bf16[192,768]{1,0:T(8,128)(2,1)}, bf16[192,768]{1,0:T(8,128)(2,1)S(1)}, u32[]{:S(2)}, u32[]{:S(2)}) collective-permute-start(bf16[192,768]{1,0:T(8,128)(2,1)} %reduce-scatter.21.cloned.1.call-done), channel_id=1, source_target_pairs={{16,8},{20,12},{24,0},{28,4},{17,9},{21,13},{25,1},{29,5},{18,10},... | collective-permute-start | bytes 884744 | tf_op jit(solution)/shard_map/ppermute | solution.py:362
  604.0 59.1 %all-gather.9.cloned.1.call-start = ((), (), s32[]{:S(2)}) async-start(), calls=%async_computation.16 | async-start | bytes 1474560 | tf_op jit(solution)/shard_map/all_gather | solution.py:534
  (130 other events, 856.1 us)
Sparse Core Ops, SparseCore 0:
  48.7 30.9 all-gather.6
  89.1 25.9 all-gather.4
  314.0 22.1 reduce-scatter.14
  338.9 28.5 reduce-scatter.22
  370.8 28.5 reduce-scatter.18
  402.0 24.1 reduce-scatter.12
  429.1 28.5 reduce-scatter.10
  460.6 28.5 reduce-scatter.20
  492.1 29.4 reduce-scatter.16
  550.6 27.3 reduce-scatter.8
  604.2 29.0 all-gather.10
  635.0 28.1 all-gather.8

commit v3 on v2

--- a/solution.py
+++ b/solution.py
@@ -68,57 +68,6 @@
     key = lax.broadcasted_iota(jnp.int32, (count, rows.stop - rows.start), 0)
     query = lax.broadcasted_iota(jnp.int32, (count, rows.stop - rows.start), 1) + rows.start
     return same & (key <= query)
-
-
-def attend_back_kernel(
-    q_ref, k_ref, v_ref, grad_ref, logsum_ref, seg_col, seg_row, dq_ref, dk_ref, dv_ref, dk_sum, dv_sum
-):
-    length, width = q_ref.shape
-    dk_sum[...] = jnp.zeros_like(dk_sum)
-    dv_sum[...] = jnp.zeros_like(dv_sum)
-    scale = bf16(HEAD ** (-0.5))
-    for start in range(0, length, block):
-        rows = slice(start, start + block)
-        count = start + block
-        mask = block_mask(seg_col, seg_row, rows, count)
-        mixed = []
-        for head, (lane, lanes, upper) in enumerate(head_lanes(width // HEAD)):
-            cols = slice(lane, lane + lanes)
-            queries = own_lanes(q_ref[rows, cols], lanes, upper) * scale
-            grads = own_lanes(grad_ref[rows, cols], lanes, upper)
-            keys = k_ref[0:count, cols]
-            scores = mm_nt(keys, queries)
-            scores = jnp.where(mask, scores, masked_score)
-            probs = jnp.exp(scores - logsum_ref[head : head + 1, rows])
-            grad_probs = mm_nt(v_ref[0:count, cols], grads)
-            dv_sum[0:count, cols] += mm(probs.astype(bf16), grads)
-            term = probs * grad_probs
-            delta = jnp.sum(term, axis=0, keepdims=True)
-            grad_scores = (term - probs * delta).astype(bf16)
-            dk_sum[0:count, cols] += mm(grad_scores, queries)
-            mixed.append((lanes, mm_tn(keys, grad_scores)))
-        for pair in range(0, len(mixed), 2):
-            lane = pair * HEAD
-            lanes, result = mixed[pair]
-            if lanes > HEAD:
-                result = jnp.concatenate([result[:HEAD], mixed[pair + 1][1][HEAD:]], axis=0)
-            dq_ref[rows, lane : lane + lanes] = (result.T * HEAD ** (-0.5)).astype(bf16)
-    dk_ref[...] = dk_sum[...].astype(bf16)
-    dv_ref[...] = dv_sum[...].astype(bf16)
-
-
-def attend_back(q, k, v, grad, logsum, seg_col, seg_row):
-    length, width = q.shape
-    like = jax.ShapeDtypeStruct((length, width), bf16)
-    return pl.pallas_call(
-        attend_back_kernel,
-        out_shape=(like, like, like),
-        in_specs=[pl.BlockSpec(memory_space=pltpu.VMEM)] * 7,
-        out_specs=[pl.BlockSpec(memory_space=pltpu.VMEM)] * 3,
-        scratch_shapes=[pltpu.VMEM((length, width), f32)] * 2,
-        compiler_params=pltpu.CompilerParams(vmem_limit_bytes=40 * 2**20),
-        name="attend_back",
-    )(q, k, v, grad, logsum, seg_col, seg_row)
 
 
 MESH = pl.DeviceIdType.MESH
@@ -319,6 +268,259 @@
     )(state, w_in, w_out, w_up, w_down, b_in, b_up, vec, seg_col, seg_row)
 
 
+def attend_back_block(qkv_ref, grad_ref, mask, rows, count, logsum_ref, dqkv_ref, dk_sum, dv_sum):
+    heads = qkv_ref.shape[2] // HEAD
+    scale = bf16(HEAD ** (-0.5))
+    mixed = []
+    for head, (lane, lanes, upper) in enumerate(head_lanes(heads)):
+        cols = slice(lane, lane + lanes)
+        queries = own_lanes(qkv_ref[0, rows, cols], lanes, upper) * scale
+        grads = own_lanes(grad_ref[rows, cols], lanes, upper)
+        keys = qkv_ref[1, 0:count, cols]
+        scores = mm_nt(keys, queries)
+        scores = jnp.where(mask, scores, masked_score)
+        probs = jnp.exp(scores - logsum_ref[head : head + 1, rows])
+        grad_probs = mm_nt(qkv_ref[2, 0:count, cols], grads)
+        dv_sum[0:count, cols] += mm(probs.astype(bf16), grads)
+        term = probs * grad_probs
+        delta = jnp.sum(term, axis=0, keepdims=True)
+        grad_scores = (term - probs * delta).astype(bf16)
+        dk_sum[0:count, cols] += mm(grad_scores, queries)
+        mixed.append((lanes, mm_tn(keys, grad_scores)))
+    for pair in range(0, heads, 2):
+        lane = pair * HEAD
+        lanes, result = mixed[pair]
+        if lanes > HEAD:
+            result = jnp.concatenate([result[:HEAD], mixed[pair + 1][1][HEAD:]], axis=0)
+        dqkv_ref[0, rows, lane : lane + lanes] = (result.T * HEAD ** (-0.5)).astype(bf16)
+
+
+def backward_kernel(
+    grad_ref,
+    start_ref,
+    normed_ref,
+    qkv_ref,
+    logsum_ref,
+    att_ref,
+    middle_ref,
+    upper_ref,
+    hidden_ref,
+    slope_ref,
+    w_in,
+    w_out,
+    w_up,
+    w_down,
+    vec_ref,
+    seg_col,
+    seg_row,
+    out_ref,
+    d_in,
+    d_out,
+    d_up,
+    d_down,
+    d_vec,
+    d_b_up,
+    d_b_in,
+    gz_ref,
+    dpre_ref,
+    dmiddle_ref,
+    gy_ref,
+    datt_out,
+    datt_ref,
+    dqkv_ref,
+    dk_sum,
+    dv_sum,
+    dmix_ref,
+    low,
+    got,
+    att_sems,
+    mix_sems,
+    pair_sems,
+):
+    core = lax.axis_index("section")
+    z = lax.axis_index("mp")
+    dp = lax.axis_index("dp")
+    sibling = (1 - core, z, dp)
+    partner = (core, z + 1 - 2 * lax.rem(z, 2), dp)
+    barrier = pltpu.get_barrier_semaphore()
+    for device in (sibling, partner):
+        pl.semaphore_signal(barrier, inc=1, device_id=device, device_id_type=MESH)
+    pl.semaphore_wait(barrier, 2)
+
+    half = grad_ref.shape[0]
+    blocks = half // block
+    first = pl.multiple_of(core * half, half)
+    order = list(range(blocks))[::-1]
+
+    def pair_copy(index, rows):
+        return send(low.at[index, rows], got.at[index, rows], pair_sems, index * blocks + rows.start // block, partner)
+
+    def send_low(index, rows, value):
+        low[index, rows, :] = value.astype(bf16)
+        pair_copy(index, rows).start()
+
+    def received(index, rows):
+        pair_copy(index, rows).wait()
+        return low[index, rows, :].astype(f32) + got[index, rows, :].astype(f32)
+
+    def own_rows(j):
+        return slice(j * block, (j + 1) * block)
+
+    def total(value):
+        return jnp.sum(value, axis=0, keepdims=True)
+
+    d_vec[...] = jnp.zeros_like(d_vec)
+    dk_sum[...] = jnp.zeros_like(dk_sum)
+    dv_sum[...] = jnp.zeros_like(dv_sum)
+
+    for j in order:
+        rows = own_rows(j)
+        gz = branch_scale * grad_ref[rows, :].astype(f32)
+        d_vec[5:6, :] += total(gz)
+        gz = gz.astype(bf16)
+        gz_ref[rows, :] = gz
+        part = None
+        for k in range(2):
+            dpre = (mm_nt(gz, w_down[k]) * slope_ref[k, rows, :].astype(f32)).astype(bf16)
+            dpre_ref[k, rows, :] = dpre
+            term = mm_nt(dpre, w_up[k])
+            part = term if part is None else part + term
+        send_low(0, rows, part)
+    for k in range(2):
+        d_down[k] = mm_tn(hidden_ref[k], gz_ref[...]).astype(bf16)
+        d_up[k] = mm_tn(upper_ref[...], dpre_ref[k]).astype(bf16)
+        d_b_up[k] = total(dpre_ref[k].astype(f32))
+
+    def datt_copy(j):
+        there = pl.ds(pl.multiple_of(first + j * block, block), block)
+        return send(datt_out.at[j], datt_ref.at[there, :], att_sems, j, sibling)
+
+    for j in order:
+        rows = own_rows(j)
+        d_upper = received(0, rows)
+        normal, rstd = normalize(middle_ref[rows, :])
+        d_vec[1:2, :] += total(d_upper * normal)
+        d_vec[3:4, :] += total(d_upper)
+        d_middle = grad_ref[rows, :].astype(f32) + norm_back(normal, rstd, d_upper, vec_ref[1:2, :])
+        dmiddle_ref[rows, :] = d_middle
+        gy = branch_scale * d_middle
+        d_vec[4:5, :] += total(gy)
+        gy = gy.astype(bf16)
+        gy_ref[rows, :] = gy
+        datt_out[j] = mm_nt(gy, w_out[1 - core]).astype(bf16)
+        datt_copy(j).start()
+        there = pl.ds(pl.multiple_of(first + j * block, block), block)
+        datt_ref[there, :] = mm_nt(gy, w_out[core]).astype(bf16)
+
+    def mix_copy(j):
+        return send(
+            dqkv_ref.at[:, pl.ds(pl.multiple_of(half - first + j * block, block), block), :],
+            dmix_ref.at[core, :, pl.ds(j * block, block), :],
+            mix_sems,
+            j,
+            sibling,
+        )
+
+    def finish(i):
+        owner, j = i // blocks, i % blocks
+        rows = slice(i * block, (i + 1) * block)
+        dqkv_ref[1, rows, :] = dk_sum[rows, :].astype(bf16)
+        dqkv_ref[2, rows, :] = dv_sum[rows, :].astype(bf16)
+
+        @pl.when(core == owner)
+        def _():
+            dmix_ref[core, :, own_rows(j), :] = dqkv_ref[:, rows, :]
+
+        @pl.when(core != owner)
+        def _():
+            mix_copy(j).start()
+
+    left = list(range(2 * blocks))
+    for j in order:
+        datt_copy(j).wait()
+        for i in (blocks + j, j):
+            rows = slice(i * block, (i + 1) * block)
+            count = (i + 1) * block
+            mask = block_mask(seg_col, seg_row, rows, count)
+            attend_back_block(qkv_ref, datt_ref, mask, rows, count, logsum_ref, dqkv_ref, dk_sum, dv_sum)
+            left.remove(i)
+            if j == 0:
+                for done in [n for n in range(2 * blocks) if n > max(left, default=-1) and n // blocks == i // blocks][::-1]:
+                    finish(done)
+    for k in range(2):
+        d_out[k] = mm_tn(att_ref[k], gy_ref[...]).astype(bf16)
+
+    for j in order:
+        rows = own_rows(j)
+        mix_copy(j).wait_recv()
+        part = None
+        for k in range(2):
+            for p in range(3):
+                term = mm_nt(dmix_ref[k, p, rows, :], w_in[k, p])
+                part = term if part is None else part + term
+        send_low(1, rows, part)
+    for k in range(2):
+        for p in range(3):
+            d_in[k, p] = mm_tn(normed_ref[...], dmix_ref[k, p]).astype(bf16)
+            d_b_in[k, p : p + 1, :] = total(dmix_ref[k, p].astype(f32))
+    for j in order:
+        rows = own_rows(j)
+        d_normed = received(1, rows)
+        normal, rstd = normalize(start_ref[rows, :].astype(f32))
+        d_vec[0:1, :] += total(d_normed * normal)
+        d_vec[2:3, :] += total(d_normed)
+        d_state = dmiddle_ref[rows, :] + norm_back(normal, rstd, d_normed, vec_ref[0:1, :])
+        out_ref[rows, :] = d_state.astype(bf16)
+    for j in order:
+        mix_copy(j).wait_send()
+
+
+def backward_layer(grad, kept, w_in, w_out, w_up, w_down, vec, seg_col, seg_row):
+    half, width = grad.shape
+    length = seg_col.shape[0]
+    local = w_in.shape[3]
+    units = w_up.shape[2]
+    blocks = half // block
+    vmem = pl.BlockSpec(memory_space=pltpu.VMEM)
+    shape = jax.ShapeDtypeStruct
+    return pl.pallas_call(
+        backward_kernel,
+        out_shape=(
+            shape((half, width), bf16),
+            shape(w_in.shape, bf16),
+            shape(w_out.shape, bf16),
+            shape(w_up.shape, bf16),
+            shape(w_down.shape, bf16),
+            shape((8, width), f32),
+            shape((2, 1, units), f32),
+            shape((2, 3, local), f32),
+        ),
+        in_specs=[vmem] * 17,
+        out_specs=[vmem] * 8,
+        scratch_shapes=[
+            pltpu.VMEM((half, width), bf16),
+            pltpu.VMEM((2, half, units), bf16),
+            pltpu.VMEM((half, width), f32),
+            pltpu.VMEM((half, width), bf16),
+            pltpu.VMEM((blocks, block, local), bf16),
+            pltpu.VMEM((length, local), bf16),
+            pltpu.VMEM((3, length, local), bf16),
+            pltpu.VMEM((length, local), f32),
+            pltpu.VMEM((length, local), f32),
+            pltpu.VMEM((2, 3, half, local), bf16),
+            pltpu.VMEM((2, half, width), bf16),
+            pltpu.VMEM((2, half, width), bf16),
+            pltpu.SemaphoreType.DMA((2, blocks)),
+            pltpu.SemaphoreType.DMA((2, blocks)),
+            pltpu.SemaphoreType.DMA((2, 2 * blocks)),
+        ],
+        compiler_params=pltpu.CompilerParams(
+            vmem_limit_bytes=56 * 2**20, collective_id=2, has_side_effects=True
+        ),
+        name="backward_layer",
+    )(grad, *kept, w_in, w_out, w_up, w_down, vec, seg_col, seg_row)
+
+
 def segment_ids(lengths, length):
     ends = jnp.cumsum(lengths)
     positions = jnp.arange(length, dtype=jnp.int32)
@@ -447,7 +649,7 @@
         return low.astype(f32) + route(low, swap_side).astype(f32)
 
     state = rows_in(inputs)
-    grad = rows_in(cotangent).astype(f32)
+    grad = rows_in(cotangent)
     saved = []
     outputs = []
     for layer in range(2):
@@ -460,63 +662,23 @@
         state, *kept = forward_layer(
             state, w_in[layer], w_out[layer], w_up[layer], w_down[layer], b_in, b_up, vec, seg_col, seg_row
         )
-        saved.append((start, *kept))
+        saved.append(((start, *kept), vec))
         outputs.append(state)
 
     partials = [None, None]
     vectors = [None, None]
     grads_out = [None, None]
     for layer in (1, 0):
-        start, normed, qkv, logsum, attended, middle, upper, hidden, slope = saved[layer]
-        q, k, v = qkv[0], qkv[1], qkv[2]
-        start = start.astype(f32)
-        bias_own, up_b_own, bias_far, up_b_far, gains, shifts, branch = unpack(vecs[layer])
-        gz = branch_scale * grad
-        d_branch1 = jnp.sum(gz, axis=0)
-        gz = gz.astype(bf16)
-        d_pre, d_up, d_down, d_up_bias = [], [], [], []
-        for i, w in enumerate(w_down[layer]):
-            dp_ = (mm_nt(gz, w) * slope[i].astype(f32)).astype(bf16)
-            d_pre.append(dp_)
-            d_down.append(mm_tn(hidden[i], gz).astype(bf16))
-            d_up.append(mm_tn(upper, dp_).astype(bf16))
-            d_up_bias.append(jnp.sum(dp_.astype(f32), axis=0))
-        part = mm_nt(d_pre[0], w_up[layer][0]) + mm_nt(d_pre[1], w_up[layer][1])
-        d_upper = pair_sum(part)
-        normal2, rstd2 = normalize(middle)
-        d_gain1 = jnp.sum(d_upper * normal2, axis=0)
-        d_shift1 = jnp.sum(d_upper, axis=0)
-        d_middle = grad + norm_back(normal2, rstd2, d_upper, gains[1])
-        gy = branch_scale * d_middle
-        d_branch0 = jnp.sum(gy, axis=0)
-        gy = gy.astype(bf16)
-        d_out = [mm_tn(attended[i], gy).astype(bf16) for i in range(2)]
-        d_att = jnp.stack(
-            [mm_nt(gy, w).astype(bf16) for w in w_out[layer]]
+        kept, vec = saved[layer]
+        grad, d_in, d_out, d_up, d_down, d_vec, d_b_up, d_b_in = backward_layer(
+            grad, kept, w_in[layer], w_out[layer], w_up[layer], w_down[layer], vec, seg_col, seg_row
         )
-        d_heads = to_heads(d_att)
-        dq, dk, dv = attend_back(q, k, v, d_heads, logsum, seg_col, seg_row)
-        d_mix = to_tokens(jnp.concatenate([dq, dk, dv], axis=1))
-        d_in = [jnp.stack([mm_tn(normed, d_mix[i][:, j * local : (j + 1) * local]).astype(bf16) for j in range(3)]) for i in range(2)]
-        d_mix_sum = jnp.sum(d_mix.astype(f32), axis=1)
-        part = sum(mm_nt(d_mix[i][:, j * local : (j + 1) * local], w_in[layer][i, j]) for i in range(2) for j in range(3))
-        d_normed = pair_sum(part)
-        normal, rstd = normalize(start)
-        d_gain0 = jnp.sum(d_normed * normal, axis=0)
-        d_shift0 = jnp.sum(d_normed, axis=0)
-        d_state = d_middle + norm_back(normal, rstd, d_normed, gains[0])
-        low = d_state.astype(bf16)
-        grads_out[layer] = low
-        grad = low.astype(f32)
+        grads_out[layer] = grad
         partials[layer] = (d_in, d_out, d_up, d_down)
         shard_terms = [
-            jnp.concatenate([d_mix_sum[i, :local], d_mix_sum[i, 2 * local :], d_up_bias[i]])
-            for i in range(2)
+            jnp.concatenate([d_b_in[i, 0], d_b_in[i, 2], d_b_up[i, 0]]) for i in range(2)
         ]
-        vectors[layer] = (
-            shard_terms,
-            jnp.concatenate([d_gain0, d_gain1, d_shift0, d_shift1, d_branch0, d_branch1]),
-        )
+        vectors[layer] = (shard_terms, d_vec[:6].reshape(-1))
 
     def reduce_layer(index, layer):
         own, far = partials[layer][index]

time: 684 us -> 675 us (0.987)
  Pallas kernels: 108 us -> 218 us
  matrix products: 70 us -> 0 us
  other arithmetic: 117 us -> 80.2 us
  starting transfers between devices: 65.9 us -> 53.6 us
  waiting for transfers between devices: 128 us -> 139 us
  local copies, waits for them, and re-layouts: 51 us -> 40.9 us
    pallas_call x2, Pallas kernels: 14.6 us -> 126 us  [backward_layer(): pl.pallas_call(backward_kernel, out_shape=(shape((half, width), bf16), sh...]
    dot_general x48 -> x0, matrix products: 70 us -> none  [the longest x24 37.1 us: mm_nt(): lax.dot_general(left, right, (((1,), (1,)), ((), ())), preferred_element_...]
    reduce_sum x17 -> x0, other arithmetic: 30.3 us -> none  [the longest x2 5.75 us: per_device(): d_branch0 = jnp.sum(gy, axis=0)]
    ppermute x51 -> x43, waiting for transfers between devices: 112 us -> 82.4 us  [route(): return lax.ppermute(value, ('section', 'mp'), pairs)]
    reduce_scatter x8, waiting for transfers between devices: 0.09 us -> 27.5 us  [reduce_layer(): lax.psum_scatter(total, 'dp', scatter_dimension=total.ndim - 2, tiled=True)]
    all_gather x2, waiting for transfers between devices: 15.5 us -> 29.3 us  [per_device(): lax.all_gather(pick(core == 0, first, second), 'dp', axis=first.ndim - 2,...]
    ppermute x51 -> x43, starting transfers between devices: 64.9 us -> 52.7 us  [route(): return lax.ppermute(value, ('section', 'mp'), pairs)]
    select_n x19 -> x25, other arithmetic: 12 us -> 23.9 us  [pick(): return jnp.where(flag, yes, no)]
  transfers between devices with their start and end apart: 63 -> 55, of which waited for: 15 -> 13; matrix products, arithmetic and copies ran while one was open for 32% -> 15% of each run, Pallas kernels for 16% -> 9%
where the time goes in v3:
time: 675 us; the launch traced here: 664 us
  Pallas kernels  218 us (32%)
  waiting for transfers between devices  139 us (21%)
  blocking collectives  116 us (17%)
  other arithmetic  80.2 us (12%)
  starting transfers between devices  53.6 us (8%)
  local copies, waits for them, and re-layouts  40.9 us (6%)
  between operations  15.8 us (2%)
    pallas_call x2, Pallas kernels, backward_layer(): pl.pallas_call(backward_kernel, out_shape=(shape((half, width), bf16), sh...  126 us
    pallas_call x2, Pallas kernels, forward_layer(): pl.pallas_call(forward_kernel, out_shape=(shape((half, width), bf16), sha...  92.7 us
    ppermute x43, waiting for transfers between devices, route(): return lax.ppermute(value, ('section', 'mp'), pairs)  82.4 us
    ppermute x43, starting transfers between devices, route(): return lax.ppermute(value, ('section', 'mp'), pairs)  52.7 us
    psum x1, blocking collectives, per_device(): whole_sum = lax.psum(jnp.stack(whole_sum), ('section', 'mp', 'dp')) * 0.5  39.9 us
    all_gather x2, blocking collectives, fetch(): return lax.all_gather(piece, 'dp', axis=axis, tiled=True)  31.8 us
    all_gather x2, waiting for transfers between devices, per_device(): lax.all_gather(pick(core == 0, first, second), 'dp', axis=first.ndim - 2,...  29.3 us
    all_gather x2, blocking collectives, per_device(): lax.all_gather(pick(core == 0, first, second), 'dp', axis=first.ndim - 2,...  27.6 us
  transfers between devices with their start and end apart: 55, of which 13 were waited for; matrix products, arithmetic and copies ran while one was open for 15% of the time, Pallas kernels for 9%

profile of v3, /device:TPU:0, one launch (start us, length us, event | category | flops | bytes accessed | tf_op | source)
XLA Modules:
  0.0 664.4 jit_solution(3114819398291243370)
XLA Ops:
  8.7 4.1 collective-permute-start.14
  16.1 2.9 collective-permute-start.12
  21.5 2.9 collective-permute-start.3
  26.2 2.3 copy.82
  29.2 24.2 %collective-permute-done.9 = bf16[192,768]{1,0:T(8,128)(2,1)S(1)} collective-permute-done((bf16[192,768]{1,0:T(8,128)(2,1)S(1)}, bf16[192,768]{1,0:T(8,128)(2,1)S(1)}, u32[]{:S(2)}, u32[]{:S(2)}) %collective-permute-start.9) | collective-permute-done | bytes 294944 | tf_op jit(solution)/shard_map/ppermute | solution.py:564
  55.4 2.1 collective-permute-start
  57.5 10.8 %all_gather.25 = bf16[192,768]{1,0:T(8,128)(2,1)S(1)} all-gather(bf16[48,768]{1,0:T(8,128)(2,1)} %collective-permute-done.6), channel_id=1, replica_groups=mesh['section'=2,'mp'=4,'dp'=4] {'dp'}, dimensions={0}, use_global_device_ids=true | all-gather | bytes 368640 | tf_op jit(solution)/shard_map/all_gather | solution.py:588
  68.9 21.0 %all_gather.24 = bf16[3,768,192]{2,1,0:T(8,128)(2,1)S(1)} all-gather(bf16[3,192,192]{2,1,0:T(8,128)(2,1)} %copy-done.45), channel_id=1, replica_groups=mesh['section'=2,'mp'=4,'dp'=4] {'dp'}, dimensions={1}, use_global_device_ids=true | all-gather | bytes 1105920 | tf_op jit(solution)/shard_map/all_gather | solution.py:588
  97.4 9.6 %collective-permute-done.19 = bf16[256,768]{1,0:T(8,128)(2,1)S(1)} collective-permute-done((bf16[256,768]{1,0:T(8,128)(2,1)S(1)}, bf16[256,768]{1,0:T(8,128)(2,1)S(1)}, u32[]{:S(2)}, u32[]{:S(2)}) %collective-permute-start.19) | collective-permute-done | bytes 393248 | tf_op jit(solution)/shard_map/ppermute | solution.py:564
  108.2 6.9 %collective-permute-done.1 = bf16[256,768]{1,0:T(8,128)(2,1)S(1)} collective-permute-done((bf16[256,768]{1,0:T(8,128)(2,1)S(1)}, bf16[256,768]{1,0:T(8,128)(2,1)S(1)}, u32[]{:S(2)}, u32[]{:S(2)}) %collective-permute-start.1) | collective-permute-done | bytes 393248 | tf_op jit(solution)/shard_map/ppermute | solution.py:564
  116.3 2.3 copy.84
  118.7 3.2 fusion.6
  121.9 2.3 copy.87
  124.2 2.7 select_bitcast_fusion.10
  129.2 3.2 pad_maximum_fusion.w_in
  137.6 2.4 pad_maximum_fusion.4
  140.0 2.4 pad_maximum_fusion.1
  142.4 43.7 %forward_layer.2 = (bf16[512,768]{1,0:T(8,128)(2,1)S(1)}, bf16[512,768]{1,0:T(8,128)(2,1)S(1)}, bf16[3,1024,192]{2,1,0:T(8,128)(2,1)}, f32[3,1024]{1,0:T(4,128)S...) custom-call(bf16[512,768]{1,0:T(8,128)(2,1)} %maximum_select_fusion., ...), custom_call_target="tpu_custom_call" | custom-call | tf_op jit(solution)/shard_map/forward_layer/pallas_call | solution.py:240
  190.2 49.0 %forward_layer.3 = (bf16[512,768]{1,0:T(8,128)(2,1)S(1)}, bf16[512,768]{1,0:T(8,128)(2,1)S(1)}, bf16[3,1024,192]{2,1,0:T(8,128)(2,1)}, f32[3,1024]{1,0:T(4,128)S...) custom-call(bf16[512,768]{1,0:T(8,128)(2,1)} %copy-done.1, ...), custom_call_target="tpu_custom_call" | custom-call | tf_op jit(solution)/shard_map/forward_layer/pallas_call | solution.py:240
  242.4 64.6 %backward_layer.2 = (bf16[512,768]{1,0:T(8,128)(2,1)}, bf16[2,3,768,192]{3,2,1,0:T(8,128)(2,1)}, bf16[2,192,768]{2,1,0:T(8,128)(2,1)}, bf16[2,768,768]{2,1,0:T(8...) custom-call(bf16[512,768]{1,0:T(8,128)(2,1)} %maximum_select_fusion.3, ...), custom_call_target="tpu_custom_call" | custom-call | tf_op jit(solution)/shard_map/backward_layer/pallas_call | solution.py:486
  309.0 2.8 collective-permute-done.40
  313.8 61.0 %backward_layer.3 = (bf16[512,768]{1,0:T(8,128)(2,1)}, bf16[2,3,768,192]{3,2,1,0:T(8,128)(2,1)}, bf16[2,192,768]{2,1,0:T(8,128)(2,1)}, bf16[2,768,768]{2,1,0:T(8...) custom-call(bf16[512,768]{1,0:T(8,128)(2,1)} %get-tuple-element.55.gr, ...), custom_call_target="tpu_custom_call" | custom-call | tf_op jit(solution)/shard_map/backward_layer/pallas_call | solution.py:486
  376.8 2.8 collective-permute-done.38
  382.1 2.7 collective-permute-done.35
  393.0 3.6 fusion.3
  399.0 2.3 copy.103
  402.3 2.8 select_bitcast_fusion.5
  405.1 2.3 copy.101
  407.4 2.3 copy.104
  409.7 2.7 fusion.4
  412.6 39.9 %psum.14 = f32[2,4608]{1,0:T(2,128)S(1)} all-reduce(f32[2,4608]{1,0:T(2,128)S(1)} %pad_maximum_fusion.8), channel_id=1, replica_groups=mesh['section'=2,'mp'=4,'dp'=4] {'section','mp','dp'}, use_global_device_ids=true, to_apply=%region_2.3 | all-reduce | flops 9216 | bytes 73728 | tf_op jit(solution)/shard_map/psum | solution.py:707
  452.5 2.1 fusion.31
  455.7 2.3 copy.102
  458.0 2.7 fusion.5
  469.1 25.8 %collective-permute-done.41 = bf16[192,768]{1,0:T(8,128)(2,1)} collective-permute-done((bf16[192,768]{1,0:T(8,128)(2,1)}, bf16[192,768]{1,0:T(8,128)(2,1)}, u32[]{:S(2)}, u32[]{:S(2)}) %collective-permute-start.41) | collective-permute-done | bytes 294944 | tf_op jit(solution)/shard_map/ppermute | solution.py:564
  497.3 16.9 %psum.15 = f32[2,1152]{1,0:T(2,128)S(1)} all-reduce(f32[2,1152]{1,0:T(2,128)S(1)} %fusion.20), channel_id=1, replica_groups=mesh['section'=2,'mp'=4,'dp'=4] {'section','dp'}, use_global_device_ids=true, to_apply=%region_5.6 | all-reduce | flops 2304 | bytes 18432 | tf_op jit(solution)/shard_map/psum | solution.py:706
  522.2 4.0 collective-permute-start.17
  527.5 2.2 maximum_select_fusion.1
  538.3 6.3 collective-permute-start.37
  545.6 2.2 collective-permute-start.21
  548.6 10.9 %all_gather.29 = bf16[192,768]{1,0:T(8,128)(2,1)S(1)} all-gather(bf16[48,768]{1,0:T(8,128)(2,1)S(1)} %add_select_fusion.3), channel_id=1, replica_groups=mesh['section'=2,'mp'=4,'dp'=4] {'dp'}, dimensions={0}, use_global_device_ids=true | all-gather | bytes 368640 | tf_op jit(solution)/shard_map/all_gather | solution.py:696
  563.9 27.4 %reduce-scatter.9.cloned.1.call-done = bf16[3,192,192]{2,1,0:T(8,128)(2,1)} async-done(((bf16[3,768,192]{2,1,0:T(8,128)(2,1)}), bf16[3,192,192]{2,1,0:T(8,128)(2,1)}) %reduce-scatter.9.cloned.1.call-update) | async-done | bytes 221200 | tf_op jit(solution)/shard_map/reduce_scatter | solution.py:687
  593.7 5.2 collective-permute-start.26
  599.9 3.7 collective-permute-done.23
  603.7 16.7 %all_gather.28 = bf16[3,768,192]{2,1,0:T(8,128)(2,1)S(1)} all-gather(bf16[3,192,192]{2,1,0:T(8,128)(2,1)S(1)} %add_select_fusion.2), channel_id=1, replica_groups=mesh['section'=2,'mp'=4,'dp'=4] {'dp'}, dimensions={1}, use_global_device_ids=true | all-gather | bytes 1105920 | tf_op jit(solution)/shard_map/all_gather | solution.py:696
  623.6 2.8 bitcast_convert_fusion
  626.5 28.1 %all-gather.9.cloned.1.call-done = bf16[768,768]{1,0:T(8,128)(2,1)} async-done(((bf16[192,768]{1,0:T(8,128)(2,1)}), bf16[768,768]{1,0:T(8,128)(2,1)}) %all-gather.9.cloned.1.call-update) | async-done | bytes 1179664 | tf_op jit(solution)/shard_map/all_gather | solution.py:696
  654.5 2.8 bitcast_convert_fusion.1
  (354 shorter events, 98.4 us)
Async XLA Ops:
  7.2 117.0 %all-gather.5.cloned.1.call-start = ((), (), s32[]{:S(2)}) async-start(), calls=%async_computation.8 | async-start | bytes 1474560 | tf_op jit(solution)/shard_map/all_gather | solution.py:588
  8.7 17.3 %collective-permute-start.14 = (f32[1152]{0:T(1024)S(1)}, f32[1152]{0:T(1024)S(1)}, u32[]{:S(2)}, u32[]{:S(2)}) collective-permute-start(f32[1152]{0:T(1024)S(1)} %pad_maximum_fusion.14), channel_id=1, source_target_pairs={{0,8},{4,12},{8,0},{12,4},{16,24},{20,28},{24,16},{28,20},{1,9},{5... | collective-permute-start | bytes 13832 | tf_op jit(solution)/shard_map/ppermute | solution.py:564
  14.3 41.1 %collective-permute-start.6 = (bf16[48,768]{1,0:T(8,128)(2,1)}, bf16[48,768]{1,0:T(8,128)(2,1)}, u32[]{:S(2)}, u32[]{:S(2)}) collective-permute-start(bf16[48,768]{1,0:T(8,128)(2,1)} %dynamic-slice_bitcast_fusion.2), channel_id=1, source_target_pairs={{0,8},{4,12},{8,0},{12,4},{16,24},{20,28},{24,16},{28,20},{1,9},{5... | collective-permute-start | bytes 221192 | tf_op jit(solution)/shard_map/ppermute | solution.py:564
  16.1 75.2 %collective-permute-start.12 = (bf16[192,768]{1,0:T(8,128)(2,1)}, bf16[192,768]{1,0:T(8,128)(2,1)}, u32[]{:S(2)}, u32[]{:S(2)}) collective-permute-start(bf16[192,768]{1,0:T(8,128)(2,1)} %dynamic-slice_bitcast_fusion), channel_id=1, source_target_pairs={{0,8},{4,12},{8,0},{12,4},{16,24},{20,28},{24,16},{28,20},{1,9},{5... | collective-permute-start | bytes 884744 | tf_op jit(solution)/shard_map/ppermute | solution.py:564
  20.0 33.3 %collective-permute-start.9 = (bf16[192,768]{1,0:T(8,128)(2,1)S(1)}, bf16[192,768]{1,0:T(8,128)(2,1)S(1)}, u32[]{:S(2)}, u32[]{:S(2)}) collective-permute-start(bf16[192,768]{1,0:T(8,128)(2,1)S(1)} %dynamic-slice_bitcast_fusion.1), channel_id=1, source_target_pairs={{0,8},{4,12},{8,0},{12,4},{16,24},{20,28},{24,16},{28,20},{1,9},{5... | collective-permute-start | bytes 884744 | tf_op jit(solution)/shard_map/ppermute | solution.py:564
  21.5 46.7 %collective-permute-start.3 = (bf16[3,192,192]{2,1,0:T(8,128)(2,1)S(1)}, bf16[3,192,192]{2,1,0:T(8,128)(2,1)S(1)}, u32[]{:S(2)}, u32[]{:S(2)}) collective-permute-start(bf16[3,192,192]{2,1,0:T(8,128)(2,1)S(1)} %bitcast.229), channel_id=1, source_target_pairs={{0,8},{4,12},{8,0},{12,4},{16,24},{20,28},{24,16},{28,20},{1,9},{5... | collective-permute-start | bytes 663560 | tf_op jit(solution)/shard_map/ppermute | solution.py:564
  28.6 62.8 %collective-permute-start.5 = (bf16[192,768]{1,0:T(8,128)(2,1)S(1)}, bf16[192,768]{1,0:T(8,128)(2,1)S(1)}, u32[]{:S(2)}, u32[]{:S(2)}) collective-permute-start(bf16[192,768]{1,0:T(8,128)(2,1)S(1)} %bitcast.228), channel_id=1, source_target_pairs={{0,16},{4,20},{8,24},{12,28},{16,0},{20,4},{24,8},{28,12},{1,17},{... | collective-permute-start | bytes 884744 | tf_op jit(solution)/shard_map/ppermute | solution.py:564
  53.3 40.4 %collective-permute-start.18 = (bf16[256,768]{1,0:T(8,128)(2,1)}, bf16[256,768]{1,0:T(8,128)(2,1)S(1)}, u32[]{:S(2)}, u32[]{:S(2)}) collective-permute-start(bf16[256,768]{1,0:T(8,128)(2,1)} %select_bitcast_fusion.17), channel_id=1, source_target_pairs={{0,8},{4,12},{24,16},{28,20},{1,9},{5,13},{25,17},{29,21},{2,10},{... | collective-permute-start | bytes 1179656 | tf_op jit(solution)/shard_map/ppermute | solution.py:564
  54.8 73.9 %all-gather.7.cloned.1.call-start = ((), (), s32[]{:S(2)}) async-start(), calls=%async_computation.9 | async-start | bytes 1474560 | tf_op jit(solution)/shard_map/all_gather | solution.py:588
  55.4 39.6 %collective-permute-start = (bf16[256,768]{1,0:T(8,128)(2,1)S(1)}, bf16[256,768]{1,0:T(8,128)(2,1)}, u32[]{:S(2)}, u32[]{:S(2)}) collective-permute-start(bf16[256,768]{1,0:T(8,128)(2,1)S(1)} %select_bitcast_fusion.18), channel_id=1, source_target_pairs={{0,8},{4,12},{24,16},{28,20},{1,9},{5,13},{25,17},{29,21},{2,10},{... | collective-permute-start | bytes 1179656 | tf_op jit(solution)/shard_map/ppermute | solution.py:564
  68.9 47.4 %collective-permute-start.2 = (bf16[3,768,192]{1,2,0:T(8,128)(2,1)}, bf16[3,768,192]{1,2,0:T(8,128)(2,1)}, u32[]{:S(2)}, u32[]{:S(2)}) collective-permute-start(bf16[3,768,192]{1,2,0:T(8,128)(2,1)} %bitcast.5), channel_id=1, source_target_pairs={{0,16},{4,20},{8,24},{12,28},{16,0},{20,4},{24,8},{28,12},{1,17},{... | collective-permute-start | bytes 2654216 | tf_op jit(solution)/shard_map/ppermute | solution.py:564
  91.3 41.1 %collective-permute-start.11 = (bf16[768,768]{1,0:T(8,128)(2,1)}, bf16[768,768]{1,0:T(8,128)(2,1)}, u32[]{:S(2)}, u32[]{:S(2)}) collective-permute-start(bf16[768,768]{1,0:T(8,128)(2,1)} %bitcast.226), channel_id=1, source_target_pairs={{0,16},{4,20},{8,24},{12,28},{16,0},{20,4},{24,8},{28,12},{1,17},{... | collective-permute-start | bytes 3538952 | tf_op jit(solution)/shard_map/ppermute | solution.py:564
  91.3 369.5 %reduce-scatter.23.cloned.1.call-start = ((), (), s32[]{:S(2)}) async-start(), calls=%async_computation.18 | async-start | bytes 1474560 | tf_op jit(solution)/shard_map/reduce_scatter | solution.py:687
  92.1 4.9 collective-permute-start.7
  93.7 28.2 %collective-permute-start.4 = (bf16[3,768,192]{1,2,0:T(8,128)(2,1)}, bf16[3,768,192]{1,2,0:T(8,128)(2,1)}, u32[]{:S(2)}, u32[]{:S(2)}) collective-permute-start(bf16[3,768,192]{1,2,0:T(8,128)(2,1)} %copy.86), channel_id=1, source_target_pairs={{0,16},{4,20},{8,24},{12,28},{16,0},{20,4},{24,8},{28,12},{1,17},{... | collective-permute-start | bytes 2654216 | tf_op jit(solution)/shard_map/ppermute | solution.py:564
  95.0 12.1 %collective-permute-start.19 = (bf16[256,768]{1,0:T(8,128)(2,1)S(1)}, bf16[256,768]{1,0:T(8,128)(2,1)S(1)}, u32[]{:S(2)}, u32[]{:S(2)}) collective-permute-start(bf16[256,768]{1,0:T(8,128)(2,1)S(1)} %bitcast_select_fusion.5), channel_id=1, source_target_pairs={{0,4},{4,0},{8,12},{12,8},{16,20},{20,16},{24,28},{28,24},{1,5},{5... | collective-permute-start | bytes 1179656 | tf_op jit(solution)/shard_map/ppermute | solution.py:564
  97.0 18.1 %collective-permute-start.1 = (bf16[256,768]{1,0:T(8,128)(2,1)S(1)}, bf16[256,768]{1,0:T(8,128)(2,1)S(1)}, u32[]{:S(2)}, u32[]{:S(2)}) collective-permute-start(bf16[256,768]{1,0:T(8,128)(2,1)S(1)} %bitcast_select_fusion.6), channel_id=1, source_target_pairs={{0,4},{4,0},{8,12},{12,8},{16,20},{20,16},{24,28},{28,24},{1,5},{5... | collective-permute-start | bytes 1179656 | tf_op jit(solution)/shard_map/ppermute | solution.py:564
  107.0 26.8 %collective-permute-start.8 = (bf16[768,768]{1,0:T(8,128)(2,1)}, bf16[768,768]{1,0:T(8,128)(2,1)}, u32[]{:S(2)}, u32[]{:S(2)}) collective-permute-start(bf16[768,768]{1,0:T(8,128)(2,1)} %bitcast.14), channel_id=1, source_target_pairs={{0,16},{4,20},{8,24},{12,28},{16,0},{20,4},{24,8},{28,12},{1,17},{... | collective-permute-start | bytes 3538952 | tf_op jit(solution)/shard_map/ppermute | solution.py:564
  124.2 11.6 %collective-permute-start.10 = (bf16[768,768]{1,0:T(8,128)(2,1)}, bf16[768,768]{1,0:T(8,128)(2,1)}, u32[]{:S(2)}, u32[]{:S(2)}) collective-permute-start(bf16[768,768]{1,0:T(8,128)(2,1)} %all-gather.5.cloned.1.call-done), channel_id=1, source_target_pairs={{0,16},{4,20},{8,24},{12,28},{16,0},{20,4},{24,8},{28,12},{1,17},{... | collective-permute-start | bytes 3538952 | tf_op jit(solution)/shard_map/ppermute | solution.py:564
  128.8 8.6 %collective-permute-start.13 = (bf16[768,768]{1,0:T(8,128)(2,1)}, bf16[768,768]{1,0:T(8,128)(2,1)S(1)}, u32[]{:S(2)}, u32[]{:S(2)}) collective-permute-start(bf16[768,768]{1,0:T(8,128)(2,1)} %all-gather.7.cloned.1.call-done), channel_id=1, source_target_pairs={{0,16},{4,20},{8,24},{12,28},{16,0},{20,4},{24,8},{28,12},{1,17},{... | collective-permute-start | bytes 3538952 | tf_op jit(solution)/shard_map/ppermute | solution.py:564
  313.3 154.5 %reduce-scatter.21.cloned.1.call-start = ((), (), s32[]{:S(2)}) async-start(), calls=%async_computation.17 | async-start | bytes 1474560 | tf_op jit(solution)/shard_map/reduce_scatter | solution.py:687
  381.2 138.8 %reduce-scatter.19.cloned.1.call-start = ((), (), s32[]{:S(2)}) async-start(), calls=%async_computation.15 | async-start | bytes 1474560 | tf_op jit(solution)/shard_map/reduce_scatter | solution.py:687
  386.3 139.9 %reduce-scatter.15.cloned.1.call-start = ((), (), s32[]{:S(2)}) async-start(), calls=%async_computation.13 | async-start | bytes 368640 | tf_op jit(solution)/shard_map/reduce_scatter | solution.py:687
  390.0 139.7 %reduce-scatter.13.cloned.1.call-start = ((), (), s32[]{:S(2)}) async-start(), calls=%async_computation.12 | async-start | bytes 368640 | tf_op jit(solution)/shard_map/reduce_scatter | solution.py:687
  392.9 143.0 %reduce-scatter.17.cloned.1.call-start = ((), (), s32[]{:S(2)}) async-start(), calls=%async_computation.14 | async-start | bytes 1474560 | tf_op jit(solution)/shard_map/reduce_scatter | solution.py:687
  396.7 164.5 %reduce-scatter.11.cloned.1.call-start = ((), (), s32[]{:S(2)}) async-start(), calls=%async_computation.11 | async-start | bytes 1474560 | tf_op jit(solution)/shard_map/reduce_scatter | solution.py:687
  401.3 6.1 collective-permute-start.24
  401.7 95.6 %collective-permute-start.27 = (f32[2,1152]{1,0:T(2,128)S(1)}, f32[2,1152]{1,0:T(2,128)S(1)}, u32[]{:S(2)}, u32[]{:S(2)}) collective-permute-start(f32[2,1152]{1,0:T(2,128)S(1)} %fusion.21), channel_id=1, source_target_pairs={{0,8},{4,12},{8,0},{12,4},{16,24},{20,28},{24,16},{28,20},{1,9},{5... | collective-permute-start | bytes 27656 | tf_op jit(solution)/shard_map/ppermute | solution.py:564
  407.4 48.3 %collective-permute-start.22 = (bf16[3,768,192]{1,2,0:T(8,128)(2,1)}, bf16[3,768,192]{1,2,0:T(8,128)(2,1)}, u32[]{:S(2)}, u32[]{:S(2)}) collective-permute-start(bf16[3,768,192]{1,2,0:T(8,128)(2,1)} %copy.101), channel_id=1, source_target_pairs={{0,16},{4,20},{8,24},{12,28},{16,0},{20,4},{24,8},{28,12},{1,17},{... | collective-permute-start | bytes 2654216 | tf_op jit(solution)/shard_map/ppermute | solution.py:564
  412.5 178.8 %reduce-scatter.9.cloned.1.call-start = ((), (), s32[]{:S(2)}) async-start(), calls=%async_computation.10 | async-start | bytes 1474560 | tf_op jit(solution)/shard_map/reduce_scatter | solution.py:687
  460.8 162.8 %all-gather.11.cloned.1.call-start = ((), (), s32[]{:S(2)}) async-start(), calls=%async_computation.19 | async-start | bytes 1474560 | tf_op jit(solution)/shard_map/all_gather | solution.py:696
  460.9 34.1 %collective-permute-start.41 = (bf16[192,768]{1,0:T(8,128)(2,1)}, bf16[192,768]{1,0:T(8,128)(2,1)}, u32[]{:S(2)}, u32[]{:S(2)}) collective-permute-start(bf16[192,768]{1,0:T(8,128)(2,1)} %reduce-scatter.23.cloned.1.call-done), channel_id=1, source_target_pairs={{16,8},{20,12},{24,0},{28,4},{17,9},{21,13},{25,1},{29,5},{18,10},... | collective-permute-start | bytes 884744 | tf_op jit(solution)/shard_map/ppermute | solution.py:564
  465.2 52.2 %collective-permute-start.16 = (bf16[2,256,768]{2,1,0:T(8,128)(2,1)}, bf16[2,256,768]{2,1,0:T(8,128)(2,1)S(1)}, u32[]{:S(2)}, u32[]{:S(2)}) collective-permute-start(bf16[2,256,768]{2,1,0:T(8,128)(2,1)} %fusion.10), channel_id=1, source_target_pairs={{8,0},{12,4},{16,24},{20,28},{9,1},{13,5},{17,25},{21,29},{10,2},{... | collective-permute-start | bytes 2359304 | tf_op jit(solution)/shard_map/ppermute | solution.py:564
  466.5 61.0 %collective-permute-start.20 = (bf16[2,256,768]{2,1,0:T(8,128)(2,1)S(1)}, bf16[2,256,768]{2,1,0:T(8,128)(2,1)}, u32[]{:S(2)}, u32[]{:S(2)}) collective-permute-start(bf16[2,256,768]{2,1,0:T(8,128)(2,1)S(1)} %copy-done.36), channel_id=1, source_target_pairs={{8,0},{12,4},{16,24},{20,28},{9,1},{13,5},{17,25},{21,29},{10,2},{... | collective-permute-start | bytes 2359304 | tf_op jit(solution)/shard_map/ppermute | solution.py:564
  467.8 46.4 %collective-permute-start.39 = (bf16[192,768]{1,0:T(8,128)(2,1)}, bf16[192,768]{1,0:T(8,128)(2,1)S(1)}, u32[]{:S(2)}, u32[]{:S(2)}) collective-permute-start(bf16[192,768]{1,0:T(8,128)(2,1)} %reduce-scatter.21.cloned.1.call-done), channel_id=1, source_target_pairs={{16,8},{20,12},{24,0},{28,4},{17,9},{21,13},{25,1},{29,5},{18,10},... | collective-permute-start | bytes 884744 | tf_op jit(solution)/shard_map/ppermute | solution.py:564
  496.0 18.3 %collective-permute-start.42 = (bf16[192,768]{1,0:T(8,128)(2,1)S(1)}, bf16[192,768]{1,0:T(8,128)(2,1)S(1)}, u32[]{:S(2)}, u32[]{:S(2)}) collective-permute-start(bf16[192,768]{1,0:T(8,128)(2,1)S(1)} %add.129), channel_id=1, source_target_pairs={{0,16},{4,20},{8,24},{12,28},{1,17},{5,21},{9,25},{13,29},{2,18},{... | collective-permute-start | bytes 884744 | tf_op jit(solution)/shard_map/ppermute | solution.py:564
  516.0 138.5 %all-gather.9.cloned.1.call-start = ((), (), s32[]{:S(2)}) async-start(), calls=%async_computation.16 | async-start | bytes 1474560 | tf_op jit(solution)/shard_map/all_gather | solution.py:696
  520.0 17.3 %collective-permute-start.36 = (bf16[192,768]{1,0:T(8,128)(2,1)}, bf16[192,768]{1,0:T(8,128)(2,1)}, u32[]{:S(2)}, u32[]{:S(2)}) collective-permute-start(bf16[192,768]{1,0:T(8,128)(2,1)} %reduce-scatter.19.cloned.1.call-done), channel_id=1, source_target_pairs={{16,8},{20,12},{24,0},{28,4},{17,9},{21,13},{25,1},{29,5},{18,10},... | collective-permute-start | bytes 884744 | tf_op jit(solution)/shard_map/ppermute | solution.py:564
  522.2 76.7 %collective-permute-start.17 = (bf16[2,256,768]{2,1,0:T(8,128)(2,1)}, bf16[2,256,768]{2,1,0:T(8,128)(2,1)}, u32[]{:S(2)}, u32[]{:S(2)}) collective-permute-start(bf16[2,256,768]{2,1,0:T(8,128)(2,1)} %select_bitcast_fusion.16), channel_id=1, source_target_pairs={{0,16},{4,20},{24,8},{28,12},{1,17},{5,21},{25,9},{29,13},{2,18},{... | collective-permute-start | bytes 2359304 | tf_op jit(solution)/shard_map/ppermute | solution.py:564
  526.2 6.9 %collective-permute-start.31 = (bf16[48,768]{1,0:T(8,128)(2,1)}, bf16[48,768]{1,0:T(8,128)(2,1)}, u32[]{:S(2)}, u32[]{:S(2)}) collective-permute-start(bf16[48,768]{1,0:T(8,128)(2,1)} %reduce-scatter.15.cloned.1.call-done), channel_id=1, source_target_pairs={{16,8},{20,12},{24,0},{28,4},{17,9},{21,13},{25,1},{29,5},{18,10},... | collective-permute-start | bytes 221192 | tf_op jit(solution)/shard_map/ppermute | solution.py:564
  529.7 15.8 %collective-permute-start.29 = (bf16[48,768]{1,0:T(8,128)(2,1)}, bf16[48,768]{1,0:T(8,128)(2,1)}, u32[]{:S(2)}, u32[]{:S(2)}) collective-permute-start(bf16[48,768]{1,0:T(8,128)(2,1)} %reduce-scatter.13.cloned.1.call-done), channel_id=1, source_target_pairs={{16,8},{20,12},{24,0},{28,4},{17,9},{21,13},{25,1},{29,5},{18,10},... | collective-permute-start | bytes 221192 | tf_op jit(solution)/shard_map/ppermute | solution.py:564
  534.6 13.1 %collective-permute-start.32 = (bf16[48,768]{1,0:T(8,128)(2,1)}, bf16[48,768]{1,0:T(8,128)(2,1)S(1)}, u32[]{:S(2)}, u32[]{:S(2)}) collective-permute-start(bf16[48,768]{1,0:T(8,128)(2,1)} %add.121), channel_id=1, source_target_pairs={{0,16},{4,20},{8,24},{12,28},{1,17},{5,21},{9,25},{13,29},{2,18},{... | collective-permute-start | bytes 221192 | tf_op jit(solution)/shard_map/ppermute | solution.py:564
  535.9 23.6 %collective-permute-start.34 = (bf16[192,768]{1,0:T(8,128)(2,1)}, bf16[192,768]{1,0:T(8,128)(2,1)S(1)}, u32[]{:S(2)}, u32[]{:S(2)}) collective-permute-start(bf16[192,768]{1,0:T(8,128)(2,1)} %reduce-scatter.17.cloned.1.call-done), channel_id=1, source_target_pairs={{16,8},{20,12},{24,0},{28,4},{17,9},{21,13},{25,1},{29,5},{18,10},... | collective-permute-start | bytes 884744 | tf_op jit(solution)/shard_map/ppermute | solution.py:564
  538.3 21.2 %collective-permute-start.37 = (bf16[192,768]{1,0:T(8,128)(2,1)S(1)}, bf16[192,768]{1,0:T(8,128)(2,1)S(1)}, u32[]{:S(2)}, u32[]{:S(2)}) collective-permute-start(bf16[192,768]{1,0:T(8,128)(2,1)S(1)} %add.125), channel_id=1, source_target_pairs={{0,16},{4,20},{8,24},{12,28},{1,17},{5,21},{9,25},{13,29},{2,18},{... | collective-permute-start | bytes 884744 | tf_op jit(solution)/shard_map/ppermute | solution.py:564
  545.6 17.1 %collective-permute-start.21 = (bf16[2,256,768]{2,1,0:T(8,128)(2,1)}, bf16[2,256,768]{2,1,0:T(8,128)(2,1)}, u32[]{:S(2)}, u32[]{:S(2)}) collective-permute-start(bf16[2,256,768]{2,1,0:T(8,128)(2,1)} %fusion.8), channel_id=1, source_target_pairs={{0,16},{4,20},{24,8},{28,12},{1,17},{5,21},{25,9},{29,13},{2,18},{... | collective-permute-start | bytes 2359304 | tf_op jit(solution)/shard_map/ppermute | solution.py:564
  561.2 31.4 %collective-permute-start.25 = (bf16[3,192,192]{2,1,0:T(8,128)(2,1)}, bf16[3,192,192]{2,1,0:T(8,128)(2,1)}, u32[]{:S(2)}, u32[]{:S(2)}) collective-permute-start(bf16[3,192,192]{2,1,0:T(8,128)(2,1)} %reduce-scatter.11.cloned.1.call-done), channel_id=1, source_target_pairs={{16,8},{20,12},{24,0},{28,4},{17,9},{21,13},{25,1},{29,5},{18,10},... | collective-permute-start | bytes 663560 | tf_op jit(solution)/shard_map/ppermute | solution.py:564
  591.3 12.3 %collective-permute-start.23 = (bf16[3,192,192]{2,1,0:T(8,128)(2,1)}, bf16[3,192,192]{2,1,0:T(8,128)(2,1)S(1)}, u32[]{:S(2)}, u32[]{:S(2)}) collective-permute-start(bf16[3,192,192]{2,1,0:T(8,128)(2,1)} %reduce-scatter.9.cloned.1.call-done), channel_id=1, source_target_pairs={{16,8},{20,12},{24,0},{28,4},{17,9},{21,13},{25,1},{29,5},{18,10},... | collective-permute-start | bytes 663560 | tf_op jit(solution)/shard_map/ppermute | solution.py:564
  593.7 9.9 %collective-permute-start.26 = (bf16[3,192,192]{2,1,0:T(8,128)(2,1)S(1)}, bf16[3,192,192]{2,1,0:T(8,128)(2,1)S(1)}, u32[]{:S(2)}, u32[]{:S(2)}) collective-permute-start(bf16[3,192,192]{2,1,0:T(8,128)(2,1)S(1)} %add.116), channel_id=1, source_target_pairs={{0,16},{4,20},{8,24},{12,28},{1,17},{5,21},{9,25},{13,29},{2,18},{... | collective-permute-start | bytes 663560 | tf_op jit(solution)/shard_map/ppermute | solution.py:564
  (66 other events, 975.4 us)
Sparse Core Ops, SparseCore 0:
  54.9 32.1 all-gather.4
  91.5 26.8 all-gather.6
  313.4 26.5 reduce-scatter.22
  381.3 25.9 reduce-scatter.20
  410.7 28.5 reduce-scatter.18
  442.5 24.1 reduce-scatter.14
  469.5 24.2 reduce-scatter.12
  497.2 28.5 reduce-scatter.16
  529.3 29.7 reduce-scatter.10
  562.3 28.9 reduce-scatter.8
  593.2 30.4 all-gather.10
  625.9 28.6 all-gather.8

commit v4 on v3

--- a/solution.py
+++ b/solution.py
@@ -107,12 +107,19 @@
     return found
 
 
+class Places:
+    def __init__(self, local, units, width):
+        self.qkv = [slice(part * local, (part + 1) * local) for part in range(3)]
+        self.out = slice(3 * local, 4 * local)
+        self.up = slice(4 * local, 4 * local + width)
+        self.down = slice(4 * local + width, 4 * local + width + units)
+        self.rows = 4 * local + width + units
+
+
 def forward_kernel(
+    where,
     state_ref,
-    w_in,
-    w_out,
-    w_up,
-    w_down,
+    w_ref,
     b_in,
     b_up,
     vec_ref,
@@ -156,13 +163,13 @@
         normed = (normal * vec_ref[0:1, :] + vec_ref[2:3, :]).astype(bf16)
         normed_ref[rows, :] = normed
         for part in range(3):
-            qkv_out[j, part] = (mm(normed, w_in[1 - core, part]) + b_in[1 - core, part]).astype(bf16)
+            qkv_out[j, part] = (mm_nt(normed, w_ref[1 - core, where.qkv[part], :]) + b_in[1 - core, part]).astype(bf16)
         there = pl.ds(pl.multiple_of(first + j * block, block), block)
         copy = send(qkv_out.at[j], qkv_ref.at[:, there, :], qkv_sems, j, sibling)
         copy.start()
         copies.append(copy)
         for part in range(3):
-            qkv_ref[part, there, :] = (mm(normed, w_in[core, part]) + b_in[core, part]).astype(bf16)
+            qkv_ref[part, there, :] = (mm_nt(normed, w_ref[core, where.qkv[part], :]) + b_in[core, part]).astype(bf16)
     for copy in copies:
         copy.wait()
 
@@ -190,7 +197,7 @@
             for lane, lanes, result in found:
                 att_ref[core, own, lane : lane + lanes] = result
             copy.wait_recv()
-            send_low(0, own, mm(att_ref[0, own, :], w_out[0]) + mm(att_ref[1, own, :], w_out[1]))
+            send_low(0, own, sum(mm(att_ref[k, own, :], w_ref[k, where.out, :]) for k in range(2)))
 
         @pl.when(core != owner)
         def _():
@@ -211,7 +218,7 @@
         upper_ref[rows, :] = upper
         total = None
         for k in range(2):
-            pre = mm(upper, w_up[k]) + b_up[k]
+            pre = mm(upper, w_ref[k, where.up, :]) + b_up[k]
             square = pre * pre
             curve = jnp.tanh(root * pre * (1.0 + cube * square))
             rise = 0.5 * (1.0 + curve)
@@ -219,7 +226,7 @@
             hidden_ref[k, rows, :] = hidden
             slope = rise + pre * (rise * (1.0 - curve)) * (root * (1.0 + 3.0 * cube * square))
             slope_ref[k, rows, :] = slope.astype(bf16)
-            term = mm(hidden, w_down[k])
+            term = mm(hidden, w_ref[k, where.down, :])
             total = term if total is None else total + term
         send_low(1, rows, total)
 
@@ -229,16 +236,16 @@
         out_ref[rows, :] = result.astype(bf16)
 
 
-def forward_layer(state, w_in, w_out, w_up, w_down, b_in, b_up, vec, seg_col, seg_row):
+def forward_layer(where, state, weights, b_in, b_up, vec, seg_col, seg_row):
     half, width = state.shape
     length = seg_col.shape[0]
-    local = w_in.shape[3]
-    units = w_up.shape[2]
+    local = where.qkv[0].stop
+    units = b_up.shape[2]
     blocks = half // block
     vmem = pl.BlockSpec(memory_space=pltpu.VMEM)
     shape = jax.ShapeDtypeStruct
     return pl.pallas_call(
-        forward_kernel,
+        partial(forward_kernel, where),
         out_shape=(
             shape((half, width), bf16),
             shape((half, width), bf16),
@@ -250,7 +257,7 @@
             shape((2, half, units), bf16),
             shape((2, half, units), bf16),
         ),
-        in_specs=[vmem] * 10,
+        in_specs=[vmem] * 7,
         out_specs=[vmem] * 9,
         scratch_shapes=[
             pltpu.VMEM((blocks, 3, block, local), bf16),
@@ -265,7 +272,7 @@
             vmem_limit_bytes=50 * 2**20, collective_id=1, has_side_effects=True
         ),
         name="forward_layer",
-    )(state, w_in, w_out, w_up, w_down, b_in, b_up, vec, seg_col, seg_row)
+    )(state, weights, b_in, b_up, vec, seg_col, seg_row)
 
 
 def attend_back_block(qkv_ref, grad_ref, mask, rows, count, logsum_ref, dqkv_ref, dk_sum, dv_sum):
@@ -296,6 +303,7 @@
 
 
 def backward_kernel(
+    where,
     grad_ref,
     start_ref,
     normed_ref,
@@ -306,21 +314,13 @@
     upper_ref,
     hidden_ref,
     slope_ref,
-    w_in,
-    w_out,
-    w_up,
-    w_down,
+    w_ref,
     vec_ref,
     seg_col,
     seg_row,
     out_ref,
-    d_in,
-    d_out,
-    d_up,
-    d_down,
+    d_ref,
     d_vec,
-    d_b_up,
-    d_b_in,
     gz_ref,
     dpre_ref,
     dmiddle_ref,
@@ -381,15 +381,15 @@
         gz_ref[rows, :] = gz
         part = None
         for k in range(2):
-            dpre = (mm_nt(gz, w_down[k]) * slope_ref[k, rows, :].astype(f32)).astype(bf16)
+            dpre = (mm_nt(gz, w_ref[k, where.down, :]) * slope_ref[k, rows, :].astype(f32)).astype(bf16)
             dpre_ref[k, rows, :] = dpre
-            term = mm_nt(dpre, w_up[k])
+            term = mm_nt(dpre, w_ref[k, where.up, :])
             part = term if part is None else part + term
         send_low(0, rows, part)
     for k in range(2):
-        d_down[k] = mm_tn(hidden_ref[k], gz_ref[...]).astype(bf16)
-        d_up[k] = mm_tn(upper_ref[...], dpre_ref[k]).astype(bf16)
-        d_b_up[k] = total(dpre_ref[k].astype(f32))
+        d_ref[k, where.down, :] = mm_tn(hidden_ref[k], gz_ref[...]).astype(bf16)
+        d_ref[k, where.up, :] = mm_tn(upper_ref[...], dpre_ref[k]).astype(bf16)
+        d_vec[8 + 2 * k : 9 + 2 * k, :] = total(dpre_ref[k].astype(f32))
 
     def datt_copy(j):
         there = pl.ds(pl.multiple_of(first + j * block, block), block)
@@ -407,10 +407,10 @@
         d_vec[4:5, :] += total(gy)
         gy = gy.astype(bf16)
         gy_ref[rows, :] = gy
-        datt_out[j] = mm_nt(gy, w_out[1 - core]).astype(bf16)
+        datt_out[j] = mm_nt(gy, w_ref[1 - core, where.out, :]).astype(bf16)
         datt_copy(j).start()
         there = pl.ds(pl.multiple_of(first + j * block, block), block)
-        datt_ref[there, :] = mm_nt(gy, w_out[core]).astype(bf16)
+        datt_ref[there, :] = mm_nt(gy, w_ref[core, where.out, :]).astype(bf16)
 
     def mix_copy(j):
         return send(
@@ -448,7 +448,7 @@
                 for done in [n for n in range(2 * blocks) if n > max(left, default=-1) and n // blocks == i // blocks][::-1]:
                     finish(done)
     for k in range(2):
-        d_out[k] = mm_tn(att_ref[k], gy_ref[...]).astype(bf16)
+        d_ref[k, where.out, :] = mm_tn(att_ref[k], gy_ref[...]).astype(bf16)
 
     for j in order:
         rows = own_rows(j)
@@ -456,13 +456,15 @@
         part = None
         for k in range(2):
             for p in range(3):
-                term = mm_nt(dmix_ref[k, p, rows, :], w_in[k, p])
+                term = mm(dmix_ref[k, p, rows, :], w_ref[k, where.qkv[p], :])
                 part = term if part is None else part + term
         send_low(1, rows, part)
     for k in range(2):
         for p in range(3):
-            d_in[k, p] = mm_tn(normed_ref[...], dmix_ref[k, p]).astype(bf16)
-            d_b_in[k, p : p + 1, :] = total(dmix_ref[k, p].astype(f32))
+            d_ref[k, where.qkv[p], :] = mm_tn(dmix_ref[k, p], normed_ref[...]).astype(bf16)
+        for n, p in enumerate((0, 2)):
+            local = dmix_ref.shape[3]
+            d_vec[9 + 2 * k : 10 + 2 * k, n * 2 * block : n * 2 * block + local] = total(dmix_ref[k, p].astype(f32))
     for j in order:
         rows = own_rows(j)
         d_normed = received(1, rows)
@@ -475,28 +477,23 @@
         mix_copy(j).wait_send()
 
 
-def backward_layer(grad, kept, w_in, w_out, w_up, w_down, vec, seg_col, seg_row):
+def backward_layer(where, grad, kept, weights, vec, seg_col, seg_row):
     half, width = grad.shape
     length = seg_col.shape[0]
-    local = w_in.shape[3]
-    units = w_up.shape[2]
+    local = where.qkv[0].stop
+    units = kept[7].shape[2]
     blocks = half // block
     vmem = pl.BlockSpec(memory_space=pltpu.VMEM)
     shape = jax.ShapeDtypeStruct
     return pl.pallas_call(
-        backward_kernel,
+        partial(backward_kernel, where),
         out_shape=(
             shape((half, width), bf16),
-            shape(w_in.shape, bf16),
-            shape(w_out.shape, bf16),
-            shape(w_up.shape, bf16),
-            shape(w_down.shape, bf16),
-            shape((8, width), f32),
-            shape((2, 1, units), f32),
-            shape((2, 3, local), f32),
+            shape(weights.shape, bf16),
+            shape((16, width), f32),
         ),
-        in_specs=[vmem] * 17,
-        out_specs=[vmem] * 8,
+        in_specs=[vmem] * 14,
+        out_specs=[vmem] * 3,
         scratch_shapes=[
             pltpu.VMEM((half, width), bf16),
             pltpu.VMEM((2, half, units), bf16),
@@ -518,7 +515,328 @@
             vmem_limit_bytes=56 * 2**20, collective_id=2, has_side_effects=True
         ),
         name="backward_layer",
-    )(grad, *kept, w_in, w_out, w_up, w_down, vec, seg_col, seg_row)
+    )(grad, *kept, weights, vec, seg_col, seg_row)
+
+
+def others(dp, copies):
+    return [dp + 1 - 2 * lax.rem(dp, 2), dp + 2 - 4 * lax.rem(dp // 2, 2)]
+
+
+def more_bits(copies):
+    return [1 << n for n in range(2, copies.bit_length()) if (1 << n) < copies]
+
+
+def flipped(dp, bit):
+    return dp + bit - 2 * bit * lax.rem(dp // bit, 2)
+
+
+class GradSum:
+    kinds = 10
+
+    def __init__(self, layer, part, twin, first, second, cross, groups, final, sems, pieces, copies):
+        self.layer, self.part, self.twin, self.first, self.second = layer, part, twin, first, second
+        self.cross, self.final, self.sems, self.pieces = cross, final, sems, pieces
+        self.core = lax.axis_index("section")
+        self.z = lax.axis_index("mp")
+        self.dp = lax.axis_index("dp")
+        self.bits_above = more_bits(copies)
+        self.groups = groups
+        self.stages = 6 + len(self.bits_above)
+        self.rows = part.shape[1] // pieces
+        self.slot = lax.rem(self.core + layer, 2)
+        self.near = others(self.dp, copies)
+        self.bits = [lax.rem(self.dp, 2), lax.rem(self.dp // 2, 2)]
+        self.pair = self.z + 2 - 4 * (self.z // 2)
+
+    def copy(self, piece, kind, src, dst, device):
+        return send(src, dst, self.sems, piece * self.kinds + kind, device)
+
+    def span(self, piece, start, count):
+        return pl.ds(pl.multiple_of(piece * self.rows + start, 16), count)
+
+    def chunk(self, half, outer, inner):
+        eighth = self.rows // 8
+        return half * 4 * eighth + outer * 2 * eighth + inner * eighth
+
+    def twin_copy(self, piece):
+        rows = self.span(piece, 0, self.rows)
+        return self.copy(
+            piece, 0, self.part.at[1 - self.slot, rows], self.twin.at[rows], (1 - self.core, self.z, self.dp)
+        )
+
+    def first_copy(self, piece, half):
+        count = self.rows // 4
+        axis = half
+        src = self.span(piece, self.chunk(half, 1 - self.bits[axis], 0), count)
+        dst = self.span(piece, 0, count)
+        dst = pl.ds(pl.multiple_of((piece * 2 + half) * count, 16), count)
+        return self.copy(
+            piece, 1 + half, self.part.at[self.slot, src], self.first.at[dst], (self.core, self.z, self.near[axis])
+        )
+
+    def second_copy(self, piece, half):
+        count = self.rows // 8
+        axis = 1 - half
+        src = self.span(piece, self.chunk(half, self.bits[half], 1 - self.bits[axis]), count)
+        dst = pl.ds(pl.multiple_of((piece * 2 + half) * count, 16), count)
+        return self.copy(
+            piece, 3 + half, self.part.at[self.slot, src], self.second.at[dst], (self.core, self.z, self.near[axis])
+        )
+
+    def own(self, piece, half):
+        return self.span(piece, self.chunk(half, self.bits[half], self.bits[1 - half]), self.rows // 8)
+
+    def cross_copy(self, piece, half):
+        count = self.rows // 8
+        dst = pl.ds(pl.multiple_of((piece * 2 + half) * count, 16), count)
+        return self.copy(
+            piece,
+            5 + half,
+            self.part.at[self.slot, self.own(piece, half)],
+            self.cross.at[dst],
+            (1 - self.core, self.pair, self.dp),
+        )
+
+    def gather_copies(self, piece, half):
+        rows = self.own(piece, half)
+        near, far = self.near[half], self.near[1 - half]
+        both = near + far - self.dp
+        return [
+            send(
+                self.final.at[rows],
+                self.final.at[rows],
+                self.sems,
+                (self.pieces * self.kinds) + (piece * 2 + half) * 3 + n,
+                (self.core, self.z, device),
+            )
+            for n, device in enumerate((near, far, both))
+        ]
+
+    def group_copy(self, step, piece, half):
+        count = self.rows // 8
+        rows = self.own(piece, half)
+        dst = pl.ds(pl.multiple_of((piece * 2 + half) * count, 16), count)
+        index = self.pieces * (self.kinds + 6) + (step * self.pieces + piece) * 2 + half
+        device = (self.core, self.z, flipped(self.dp, self.bits_above[step]))
+        return send(self.final.at[rows], self.groups.at[step, dst], self.sems, index, device)
+
+    @staticmethod
+    def semaphores(pieces, copies):
+        return pieces * (GradSum.kinds + 6 + 2 * len(more_bits(copies)))
+
+    def stage(self, number, piece):
+        if number < 4:
+            (self.stage0, self.stage1, self.stage2, self.stage3)[number](piece)
+        elif number < self.stages - 1:
+            self.stage4(number - 4, piece)
+        else:
+            self.stage5(piece)
+
+    def add(self, dst_rows, other):
+        value = self.part[self.slot, dst_rows, :].astype(f32) + other.astype(f32)
+        self.part[self.slot, dst_rows, :] = value.astype(bf16)
+
+    def stage0(self, piece):
+        self.twin_copy(piece).start()
+
+    def stage1(self, piece):
+        self.twin_copy(piece).wait_recv()
+        rows = self.span(piece, 0, self.rows)
+        self.add(rows, self.twin[rows, :])
+        for half in range(2):
+            self.first_copy(piece, half).start()
+
+    def stage2(self, piece):
+        count = self.rows // 4
+        for half in range(2):
+            self.first_copy(piece, half).wait()
+            rows = self.span(piece, self.chunk(half, self.bits[half], 0), count)
+            self.add(rows, self.first[pl.ds(pl.multiple_of((piece * 2 + half) * count, 16), count), :])
+            self.second_copy(piece, half).start()
+
+    def stage3(self, piece):
+        count = self.rows // 8
+        for half in range(2):
+            self.second_copy(piece, half).wait()
+            self.add(self.own(piece, half), self.second[pl.ds(pl.multiple_of((piece * 2 + half) * count, 16), count), :])
+
+            @pl.when(self.core != self.layer)
+            def _():
+                self.cross_copy(piece, half).start()
+
+    def stage4(self, step, piece):
+        count = self.rows // 8
+
+        @pl.when(self.core == self.layer)
+        def _():
+            for half in range(2):
+                rows = self.own(piece, half)
+                slot = pl.ds(pl.multiple_of((piece * 2 + half) * count, 16), count)
+                if step == 0:
+                    self.cross_copy(piece, half).wait_recv()
+                    value = self.part[self.slot, rows, :].astype(f32) + self.cross[slot, :].astype(f32)
+                else:
+                    self.group_copy(step - 1, piece, half).wait()
+                    value = self.final[rows, :].astype(f32) + self.groups[step - 1, slot, :].astype(f32)
+                self.final[rows, :] = value.astype(bf16)
+                if step < len(self.bits_above):
+                    self.group_copy(step, piece, half).start()
+                else:
+                    for copy in self.gather_copies(piece, half):
+                        copy.start()
+
+    def stage5(self, piece):
+        self.twin_copy(piece).wait_send()
+
+        @pl.when(self.core == self.layer)
+        def _():
+            for half in range(2):
+                for copy in self.gather_copies(piece, half):
+                    copy.wait()
+
+        @pl.when(self.core != self.layer)
+        def _():
+            for half in range(2):
+                self.cross_copy(piece, half).wait_send()
+
+
+class VectorSum:
+    def __init__(self, layer, part, got, out, sems, copies):
+        self.layer, self.part, self.got, self.out, self.sems = layer, part, got, out, sems
+        core, z, dp = (lax.axis_index(name) for name in ("section", "mp", "dp"))
+        self.devices = [(1 - core, z, dp)] + [(core, z, near) for near in others(dp, copies)]
+        self.devices += [(core, z, flipped(dp, bit)) for bit in more_bits(copies)]
+        self.devices.append((core, z + 2 - 4 * (z // 2), dp))
+        self.last = len(self.devices) - 1
+
+    def copy(self, step):
+        return send(self.part, self.got.at[step], self.sems, step, self.devices[step])
+
+    def start(self, step):
+        self.copy(step).start()
+
+    def add(self, step):
+        self.copy(step).wait()
+        if step < self.last:
+            self.part[...] += self.got[step]
+            self.start(step + 1)
+        else:
+            self.out[0:8, :] = self.part[0:8, :] + self.got[step, 0:8, :]
+            self.out[8:10, :] = self.part[8:10, :] + self.got[step, 10:12, :]
+            self.out[10:16, :] = jnp.zeros_like(self.out[10:16, :])
+
+
+def grads_kernel(
+    copies,
+    pieces,
+    part1,
+    part0,
+    vec1,
+    vec0,
+    final,
+    out1,
+    out0,
+    sum1,
+    sum0,
+    twin1,
+    first1,
+    second1,
+    cross1,
+    groups1,
+    twin0,
+    first0,
+    second0,
+    cross0,
+    groups0,
+    got1,
+    got0,
+    work1,
+    work0,
+    sems1,
+    sems0,
+    vec_sems1,
+    vec_sems0,
+    load_sems,
+):
+    core, z, dp = (lax.axis_index(name) for name in ("section", "mp", "dp"))
+    near = others(dp, copies)
+    pair = z + 2 - 4 * (z // 2)
+    devices = [
+        (1 - core, z, dp),
+        (core, z, near[0]),
+        (core, z, near[1]),
+        (core, z, near[0] + near[1] - dp),
+        (core, pair, dp),
+        (1 - core, pair, dp),
+    ] + [(core, z, flipped(dp, bit)) for bit in more_bits(copies)]
+    barrier = pltpu.get_barrier_semaphore()
+    for device in devices:
+        pl.semaphore_signal(barrier, inc=1, device_id=device, device_id_type=MESH)
+    loads = [
+        pltpu.make_async_copy(src, dst, load_sems.at[n])
+        for n, (src, dst) in enumerate(((part1, sum1), (part0, sum0)))
+    ]
+    for load in loads:
+        load.start()
+    pl.semaphore_wait(barrier, len(devices))
+    work1[...] = vec1[...]
+    work0[...] = vec0[...]
+    vectors = [
+        VectorSum(1, work1, got1, out1, vec_sems1, copies),
+        VectorSum(0, work0, got0, out0, vec_sems0, copies),
+    ]
+    sums = [
+        GradSum(1, sum1, twin1, first1, second1, cross1, groups1, final, sems1, pieces, copies),
+        GradSum(0, sum0, twin0, first0, second0, cross0, groups0, final, sems0, pieces, copies),
+    ]
+    for vector in vectors:
+        vector.start(0)
+    for load in loads:
+        load.wait()
+    work = [(one, piece) for one in sums for piece in range(pieces)]
+    stages = sums[0].stages
+    for tick in range(max(len(work) + stages - 1, vectors[0].last + 1)):
+        for stage in range(stages):
+            n = tick - stage
+            if 0 <= n < len(work):
+                one, piece = work[n]
+                one.stage(stage, piece)
+        if tick <= vectors[0].last:
+            for vector in vectors:
+                vector.add(tick)
+
+
+def sum_grads(copies, part1, part0, vec1, vec0):
+    pieces = 6
+    above = len(more_bits(copies))
+    _, rows, width = part1.shape
+    vmem = pl.BlockSpec(memory_space=pltpu.VMEM)
+    hbm = pl.BlockSpec(memory_space=pl.ANY)
+    shape = jax.ShapeDtypeStruct
+    buffers = [
+        pltpu.VMEM((rows, width), bf16),
+        pltpu.VMEM((rows // 2, width), bf16),
+        pltpu.VMEM((rows // 4, width), bf16),
+        pltpu.VMEM((rows // 4, width), bf16),
+        pltpu.VMEM((max(1, above), rows // 4 if above else 16, width), bf16),
+    ]
+    return pl.pallas_call(
+        partial(grads_kernel, copies, pieces),
+        out_shape=(shape((rows, width), bf16), shape(vec1.shape, f32), shape(vec1.shape, f32)),
+        in_specs=[hbm, hbm, vmem, vmem],
+        out_specs=[vmem] * 3,
+        scratch_shapes=[pltpu.VMEM(part1.shape, bf16)] * 2
+        + buffers * 2
+        + [pltpu.VMEM((4 + above, *vec1.shape), f32)] * 2
+        + [pltpu.VMEM(vec1.shape, f32)] * 2
+        + [pltpu.SemaphoreType.DMA((2, GradSum.semaphores(pieces, copies)))] * 2
+        + [pltpu.SemaphoreType.DMA((2, 4 + above))] * 2
+        + [pltpu.SemaphoreType.DMA((2,))],
+        compiler_params=pltpu.CompilerParams(
+            vmem_limit_bytes=56 * 2**20, collective_id=3, has_side_effects=True
+        ),
+        name="sum_grads",
+    )(part1, part0, vec1, vec0)
 
 
 def segment_ids(lengths, length):
@@ -591,16 +909,12 @@
         other = route(array, swap_core)
         return [pick(core == layer, array, other) for layer in range(2)]
 
-    mixing = in_weight[0].transpose(1, 0, 2)
-
-    def slots(array, axis):
-        far = fetch(array, axis)
-        return [jnp.stack(pair) for pair in zip(both_layers(array), both_layers(far))]
-
-    w_in = slots(mixing, 1)
-    w_out = slots(out_weight[0], 0)
-    w_up = slots(up_weight[0], 0)
-    w_down = slots(down_weight[0], 0)
+    where = Places(local, units, width)
+    shard = jnp.concatenate(
+        [in_weight[0].transpose(1, 2, 0).reshape(3 * local, width), out_weight[0], up_weight[0], down_weight[0]]
+    )
+    far = fetch(shard, 0)
+    weights = [jnp.stack(pair) for pair in zip(both_layers(shard), both_layers(far))]
     shard_vec = jnp.concatenate([in_bias[0].reshape(-1), up_bias[0]])
     far_vec = route(shard_vec, swap_pair)
     whole_vec = jnp.concatenate(
@@ -660,7 +974,7 @@
         vec = jnp.concatenate([gains, shifts, branch], axis=0)
         start = state
         state, *kept = forward_layer(
-            state, w_in[layer], w_out[layer], w_up[layer], w_down[layer], b_in, b_up, vec, seg_col, seg_row
+            where, state, weights[layer], b_in, b_up, vec, seg_col, seg_row
         )
         saved.append(((start, *kept), vec))
         outputs.append(state)
@@ -670,43 +984,15 @@
     grads_out = [None, None]
     for layer in (1, 0):
         kept, vec = saved[layer]
-        grad, d_in, d_out, d_up, d_down, d_vec, d_b_up, d_b_in = backward_layer(
-            grad, kept, w_in[layer], w_out[layer], w_up[layer], w_down[layer], vec, seg_col, seg_row
+        grad, partials[layer], vectors[layer] = backward_layer(
+            where, grad, kept, weights[layer], vec, seg_col, seg_row
         )
         grads_out[layer] = grad
-        partials[layer] = (d_in, d_out, d_up, d_down)
-        shard_terms = [
-            jnp.concatenate([d_b_in[i, 0], d_b_in[i, 2], d_b_up[i, 0]]) for i in range(2)
-        ]
-        vectors[layer] = (shard_terms, d_vec[:6].reshape(-1))
-
-    def reduce_layer(index, layer):
-        own, far = partials[layer][index]
-        got = route(pick(core == 0, far, own), swap_core)
-        total = (pick(core == 0, own, far).astype(f32) + got.astype(f32)).astype(bf16)
-        piece = lax.psum_scatter(total, "dp", scatter_dimension=total.ndim - 2, tiled=True)
-        cross = route(piece, [(at(1, m), at(0, m ^ 2)) for m in range(4)])
-        return piece + cross
-
-    final = []
-    for index in range(4):
-        first = reduce_layer(index, 0)
-        second = reduce_layer(index, 1)
-        second = route(second, [(at(0, m), at(1, m)) for m in range(4)])
-        final.append(lax.all_gather(pick(core == 0, first, second), "dp", axis=first.ndim - 2, tiled=True).astype(f32))
-    g_in, g_out, g_up, g_down = final
-
-    shard_sum, whole_sum = [], []
-    for layer in range(2):
-        (own, far), whole = vectors[layer]
-        shard_sum.append(jnp.stack([own, far]))
-        whole_sum.append(whole)
-    shard_sum = jnp.stack(shard_sum)
-    across = route(shard_sum[:, 1], swap_pair)
-    shard_sum = lax.psum(shard_sum[:, 0] + across, ("section", "dp"))
-    whole_sum = lax.psum(jnp.stack(whole_sum), ("section", "mp", "dp")) * 0.5
-    shard_mine = pick(core == 0, shard_sum[0], shard_sum[1])
-    whole_mine = pick(core == 0, whole_sum[0], whole_sum[1]).reshape(3, 2, width)
+    final, vec1, vec0 = sum_grads(copies, partials[1], partials[0], vectors[1], vectors[0])
+    vec = pick(core == 0, vec0, vec1)
+    g_in = final[: 3 * local].astype(f32).reshape(3, local, width).transpose(2, 0, 1)
+    g_out, g_up, g_down = (final[rows].astype(f32) for rows in (where.out, where.up, where.down))
+    b_in = jnp.stack([vec[9, :local], vec[9, 2 * block : 2 * block + local]])
 
     def rows_out(pair):
         both = jnp.stack(pair)
@@ -725,15 +1011,15 @@
     return (
         section_outputs[None],
         input_grads[None],
-        whole_mine[0][None],
-        whole_mine[1][None],
-        g_in.transpose(1, 0, 2)[None],
-        shard_mine[: 2 * local].reshape(1, 2, local),
+        vec[0:2][None],
+        vec[2:4][None],
+        g_in[None],
+        b_in[None],
         g_out[None],
         g_up[None],
-        shard_mine[2 * local :][None],
+        vec[8][None],
         g_down[None],
-        whole_mine[2][None],
+        vec[4:6][None],
     )
 
 

time: 675 us -> 550 us (0.81)
  Pallas kernels: 218 us -> 338 us
  blocking collectives: 116 us -> 0 us
  other arithmetic: 80.2 us -> 34.2 us
  starting transfers between devices: 53.6 us -> 19 us
  local copies, waits for them, and re-layouts: 40.9 us -> 11.5 us
  waiting for transfers between devices: 139 us -> 124 us
    pallas_call x4 -> x5, Pallas kernels: 218 us -> 338 us  [the longest x2 124 us: backward_layer(): pl.pallas_call(partial(backward_kernel, where), out_shape=(shape((half, w...]
    all_gather x4 -> x0, blocking collectives: 59.4 us -> none  [the longest x2 31.8 us: fetch(): return lax.all_gather(piece, 'dp', axis=axis, tiled=True)]
    psum x2 -> x0, blocking collectives: 56.9 us -> none  [the longest x1 39.9 us: per_device(): whole_sum = lax.psum(jnp.stack(whole_sum), ('section', 'mp', 'dp')) * 0.5]
    all_gather x2 -> x1, waiting for transfers between devices: 0.01 us -> 39.4 us  [fetch(): return lax.all_gather(piece, 'dp', axis=axis, tiled=True)]
    ppermute x43 -> x13, starting transfers between devices: 52.7 us -> 19 us  [route(): return lax.ppermute(value, ('section', 'mp'), pairs)]
    all_gather x2 -> x0, waiting for transfers between devices: 29.3 us -> none  [per_device(): lax.all_gather(pick(core == 0, first, second), 'dp', axis=first.ndim - 2,...]
    reduce_scatter x8 -> x0, waiting for transfers between devices: 27.5 us -> none  [reduce_layer(): lax.psum_scatter(total, 'dp', scatter_dimension=total.ndim - 2, tiled=True)]
    select_n x25 -> x12, other arithmetic: 23.9 us -> 5.99 us  [pick(): return jnp.where(flag, yes, no)]
  transfers between devices with their start and end apart: 55 -> 14, of which waited for: 13 -> 6; matrix products, arithmetic and copies ran while one was open for 15% -> 3% of each run, Pallas kernels for 9% -> 0%
where the time goes in v4:
time: 550 us; the launch traced here: 541 us
  Pallas kernels  338 us (61%)
  waiting for transfers between devices  124 us (23%)
  other arithmetic  34.2 us (6%)
  starting transfers between devices  19 us (3%)
  between operations  15 us (3%)
  local copies, waits for them, and re-layouts  11.5 us (2%)
    pallas_call x2, Pallas kernels, backward_layer(): pl.pallas_call(partial(backward_kernel, where), out_shape=(shape((half, w...  124 us
    pallas_call x1, Pallas kernels, sum_grads(): pl.pallas_call(partial(grads_kernel, copies, pieces), out_shape=(shape((r...  121 us
    pallas_call x2, Pallas kernels, forward_layer(): pl.pallas_call(partial(forward_kernel, where), out_shape=(shape((half, wi...  92.6 us
    ppermute x13, waiting for transfers between devices, route(): return lax.ppermute(value, ('section', 'mp'), pairs)  84.6 us
    all_gather x1, waiting for transfers between devices, fetch(): return lax.all_gather(piece, 'dp', axis=axis, tiled=True)  39.4 us
    ppermute x13, starting transfers between devices, route(): return lax.ppermute(value, ('section', 'mp'), pairs)  19 us
    another operation x4, other arithmetic, per_device(): jnp.stack(pair)  16.4 us
  transfers between devices with their start and end apart: 14, of which 6 were waited for; matrix products, arithmetic and copies ran while one was open for 3% of the time, Pallas kernels for 0%

profile of v4, /device:TPU:0, one launch (start us, length us, event | category | flops | bytes accessed | tf_op | source)
XLA Modules:
  0.0 541.4 jit_solution(2561481513408750142)
XLA Ops:
  7.2 3.4 pad_maximum_fusion.2
  10.7 1.4 constant_dynamic-slice_fusion
  12.1 4.1 collective-permute-start.3
  16.2 38.6 %collective-permute-done.3 = bf16[576,768]{1,0:T(8,128)(2,1)S(1)} collective-permute-done((bf16[576,768]{1,0:T(8,128)(2,1)S(1)}, bf16[576,768]{1,0:T(8,128)(2,1)S(1)}, u32[]{:S(2)}, u32[]{:S(2)}) %collective-permute-start.3) | collective-permute-done | bytes 884768 | tf_op jit(solution)/shard_map/ppermute | solution.py:882
  54.8 0.9 copy-done.24
  56.0 0.8 select_bitcast_fusion.5
  56.8 4.9 collective-permute-start.9
  61.8 2.0 collective-permute-start
  64.8 39.4 %all-gather.2.cloned.1.call-done = bf16[2304,768]{1,0:T(8,128)(2,1)} async-done(((bf16[576,768]{1,0:T(8,128)(2,1)}), bf16[2304,768]{1,0:T(8,128)(2,1)}) %all-gather.2.cloned.1.call-update) | async-done | bytes 3538960 | tf_op jit(solution)/shard_map/all_gather | solution.py:906
  104.7 1.6 collective-permute-start.10
  106.3 0.6 collective-permute-start.1
  107.1 9.6 %collective-permute-done.10 = bf16[256,768]{1,0:T(8,128)(2,1)} collective-permute-done((bf16[256,768]{1,0:T(8,128)(2,1)S(1)}, bf16[256,768]{1,0:T(8,128)(2,1)}, u32[]{:S(2)}, u32[]{:S(2)}) %collective-permute-start.10) | collective-permute-done | bytes 393248 | tf_op jit(solution)/shard_map/ppermute | solution.py:882
  116.7 2.3 maximum_select_fusion.3.grad_ref
  119.0 5.7 %collective-permute-done.1 = bf16[256,768]{1,0:T(8,128)(2,1)S(1)} collective-permute-done((bf16[256,768]{1,0:T(8,128)(2,1)S(1)}, bf16[256,768]{1,0:T(8,128)(2,1)S(1)}, u32[]{:S(2)}, u32[]{:S(2)}) %collective-permute-start.1) | collective-permute-done | bytes 393248 | tf_op jit(solution)/shard_map/ppermute | solution.py:882
  124.7 1.2 maximum_select_fusion.2.state_ref.start_ref
  125.9 3.1 select_bitcast_fusion.1
  129.1 4.3 select_bitcast_fusion
  133.4 5.5 %pad_maximum_fusion.1.w_ref = bf16[2,2304,768]{2,1,0:T(8,128)(2,1)} fusion(bf16[1,2304,768]{2,1,0:T(8,128)(2,1)} %get-tuple-element.67, bf16[1,2304,768]{2,1,0:T(8,128)(2,1)S(1)} %get-tuple-element.65), kind=kLoop, calls=%fused_computation.1 | loop fusion | flops 3538944 | bytes 14155776 | tf_op jit(solution)/shard_map/stack | solution.py:917
  138.9 3.4 pad_maximum_fusion.w_ref
  142.4 44.4 %forward_layer.2 = (bf16[512,768]{1,0:T(8,128)(2,1)S(1)}, bf16[512,768]{1,0:T(8,128)(2,1)S(1)}, bf16[3,1024,192]{2,1,0:T(8,128)(2,1)}, f32[3,1024]{1,0:T(4,128)S...) custom-call(bf16[512,768]{1,0:T(8,128)(2,1)} %maximum_select_fusion., ...), custom_call_target="tpu_custom_call" | custom-call | tf_op jit(solution)/shard_map/forward_layer/pallas_call | solution.py:247
  186.8 0.9 copy-done.1
  187.6 0.9 copy-done.3
  188.5 0.9 copy-done.4
  189.4 0.8 copy-done.7
  190.2 0.6 copy-done.12
  190.8 48.2 %forward_layer.3 = (bf16[512,768]{1,0:T(8,128)(2,1)S(1)}, bf16[512,768]{1,0:T(8,128)(2,1)S(1)}, bf16[3,1024,192]{2,1,0:T(8,128)(2,1)}, f32[3,1024]{1,0:T(4,128)S...) custom-call(bf16[512,768]{1,0:T(8,128)(2,1)} %copy-done.1, ...), custom_call_target="tpu_custom_call" | custom-call | tf_op jit(solution)/shard_map/forward_layer/pallas_call | solution.py:247
  239.1 0.9 copy-done.5
  239.9 0.9 copy-done.6
  240.8 0.8 copy-done.8
  241.6 0.6 copy-done.13
  242.2 64.3 %backward_layer.2 = (bf16[512,768]{1,0:T(8,128)(2,1)}, bf16[2,2304,768]{2,1,0:T(8,128)(2,1)}, f32[16,768]{1,0:T(8,128)}) custom-call(bf16[512,768]{1,0:T(8,128)(2,1)} %maximum_select_fusion.3.grad_ref, bf16[512,768]{1,0:T(8,128)(2,1)} %copy-done.1, bf16[512,768]{1,0:T(8,128)(2,1)} %copy-done.5, bf16[3,1024,192]{2,1,0:T(8,128)(2,1)} %get-tuple-element.41.qkv_ref, ...), custom_call_target="tpu_custom_call" | custom-call | tf_op jit(solution)/shard_map/backward_layer/pallas_call | solution.py:488
  306.6 59.7 %backward_layer.3 = (bf16[512,768]{1,0:T(8,128)(2,1)}, bf16[2,2304,768]{2,1,0:T(8,128)(2,1)}, f32[16,768]{1,0:T(8,128)}) custom-call(bf16[512,768]{1,0:T(8,128)(2,1)} %get-tuple-element.48.grad_ref, bf16[512,768]{1,0:T(8,128)(2,1)} %maximum_select_fusion.2.state_ref.start_ref, bf16[512,768]{1,0:T(8,128)(2,1)} %copy-done.3, ...), custom_call_target="tpu_custom_call" | custom-call | tf_op jit(solution)/shard_map/backward_layer/pallas_call | solution.py:488
  366.3 121.0 %sum_grads.1 = (bf16[2304,768]{1,0:T(8,128)(2,1)}, f32[16,768]{1,0:T(8,128)}, f32[16,768]{1,0:T(8,128)}) custom-call(bf16[2,2304,768]{2,1,0:T(8,128)(2,1)} %get-tuple-element.58.part1, bf16[2,2304,768]{2,1,0:T(8,128)(2,1)} %get-tuple-element.59.part0, f32[16,768]{1,0:T(8,128)} %get-tuple-element.60.vec1, f32[16,768]{1,0:T(8,128)} %get-tuple-element.61.vec0), custom_call_target="tpu_custom_call" | custom-call | tf_op jit(solution)/shard_map/sum_grads/pallas_call | solution.py:823
  487.4 0.9 broadcast_select_fusion
  488.3 0.6 slice_bitcast_fusion
  488.9 1.6 collective-permute-start.7
  490.6 1.3 collective-permute-start.11
  492.0 0.9 bitcast_convert_fusion.2
  492.9 1.4 convert_bitcast_fusion
  494.3 23.9 %collective-permute-done.7 = bf16[2,256,768]{2,1,0:T(8,128)(2,1)S(1)} collective-permute-done((bf16[2,256,768]{2,1,0:T(8,128)(2,1)S(1)}, bf16[2,256,768]{2,1,0:T(8,128)(2,1)S(1)}, u32[]{:S(2)}, u32[]{:S(2)}) %collective-permute-start.7) | collective-permute-done | bytes 786464 | tf_op jit(solution)/shard_map/ppermute | solution.py:882
  518.6 1.3 collective-permute-start.8
  519.9 6.7 %collective-permute-done.11 = bf16[2,256,768]{2,1,0:T(8,128)(2,1)S(1)} collective-permute-done((bf16[2,256,768]{2,1,0:T(8,128)(2,1)S(1)}, bf16[2,256,768]{2,1,0:T(8,128)(2,1)S(1)}, u32[]{:S(2)}, u32[]{:S(2)}) %collective-permute-start.11) | collective-permute-done | bytes 786464 | tf_op jit(solution)/shard_map/ppermute | solution.py:882
  527.0 1.3 collective-permute-start.12
  528.4 0.6 slice.296
  528.9 0.6 maximum_bitcast_fusion.5
  529.5 2.5 bitcast_convert_fusion
  532.1 1.0 fusion.7
  533.1 1.3 fusion.6
  (126 shorter events, 2.7 us)
Async XLA Ops:
  7.2 97.1 %all-gather.2.cloned.1.call-start = ((), (), s32[]{:S(2)}) async-start(), calls=%async_computation | async-start | bytes 4423680 | tf_op jit(solution)/shard_map/all_gather | solution.py:906
  10.7 45.1 %copy-start.29 = (f32[1,2,192]{2,1,0:T(2,128)S(1)}, f32[1,2,192]{2,1,0:T(2,128)}, u32[]{:S(2)}) copy-start(f32[1,2,192]{2,1,0:T(2,128)} %param.18) | copy-start | bytes 4612
  10.7 45.2 %copy-start.28 = (f32[1,768]{1,0:T(1,128)S(1)}, f32[1,768]{1,0:T(1,128)}, u32[]{:S(2)}) copy-start(f32[1,768]{1,0:T(1,128)} %param.21) | copy-start | bytes 9220
  10.7 45.3 %copy-start.21 = (bf16[2,256,768]{2,1,0:T(8,128)(2,1)S(1)}, bf16[2,256,768]{2,1,0:T(8,128)(2,1)}, u32[]{:S(2)}) copy-start(bf16[2,256,768]{2,1,0:T(8,128)(2,1)} %param.13) | copy-start | bytes 2359300
  10.7 51.1 %copy-start.22 = (bf16[2,256,768]{2,1,0:T(8,128)(2,1)S(1)}, bf16[2,256,768]{2,1,0:T(8,128)(2,1)}, u32[]{:S(2)}) copy-start(bf16[2,256,768]{2,1,0:T(8,128)(2,1)} %param.12) | copy-start | bytes 2359300
  12.1 42.7 %collective-permute-start.3 = (bf16[576,768]{1,0:T(8,128)(2,1)S(1)}, bf16[576,768]{1,0:T(8,128)(2,1)S(1)}, u32[]{:S(2)}, u32[]{:S(2)}) collective-permute-start(bf16[576,768]{1,0:T(8,128)(2,1)S(1)} %constant_dynamic-slice_fusion), channel_id=1, source_target_pairs={{0,8},{4,12},{8,0},{12,4},{16,24},{20,28},{24,16},{28,20},{1,9},{5... | collective-permute-start | bytes 2654216 | tf_op jit(solution)/shard_map/ppermute | solution.py:882
  54.8 0.9 copy-start.24
  54.8 9.1 %copy-start.30 = (s32[2,4]{1,0:T(2,128)S(1)}, s32[2,4]{1,0:T(2,128)}, u32[]{:S(2)}) copy-start(s32[2,4]{1,0:T(2,128)} %param.14) | copy-start | bytes 100
  55.7 70.2 %collective-permute-start.2 = (bf16[2304,768]{1,0:T(8,128)(2,1)}, bf16[2304,768]{1,0:T(8,128)(2,1)}, u32[]{:S(2)}, u32[]{:S(2)}) collective-permute-start(bf16[2304,768]{1,0:T(8,128)(2,1)} %pad_maximum_fusion.2), channel_id=1, source_target_pairs={{0,16},{4,20},{8,24},{12,28},{16,0},{20,4},{24,8},{28,12},{1,17},{... | collective-permute-start | bytes 10616840 | tf_op jit(solution)/shard_map/ppermute | solution.py:882
  55.9 8.7 %collective-permute-start.5 = (f32[1152]{0:T(1024)S(1)}, f32[1152]{0:T(1024)S(1)}, u32[]{:S(2)}, u32[]{:S(2)}) collective-permute-start(f32[1152]{0:T(1024)S(1)} %pad_maximum_fusion.5), channel_id=1, source_target_pairs={{0,8},{4,12},{8,0},{12,4},{16,24},{20,28},{24,16},{28,20},{1,9},{5... | collective-permute-start | bytes 13832 | tf_op jit(solution)/shard_map/ppermute | solution.py:882
  56.8 7.7 %copy-start.25 = (f32[1,2,768]{2,1,0:T(2,128)S(1)}, f32[1,2,768]{2,1,0:T(2,128)}, u32[]{:S(2)}) copy-start(f32[1,2,768]{2,1,0:T(2,128)} %param.15) | copy-start | bytes 18436
  56.8 7.7 %copy-start.26 = (f32[1,2,768]{2,1,0:T(2,128)S(1)}, f32[1,2,768]{2,1,0:T(2,128)}, u32[]{:S(2)}) copy-start(f32[1,2,768]{2,1,0:T(2,128)} %param.16) | copy-start | bytes 18436
  56.8 7.7 %copy-start.27 = (f32[1,2,768]{2,1,0:T(2,128)S(1)}, f32[1,2,768]{2,1,0:T(2,128)}, u32[]{:S(2)}) copy-start(f32[1,2,768]{2,1,0:T(2,128)} %param.23) | copy-start | bytes 18436
  56.8 47.8 %collective-permute-start.9 = (bf16[256,768]{1,0:T(8,128)(2,1)}, bf16[256,768]{1,0:T(8,128)(2,1)S(1)}, u32[]{:S(2)}, u32[]{:S(2)}) collective-permute-start(bf16[256,768]{1,0:T(8,128)(2,1)} %select_bitcast_fusion.5), channel_id=1, source_target_pairs={{0,8},{4,12},{24,16},{28,20},{1,9},{5,13},{25,17},{29,21},{2,10},{... | collective-permute-start | bytes 1179656 | tf_op jit(solution)/shard_map/ppermute | solution.py:882
  61.8 44.4 %collective-permute-start = (bf16[256,768]{1,0:T(8,128)(2,1)S(1)}, bf16[256,768]{1,0:T(8,128)(2,1)}, u32[]{:S(2)}, u32[]{:S(2)}) collective-permute-start(bf16[256,768]{1,0:T(8,128)(2,1)S(1)} %select_bitcast_fusion.6), channel_id=1, source_target_pairs={{0,8},{4,12},{24,16},{28,20},{1,9},{5,13},{25,17},{29,21},{2,10},{... | collective-permute-start | bytes 1179656 | tf_op jit(solution)/shard_map/ppermute | solution.py:882
  64.4 126.4 %copy-start = (s32[1024,1]{1,0:T(8,128)}, s32[1024,1]{1,0:T(8,128)S(1)}, u32[]{:S(2)}) copy-start(s32[1024,1]{1,0:T(8,128)S(1)} %compare_select_fusion.seg_col) | copy-start | bytes 12292
  64.6 39.7 %collective-permute-start.6 = (f32[6912]{0:T(1024)S(1)}, f32[6912]{0:T(1024)S(1)}, u32[]{:S(2)}, u32[]{:S(2)}) collective-permute-start(f32[6912]{0:T(1024)S(1)} %constant_dynamic-update-slice_fusion), channel_id=1, source_target_pairs={{0,16},{4,20},{8,24},{12,28},{16,0},{20,4},{24,8},{28,12},{1,17},{... | collective-permute-start | bytes 82952 | tf_op jit(solution)/shard_map/ppermute | solution.py:882
  64.7 126.1 %copy-start.11 = (s32[1,1024]{1,0:T(1,128)}, s32[1,1024]{1,0:T(1,128)S(1)}, u32[]{:S(2)}) copy-start(s32[1,1024]{1,0:T(1,128)S(1)} %compare_select_fusion.1.seg_row) | copy-start | bytes 12292
  104.3 24.8 %collective-permute-start.4 = (bf16[2304,768]{1,0:T(8,128)(2,1)}, bf16[2304,768]{1,0:T(8,128)(2,1)}, u32[]{:S(2)}, u32[]{:S(2)}) collective-permute-start(bf16[2304,768]{1,0:T(8,128)(2,1)} %all-gather.2.cloned.1.call-done), channel_id=1, source_target_pairs={{0,16},{4,20},{8,24},{12,28},{16,0},{20,4},{24,8},{28,12},{1,17},{... | collective-permute-start | bytes 10616840 | tf_op jit(solution)/shard_map/ppermute | solution.py:882
  104.7 12.1 %collective-permute-start.10 = (bf16[256,768]{1,0:T(8,128)(2,1)S(1)}, bf16[256,768]{1,0:T(8,128)(2,1)}, u32[]{:S(2)}, u32[]{:S(2)}) collective-permute-start(bf16[256,768]{1,0:T(8,128)(2,1)S(1)} %bitcast_select_fusion.3), channel_id=1, source_target_pairs={{0,4},{4,0},{8,12},{12,8},{16,20},{20,16},{24,28},{28,24},{1,5},{5... | collective-permute-start | bytes 1179656 | tf_op jit(solution)/shard_map/ppermute | solution.py:882
  106.2 19.7 %copy-start.23 = (bf16[1,192,768]{2,1,0:T(8,128)(2,1)S(1)}, bf16[1,192,768]{2,1,0:T(8,128)(2,1)}, u32[]{:S(2)}) copy-start(bf16[1,192,768]{2,1,0:T(8,128)(2,1)} %param.19) | copy-start | bytes 884740
  106.3 18.4 %collective-permute-start.1 = (bf16[256,768]{1,0:T(8,128)(2,1)S(1)}, bf16[256,768]{1,0:T(8,128)(2,1)S(1)}, u32[]{:S(2)}, u32[]{:S(2)}) collective-permute-start(bf16[256,768]{1,0:T(8,128)(2,1)S(1)} %bitcast_select_fusion.4), channel_id=1, source_target_pairs={{0,4},{4,0},{8,12},{12,8},{16,20},{20,16},{24,28},{28,24},{1,5},{5... | collective-permute-start | bytes 1179656 | tf_op jit(solution)/shard_map/ppermute | solution.py:882
  107.0 18.9 %copy-start.17 = (bf16[1,768,3,192]{1,3,2,0:T(8,128)(2,1)S(1)}, bf16[1,768,3,192]{1,3,2,0:T(8,128)(2,1)}, u32[]{:S(2)}) copy-start(bf16[1,768,3,192]{1,3,2,0:T(8,128)(2,1)} %param.17) | copy-start | bytes 2654212
  107.1 83.7 %copy-start.10 = (f32[6,768]{1,0:T(8,128)}, f32[6,768]{1,0:T(8,128)S(1)}, u32[]{:S(2)}) copy-start(f32[6,768]{1,0:T(8,128)S(1)} %pad_maximum_fusion.4.vec_ref) | copy-start | bytes 55300
  107.1 35.2 %copy-start.9 = (f32[6,768]{1,0:T(8,128)}, f32[6,768]{1,0:T(8,128)S(1)}, u32[]{:S(2)}) copy-start(f32[6,768]{1,0:T(8,128)S(1)} %pad_maximum_fusion.3.vec_ref) | copy-start | bytes 55300
  107.1 18.8 %copy-start.15 = (bf16[1,768,768]{2,1,0:T(8,128)(2,1)S(1)}, bf16[1,768,768]{2,1,0:T(8,128)(2,1)}, u32[]{:S(2)}) copy-start(bf16[1,768,768]{2,1,0:T(8,128)(2,1)} %param.22) | copy-start | bytes 3538948
  107.1 18.8 %copy-start.16 = (bf16[1,768,768]{2,1,0:T(8,128)(2,1)S(1)}, bf16[1,768,768]{2,1,0:T(8,128)(2,1)}, u32[]{:S(2)}) copy-start(bf16[1,768,768]{2,1,0:T(8,128)(2,1)} %param.20) | copy-start | bytes 3538948
  125.9 3.2 copy-start.18
  186.7 0.9 copy-start.1
  187.6 0.9 copy-start.3
  188.5 0.9 copy-start.4
  189.4 0.8 copy-start.7
  190.2 0.6 copy-start.12
  239.1 0.9 copy-start.5
  239.9 0.9 copy-start.6
  240.8 0.8 copy-start.8
  241.6 0.6 copy-start.13
  366.3 122.5 %copy-start.2 = (bf16[512,768]{1,0:T(8,128)(2,1)S(1)}, bf16[512,768]{1,0:T(8,128)(2,1)}, u32[]{:S(2)}) copy-start(bf16[512,768]{1,0:T(8,128)(2,1)} %copy-done.1) | copy-start | bytes 2359300
  366.3 124.2 %copy-start.20 = (bf16[512,768]{1,0:T(8,128)(2,1)S(1)}, bf16[512,768]{1,0:T(8,128)(2,1)}, u32[]{:S(2)}) copy-start(bf16[512,768]{1,0:T(8,128)(2,1)} %get-tuple-element.57) | copy-start | bytes 2359300
  487.4 3.1 copy-start.14
  488.9 3.0 copy-start.19
  488.9 29.3 %collective-permute-start.7 = (bf16[2,256,768]{2,1,0:T(8,128)(2,1)S(1)}, bf16[2,256,768]{2,1,0:T(8,128)(2,1)S(1)}, u32[]{:S(2)}, u32[]{:S(2)}) collective-permute-start(bf16[2,256,768]{2,1,0:T(8,128)(2,1)S(1)} %fusion.2), channel_id=1, source_target_pairs={{8,0},{12,4},{16,24},{20,28},{9,1},{13,5},{17,25},{21,29},{10,2},{... | collective-permute-start | bytes 2359304 | tf_op jit(solution)/shard_map/ppermute | solution.py:882
  490.6 36.1 %collective-permute-start.11 = (bf16[2,256,768]{2,1,0:T(8,128)(2,1)S(1)}, bf16[2,256,768]{2,1,0:T(8,128)(2,1)S(1)}, u32[]{:S(2)}, u32[]{:S(2)}) collective-permute-start(bf16[2,256,768]{2,1,0:T(8,128)(2,1)S(1)} %fusion.1), channel_id=1, source_target_pairs={{8,0},{12,4},{16,24},{20,28},{9,1},{13,5},{17,25},{21,29},{10,2},{... | collective-permute-start | bytes 2359304 | tf_op jit(solution)/shard_map/ppermute | solution.py:882
  518.6 13.5 %collective-permute-start.8 = (bf16[2,256,768]{2,1,0:T(8,128)(2,1)S(1)}, bf16[2,256,768]{2,1,0:T(8,128)(2,1)S(1)}, u32[]{:S(2)}, u32[]{:S(2)}) collective-permute-start(bf16[2,256,768]{2,1,0:T(8,128)(2,1)S(1)} %select_bitcast_fusion.4), channel_id=1, source_target_pairs={{0,16},{4,20},{24,8},{28,12},{1,17},{5,21},{25,9},{29,13},{2,18},{... | collective-permute-start | bytes 2359304 | tf_op jit(solution)/shard_map/ppermute | solution.py:882
  527.0 6.1 %collective-permute-start.12 = (bf16[2,256,768]{2,1,0:T(8,128)(2,1)S(1)}, bf16[2,256,768]{2,1,0:T(8,128)(2,1)S(1)}, u32[]{:S(2)}, u32[]{:S(2)}) collective-permute-start(bf16[2,256,768]{2,1,0:T(8,128)(2,1)S(1)} %fusion), channel_id=1, source_target_pairs={{0,16},{4,20},{24,8},{28,12},{1,17},{5,21},{25,9},{29,13},{2,18},{... | collective-permute-start | bytes 2359304 | tf_op jit(solution)/shard_map/ppermute | solution.py:882
Sparse Core Ops, SparseCore 0:
  55.8 48.4 all-gather.1
